TPU v7x, 32 devices: a whole 2x2x4 slice. The times are simulated.
32 devices in a mesh: section: 2 (over y), dp: 4 (over x, core), tensor: 4 (over z).
Axes of the slice: x: 2, y: 2, z: 4, core: 2. Of those that a mesh axis runs over, the one named last changes fastest.
Arguments:
- block_input: bfloat16 [4, 4096, 1024], P(None, ('dp', 'tensor')), may hold values from -6 to 6
- seq_lengths: int32 [4, 4, 4], P(None, 'dp'), may hold values from 1 to 512, as said below
- w_qkv: bfloat16 [2, 1024, 3, 1024], P('section', 'dp', None, 'tensor'), may hold values from -0.25 to 0.25
- w_out: bfloat16 [2, 1024, 1024], P('section', 'tensor', 'dp'), may hold values from -0.5 to 0.5
- w_in: bfloat16 [2, 1024, 4096], P('section', 'dp', 'tensor'), may hold values from -0.1875 to 0.1875
- w_back: bfloat16 [2, 4096, 1024], P('section', 'tensor', 'dp'), may hold values from -0.09375 to 0.09375
- gains: bfloat16 [2, 2, 1024], P('section', None, 'dp'), may hold values from 0.25 to 1.75
- biases: bfloat16 [2, 6, 1024], P('section', None, 'dp'), may hold values from -3 to 3
- ffn_bias: bfloat16 [2, 4096], P('section', 'dp'), may hold values from -3 to 3
- out_grad: bfloat16 [4, 4096, 1024], P(None, ('dp', 'tensor')), may hold values from -6 to 6
Outputs:
- layer_outputs: float32 [2, 4, 4096, 1024], P('section', None, ('dp', 'tensor'))
- input_grads: float32 [2, 4, 4096, 1024], P('section', None, ('dp', 'tensor'))
- grad_w_qkv: float32 [2, 1024, 3, 1024], P('section', 'dp', None, 'tensor')
- grad_w_out: float32 [2, 1024, 1024], P('section', 'tensor', 'dp')
- grad_w_in: float32 [2, 1024, 4096], P('section', 'dp', 'tensor')
- grad_w_back: float32 [2, 4096, 1024], P('section', 'tensor', 'dp')
- grad_gains: float32 [2, 2, 1024], P('section', None, 'dp')
- grad_biases: float32 [2, 6, 1024], P('section', None, 'dp')
- grad_ffn_bias: float32 [2, 4096], P('section', 'dp')
Inputs may be any that keep to these rules, and one draw needn't show every extreme that they name: `seq_lengths`: in each micro-batch and group the 4 lengths add up to at most 1024, and exactly 1024 in one group among all micro-batches and groups; the longest length of every group is exactly 512.
All inputs are finite; a program needn't handle non-finite values.
Results may differ from a plain program's by a relative error of at most 0.03.
Values may be sent and summed in bfloat16 or wider, within the bound.
No kernel may reach another device: no remote copies, remote signals or barrier semaphores. Data moves between devices by JAX's collectives and lax.ppermute only.
A program may use at most 512 MiB of HBM per device.

v0:
```python
import jax
import jax.numpy as jnp
from jax import lax
from jax.sharding import PartitionSpec as P

HEAD_DIM = 64


def from_behind(shard, axis, by):
    peers = lax.axis_size(axis)
    pairs = [(i, i + by) for i in range(peers) if 0 <= i + by < peers]
    return lax.ppermute(shard, axis, pairs)


def matmul(lhs_mat, rhs_mat):
    return jnp.dot(lhs_mat, rhs_mat, preferred_element_type=jnp.float32)


def lhs_inner(lhs_mat, rhs_mat):
    return lax.dot_general(
        lhs_mat, rhs_mat, (((0,), (0,)), ((), ())), preferred_element_type=jnp.float32
    )


def rhs_inner(lhs_mat, rhs_mat):
    return lax.dot_general(
        lhs_mat, rhs_mat, (((1,), (1,)), ((), ())), preferred_element_type=jnp.float32
    )


def normalize(summed, gain_row, bias_row):
    centered = summed - jnp.mean(summed, axis=-1, keepdims=True)
    variance = jnp.mean(centered * centered, axis=-1, keepdims=True)
    return centered * lax.rsqrt(variance + 1e-05) * gain_row + bias_row


def gelu_exact(values):
    return jax.nn.gelu(values, approximate=False)


def segment_ids(seq_lens, row_count):
    seq_ends = jnp.cumsum(seq_lens)
    positions = jnp.arange(row_count, dtype=jnp.int32)
    return jnp.sum((positions[:, None] >= seq_ends[None, :]).astype(jnp.int32), axis=1)


def score_block(query_block, key_rows, segment_block, segments):
    factor = query_block.shape[-1] ** (-0.5)
    scores = (
        jnp.einsum("qhd,khd->hqk", query_block, key_rows, preferred_element_type=jnp.float32)
        * factor
    )
    allowed = segment_block[:, None] == segments[None, :]
    return jnp.where(allowed[None], scores, -1000000000.0)


def attend_forward(packed, segments):
    row_count, _, heads_here, head_size = packed.shape
    block_rows = min(512, row_count)
    blocks = row_count // block_rows
    key_rows = packed[:, 1]
    value_rows = packed[:, 2]

    def one_block(carried, block_pair):
        query_block, segment_block = block_pair
        scores = score_block(query_block, key_rows, segment_block, segments)
        highest = jnp.max(scores, axis=-1, keepdims=True)
        raised = jnp.exp(scores - highest)
        totals = jnp.sum(raised, axis=-1, keepdims=True)
        weights = (raised / totals).astype(jnp.bfloat16)
        context = jnp.einsum(
            "hqk,khd->qhd", weights, value_rows, preferred_element_type=jnp.float32
        )
        return (carried, (context.astype(jnp.bfloat16), (highest + jnp.log(totals))[:, :, 0]))

    query_blocks = packed[:, 0].reshape(blocks, block_rows, heads_here, head_size)
    _, (context, logsums) = lax.scan(
        one_block, jnp.zeros((), jnp.float32), (query_blocks, segments.reshape(blocks, block_rows))
    )
    return (context.reshape(row_count, heads_here * head_size), logsums)


def attend_backward(packed, segments, logsums, context_grad):
    row_count, _, heads_here, head_size = packed.shape
    block_rows = min(512, row_count)
    blocks = row_count // block_rows
    factor = head_size ** (-0.5)
    key_rows = packed[:, 1]
    value_rows = packed[:, 2]

    def one_block(carried, block_items):
        key_grad, value_grad = carried
        query_block, segment_block, logsum_block, grad_block = block_items
        scores = score_block(query_block, key_rows, segment_block, segments)
        weights = jnp.exp(scores - logsum_block[:, :, None])
        weight_grad = jnp.einsum(
            "qhd,khd->hqk", grad_block, value_rows, preferred_element_type=jnp.float32
        )
        centre = jnp.sum(weight_grad * weights, axis=-1, keepdims=True)
        score_grad = (weights * (weight_grad - centre)).astype(jnp.bfloat16)
        query_grad = (
            jnp.einsum("hqk,khd->qhd", score_grad, key_rows, preferred_element_type=jnp.float32)
            * factor
        )
        key_grad = (
            key_grad
            + jnp.einsum(
                "hqk,qhd->khd", score_grad, query_block, preferred_element_type=jnp.float32
            )
            * factor
        )
        value_grad = value_grad + jnp.einsum(
            "hqk,qhd->khd",
            weights.astype(jnp.bfloat16),
            grad_block,
            preferred_element_type=jnp.float32,
        )
        return ((key_grad, value_grad), query_grad)

    start_grads = (
        jnp.zeros((row_count, heads_here, head_size), jnp.float32),
        jnp.zeros((row_count, heads_here, head_size), jnp.float32),
    )
    shaped = (
        packed[:, 0].reshape(blocks, block_rows, heads_here, head_size),
        segments.reshape(blocks, block_rows),
        logsums,
        context_grad.reshape(blocks, block_rows, heads_here, head_size),
    )
    (key_grad, value_grad), query_grad = lax.scan(one_block, start_grads, shaped)
    return (query_grad.reshape(row_count, heads_here, head_size), key_grad, value_grad)


def layer_forward(row_block, segments, params, tensor_place):
    w_qkv, w_out, w_in, w_back, gains, biases, ffn_bias = params
    model_width = w_qkv.shape[0]
    head_cols = w_qkv.shape[2]
    hidden_share = w_in.shape[1]
    gathered = lax.all_gather(row_block, "tensor", axis=0, tiled=True)
    projection = w_qkv.reshape(model_width, 3 * head_cols)
    query_bias = lax.dynamic_slice_in_dim(biases[0], tensor_place * head_cols, head_cols).astype(
        jnp.float32
    )
    value_bias = lax.dynamic_slice_in_dim(biases[1], tensor_place * head_cols, head_cols).astype(
        jnp.float32
    )
    offset = jnp.concatenate([query_bias, jnp.zeros((head_cols,), jnp.float32), value_bias])
    packed = (matmul(gathered, projection) + offset).astype(jnp.bfloat16)
    packed = packed.reshape(gathered.shape[0], 3, head_cols // HEAD_DIM, HEAD_DIM)
    context, logsums = attend_forward(packed, segments)
    attended = lax.psum_scatter(matmul(context, w_out), "tensor", scatter_dimension=0, tiled=True)
    first_sum = row_block.astype(jnp.float32) + attended + biases[2].astype(jnp.float32)
    middle = normalize(
        first_sum, gains[0].astype(jnp.float32), biases[3].astype(jnp.float32)
    ).astype(jnp.bfloat16)
    spread = lax.all_gather(middle, "tensor", axis=0, tiled=True)
    inner_bias = lax.dynamic_slice_in_dim(
        ffn_bias, tensor_place * hidden_share, hidden_share
    ).astype(jnp.float32)
    hidden = matmul(spread, w_in) + inner_bias
    active = gelu_exact(hidden).astype(jnp.bfloat16)
    branch = lax.psum_scatter(matmul(active, w_back), "tensor", scatter_dimension=0, tiled=True)
    second_sum = middle.astype(jnp.float32) + branch + biases[4].astype(jnp.float32)
    result = normalize(second_sum, gains[1].astype(jnp.float32), biases[5].astype(jnp.float32))
    saved = (
        gathered,
        packed,
        logsums,
        context,
        first_sum,
        middle,
        spread,
        hidden,
        active,
        second_sum,
    )
    return (result, saved)


def layer_backward(saved, segments, grad_rows, params, tensor_place):
    w_qkv, w_out, w_in, w_back, gains, biases, ffn_bias = params
    gathered, packed, logsums, context, first_sum, middle, spread, hidden, active, second_sum = (
        saved
    )
    model_width = w_qkv.shape[0]
    head_cols = w_qkv.shape[2]
    hidden_share = w_in.shape[1]
    _, second_back = jax.vjp(
        normalize, second_sum, gains[1].astype(jnp.float32), biases[5].astype(jnp.float32)
    )
    second_grad, gain_two, bias_two = second_back(grad_rows.astype(jnp.float32))
    branch_all = lax.all_gather(second_grad.astype(jnp.bfloat16), "tensor", axis=0, tiled=True)
    active_grad = rhs_inner(branch_all, w_back)
    back_grad = lhs_inner(active, branch_all)
    _, gelu_back = jax.vjp(gelu_exact, hidden)
    hidden_grad = gelu_back(active_grad)[0]
    hidden_low = hidden_grad.astype(jnp.bfloat16)
    in_grad = lhs_inner(spread, hidden_low)
    middle_grad = second_grad + lax.psum_scatter(
        rhs_inner(hidden_low, w_in), "tensor", scatter_dimension=0, tiled=True
    )
    _, first_back = jax.vjp(
        normalize, first_sum, gains[0].astype(jnp.float32), biases[3].astype(jnp.float32)
    )
    first_grad, gain_one, bias_one = first_back(middle_grad)
    attended_all = lax.all_gather(first_grad.astype(jnp.bfloat16), "tensor", axis=0, tiled=True)
    context_grad = rhs_inner(attended_all, w_out).astype(jnp.bfloat16)
    out_grad_w = lhs_inner(context, attended_all)
    query_grad, key_grad, value_grad = attend_backward(packed, segments, logsums, context_grad)
    packed_grad = jnp.stack([query_grad, key_grad, value_grad], axis=1).reshape(-1, 3 * head_cols)
    packed_low = packed_grad.astype(jnp.bfloat16)
    projection = w_qkv.reshape(model_width, 3 * head_cols)
    qkv_grad = lhs_inner(gathered, packed_low).reshape(model_width, 3, head_cols)
    input_grad = first_grad + lax.psum_scatter(
        rhs_inner(packed_low, projection), "tensor", scatter_dimension=0, tiled=True
    )
    column_start = tensor_place * head_cols
    zero_row = jnp.zeros((model_width,), jnp.float32)
    query_bias_grad = lax.dynamic_update_slice_in_dim(
        zero_row, jnp.sum(query_grad, axis=0).reshape(head_cols), column_start, 0
    )
    value_bias_grad = lax.dynamic_update_slice_in_dim(
        zero_row, jnp.sum(value_grad, axis=0).reshape(head_cols), column_start, 0
    )
    inner_grad = lax.dynamic_update_slice_in_dim(
        jnp.zeros((ffn_bias.shape[0],), jnp.float32),
        jnp.sum(hidden_grad, axis=0),
        tensor_place * hidden_share,
        0,
    )
    gain_grads = jnp.stack([gain_one, gain_two])
    bias_grads = jnp.stack(
        [
            query_bias_grad,
            value_bias_grad,
            jnp.sum(first_grad, axis=0),
            bias_one,
            jnp.sum(second_grad, axis=0),
            bias_two,
        ]
    )
    return (
        input_grad,
        (qkv_grad, out_grad_w, in_grad, back_grad, gain_grads, bias_grads, inner_grad),
    )


def store_slot(buffer, new_values, slot_index, is_valid):
    current = lax.dynamic_index_in_dim(buffer, slot_index, 0, keepdims=False)
    return lax.dynamic_update_index_in_dim(
        buffer, jnp.where(is_valid, new_values, current), slot_index, 0
    )


def load_slot(buffer, slot_index):
    return lax.dynamic_index_in_dim(buffer, slot_index, 0, keepdims=False)


def on_device(
    block_input, seq_lengths, w_qkv, w_out, w_in, w_back, gains, biases, ffn_bias, out_grad
):
    section_count = lax.axis_size("section")
    section_place = lax.axis_index("section")
    tensor_place = lax.axis_index("tensor")
    micro_count = block_input.shape[0]
    own_rows = block_input.shape[1]
    model_width = block_input.shape[2]
    group_size = own_rows * lax.axis_size("tensor")
    fetched = (
        lax.all_gather(w_qkv, "dp", axis=1, tiled=True),
        lax.all_gather(w_out, "dp", axis=2, tiled=True),
        lax.all_gather(w_in, "dp", axis=1, tiled=True),
        lax.all_gather(w_back, "dp", axis=2, tiled=True),
        lax.all_gather(gains, "dp", axis=2, tiled=True),
        lax.all_gather(biases, "dp", axis=2, tiled=True),
        lax.all_gather(ffn_bias, "dp", axis=1, tiled=True),
    )
    params = tuple((weight[0] for weight in fetched))
    lengths_here = seq_lengths[:, 0, :]
    slot_count = lengths_here.shape[-1]

    def segments_at(slot_index):
        return segment_ids(load_slot(lengths_here, slot_index), group_size)

    incoming = jnp.zeros((own_rows, model_width), jnp.bfloat16)
    returning = incoming
    outputs = jnp.zeros((micro_count, own_rows, model_width), jnp.float32)
    input_grads = jnp.zeros((micro_count, own_rows, model_width), jnp.float32)
    saved_stash = None
    totals = tuple(
        (
            jnp.zeros(weight.shape[1:], jnp.float32)
            for weight in (w_qkv, w_out, w_in, w_back, gains, biases, ffn_bias)
        )
    )
    for step_number in range(micro_count + 2 * (section_count - 1)):
        forward_number = step_number - section_place
        forward_valid = (forward_number >= 0) & (forward_number < micro_count)
        forward_slot = jnp.clip(forward_number, 0, micro_count - 1)
        rows_now = jnp.where(
            section_place == 0, block_input[min(step_number, micro_count - 1)], incoming
        )
        result, saved = layer_forward(rows_now, segments_at(forward_slot), params, tensor_place)
        outputs = store_slot(outputs, result, forward_slot, forward_valid)
        incoming = from_behind(result.astype(jnp.bfloat16), "section", 1)
        backward_number = step_number - 2 * (section_count - 1) + section_place
        backward_valid = (backward_number >= 0) & (backward_number < micro_count)
        backward_slot = jnp.clip(backward_number, 0, micro_count - 1)
        backward_segments = segments_at(backward_slot)
        if saved_stash is None:
            saved_stash = tuple(
                (jnp.zeros((micro_count,) + element.shape, element.dtype) for element in saved)
            )
        saved_stash = tuple(
            (
                store_slot(stash_slot, element, forward_slot, forward_valid)
                for stash_slot, element in zip(saved_stash, saved)
            )
        )
        saved_back = tuple((load_slot(stash_slot, backward_slot) for stash_slot in saved_stash))
        last_index = min(max(step_number - (section_count - 1), 0), micro_count - 1)
        live_here = lax.dynamic_slice_in_dim(
            backward_segments < slot_count, tensor_place * own_rows, own_rows, 0
        )
        masked_cotangent = jnp.where(
            live_here[:, None], out_grad[last_index], jnp.zeros((), jnp.bfloat16)
        )
        grad_now = jnp.where(section_place == section_count - 1, masked_cotangent, returning)
        input_grad, grad_terms = layer_backward(
            saved_back, backward_segments, grad_now, params, tensor_place
        )
        input_grads = store_slot(input_grads, input_grad, backward_slot, backward_valid)
        returning = from_behind(input_grad.astype(jnp.bfloat16), "section", -1)
        weighting = backward_valid.astype(jnp.float32)
        grad_terms = tuple((grad_part * weighting for grad_part in grad_terms))
        shares = (
            lax.psum_scatter(grad_terms[0], "dp", scatter_dimension=0, tiled=True),
            lax.psum_scatter(grad_terms[1], "dp", scatter_dimension=1, tiled=True),
            lax.psum_scatter(grad_terms[2], "dp", scatter_dimension=0, tiled=True),
            lax.psum_scatter(grad_terms[3], "dp", scatter_dimension=1, tiled=True),
            lax.psum_scatter(grad_terms[4], "dp", scatter_dimension=1, tiled=True),
            lax.psum_scatter(grad_terms[5], "dp", scatter_dimension=1, tiled=True),
            lax.psum_scatter(grad_terms[6], "dp", scatter_dimension=0, tiled=True),
        )
        totals = tuple((total_part + share_part for total_part, share_part in zip(totals, shares)))
    shares = totals
    gain_total, bias_total, inner_total = lax.psum((shares[4], shares[5], shares[6]), "tensor")
    return (
        outputs[None],
        input_grads[None],
        shares[0][None],
        shares[1][None],
        shares[2][None],
        shares[3][None],
        gain_total[None],
        bias_total[None],
        inner_total[None],
    )


def solution(mesh):
    return jax.shard_map(
        on_device,
        mesh=mesh,
        in_specs=(
            P(None, ("dp", "tensor"), None),
            P(None, "dp", None),
            P("section", "dp", None, "tensor"),
            P("section", "tensor", "dp"),
            P("section", "dp", "tensor"),
            P("section", "tensor", "dp"),
            P("section", None, "dp"),
            P("section", None, "dp"),
            P("section", "dp"),
            P(None, ("dp", "tensor"), None),
        ),
        out_specs=(
            P("section", None, ("dp", "tensor"), None),
            P("section", None, ("dp", "tensor"), None),
            P("section", "dp", None, "tensor"),
            P("section", "tensor", "dp"),
            P("section", "dp", "tensor"),
            P("section", "tensor", "dp"),
            P("section", None, "dp"),
            P("section", None, "dp"),
            P("section", "dp"),
        ),
        check_vma=False,
    )
```

profile of v0, /device:TPU:0, one launch (start us, length us, event | category | flops | bytes accessed | tf_op | source)
XLA Modules:
  0.0 3613.8 jit_solution(10315704642411285817)
XLA Ops:
  35.5 48.1 %all-gather.81.cloned.1.call-done = bf16[1,1024,1024]{2,1,0:T(8,128)(2,1)} async-done(((bf16[1,256,1024]{2,1,0:T(8,128)(2,1)}), bf16[1,1024,1024]{2,1,0:T(8,128)(2,1)}) %all-gather.81.cloned.1.call-update) | async-done | bytes 2097168 | tf_op jit(solution)/shard_map/all_gather | solution.py:139
  113.6 69.9 %reduce-scatter.33.cloned.1.call-done = f32[256,1024]{1,0:T(8,128)} async-done(((f32[1024,1024]{1,0:T(8,128)}), f32[256,1024]{1,0:T(8,128)}) %reduce-scatter.33.cloned.1.call-update) | async-done | bytes 1048592 | tf_op jit(solution)/shard_map/reduce_scatter | solution.py:151
  208.1 48.0 %all-gather.31.cloned.1.call-done = bf16[1024,1024]{1,0:T(8,128)(2,1)} async-done(((bf16[256,1024]{1,0:T(8,128)(2,1)}), bf16[1024,1024]{1,0:T(8,128)(2,1)}) %all-gather.31.cloned.1.call-update) | async-done | bytes 2097168 | tf_op jit(solution)/shard_map/all_gather | solution.py:156
  285.9 76.9 %reduce-scatter.35.cloned.1.call-done = f32[256,1024]{1,0:T(8,128)} async-done(((f32[1024,1024]{1,0:T(8,128)}), f32[256,1024]{1,0:T(8,128)}) %reduce-scatter.35.cloned.1.call-update) | async-done | bytes 1048592 | tf_op jit(solution)/shard_map/reduce_scatter | solution.py:162
  384.4 47.0 %all-gather.37.cloned.1.call-done = bf16[1024,1024]{1,0:T(8,128)(2,1)} async-done(((bf16[256,1024]{1,0:T(8,128)(2,1)}), bf16[1024,1024]{1,0:T(8,128)(2,1)}) %all-gather.37.cloned.1.call-update) | async-done | bytes 2097168 | tf_op jit(solution)/shard_map/all_gather | solution.py:139
  456.2 75.6 %reduce-scatter.37.cloned.1.call-done = f32[256,1024]{1,0:T(8,128)} async-done(((f32[1024,1024]{1,0:T(8,128)}), f32[256,1024]{1,0:T(8,128)}) %reduce-scatter.37.cloned.1.call-update) | async-done | bytes 1048592 | tf_op jit(solution)/shard_map/reduce_scatter | solution.py:151
  611.1 67.7 %reduce-scatter.39.cloned.1.call-done = f32[256,1024]{1,0:T(8,128)} async-done(((f32[1024,1024]{1,0:T(8,128)}), f32[256,1024]{1,0:T(8,128)}) %reduce-scatter.39.cloned.1.call-update) | async-done | bytes 1048592 | tf_op jit(solution)/shard_map/reduce_scatter | solution.py:162
  819.2 41.2 %reduce-scatter.57.cloned.1.call-done = f32[256,1024]{1,0:T(8,128)} async-done(((f32[1024,1024]{1,0:T(8,128)}), f32[256,1024]{1,0:T(8,128)}) %reduce-scatter.57.cloned.1.call-update) | async-done | bytes 1048592 | tf_op jit(solution)/shard_map/reduce_scatter | solution.py:199
  863.9 76.0 %reduce-scatter.41.cloned.1.call-done = f32[256,1024]{1,0:T(8,128)} async-done(((f32[1024,1024]{1,0:T(8,128)}), f32[256,1024]{1,0:T(8,128)}) %reduce-scatter.41.cloned.1.call-update) | async-done | bytes 1048592 | tf_op jit(solution)/shard_map/reduce_scatter | solution.py:151
  1075.7 43.0 %reduce-scatter.59.cloned.1.call-done = f32[256,1024]{1,0:T(8,128)} async-done(((f32[1024,1024]{1,0:T(8,128)}), f32[256,1024]{1,0:T(8,128)}) %reduce-scatter.59.cloned.1.call-update) | async-done | bytes 1048592 | tf_op jit(solution)/shard_map/reduce_scatter | solution.py:214
  1121.9 76.6 %reduce-scatter.43.cloned.1.call-done = f32[256,1024]{1,0:T(8,128)} async-done(((f32[1024,1024]{1,0:T(8,128)}), f32[256,1024]{1,0:T(8,128)}) %reduce-scatter.43.cloned.1.call-update) | async-done | bytes 1048592 | tf_op jit(solution)/shard_map/reduce_scatter | solution.py:162
  1384.8 76.2 %reduce-scatter.45.cloned.1.call-done = f32[256,1024]{1,0:T(8,128)} async-done(((f32[1024,1024]{1,0:T(8,128)}), f32[256,1024]{1,0:T(8,128)}) %reduce-scatter.45.cloned.1.call-update) | async-done | bytes 1048592 | tf_op jit(solution)/shard_map/reduce_scatter | solution.py:151
  1598.5 41.0 %reduce-scatter.63.cloned.1.call-done = f32[256,1024]{1,0:T(8,128)} async-done(((f32[1024,1024]{1,0:T(8,128)}), f32[256,1024]{1,0:T(8,128)}) %reduce-scatter.63.cloned.1.call-update) | async-done | bytes 1048592 | tf_op jit(solution)/shard_map/reduce_scatter | solution.py:214
  1642.4 76.7 %reduce-scatter.47.cloned.1.call-done = f32[256,1024]{1,0:T(8,128)} async-done(((f32[1024,1024]{1,0:T(8,128)}), f32[256,1024]{1,0:T(8,128)}) %reduce-scatter.47.cloned.1.call-update) | async-done | bytes 1048592 | tf_op jit(solution)/shard_map/reduce_scatter | solution.py:162
  1905.2 76.2 %reduce-scatter.49.cloned.1.call-done = f32[256,1024]{1,0:T(8,128)} async-done(((f32[1024,1024]{1,0:T(8,128)}), f32[256,1024]{1,0:T(8,128)}) %reduce-scatter.49.cloned.1.call-update) | async-done | bytes 1048592 | tf_op jit(solution)/shard_map/reduce_scatter | solution.py:151
  2116.8 43.5 %reduce-scatter.67.cloned.1.call-done = f32[256,1024]{1,0:T(8,128)} async-done(((f32[1024,1024]{1,0:T(8,128)}), f32[256,1024]{1,0:T(8,128)}) %reduce-scatter.67.cloned.1.call-update) | async-done | bytes 1048592 | tf_op jit(solution)/shard_map/reduce_scatter | solution.py:214
  2163.3 76.8 %reduce-scatter.51.cloned.1.call-done = f32[256,1024]{1,0:T(8,128)} async-done(((f32[1024,1024]{1,0:T(8,128)}), f32[256,1024]{1,0:T(8,128)}) %reduce-scatter.51.cloned.1.call-update) | async-done | bytes 1048592 | tf_op jit(solution)/shard_map/reduce_scatter | solution.py:162
  2426.2 76.0 %reduce-scatter.53.cloned.1.call-done = f32[256,1024]{1,0:T(8,128)} async-done(((f32[1024,1024]{1,0:T(8,128)}), f32[256,1024]{1,0:T(8,128)}) %reduce-scatter.53.cloned.1.call-update) | async-done | bytes 1048592 | tf_op jit(solution)/shard_map/reduce_scatter | solution.py:151
  2639.0 41.9 %reduce-scatter.71.cloned.1.call-done = f32[256,1024]{1,0:T(8,128)} async-done(((f32[1024,1024]{1,0:T(8,128)}), f32[256,1024]{1,0:T(8,128)}) %reduce-scatter.71.cloned.1.call-update) | async-done | bytes 1048592 | tf_op jit(solution)/shard_map/reduce_scatter | solution.py:214
  2684.0 76.4 %reduce-scatter.55.cloned.1.call-done = f32[256,1024]{1,0:T(8,128)} async-done(((f32[1024,1024]{1,0:T(8,128)}), f32[256,1024]{1,0:T(8,128)}) %reduce-scatter.55.cloned.1.call-update) | async-done | bytes 1048592 | tf_op jit(solution)/shard_map/reduce_scatter | solution.py:162
  2845.7 65.1 %reduce-scatter.73.cloned.1.call-done = f32[256,1024]{1,0:T(8,128)} async-done(((f32[1024,1024]{1,0:T(8,128)}), f32[256,1024]{1,0:T(8,128)}) %reduce-scatter.73.cloned.1.call-update) | async-done | bytes 1048592 | tf_op jit(solution)/shard_map/reduce_scatter | solution.py:199
  3011.3 73.5 %reduce-scatter.75.cloned.1.call-done = f32[256,1024]{1,0:T(8,128)} async-done(((f32[1024,1024]{1,0:T(8,128)}), f32[256,1024]{1,0:T(8,128)}) %reduce-scatter.75.cloned.1.call-update) | async-done | bytes 1048592 | tf_op jit(solution)/shard_map/reduce_scatter | solution.py:214
  3177.2 72.7 %reduce-scatter.77.cloned.1.call-done = f32[256,1024]{1,0:T(8,128)} async-done(((f32[1024,1024]{1,0:T(8,128)}), f32[256,1024]{1,0:T(8,128)}) %reduce-scatter.77.cloned.1.call-update) | async-done | bytes 1048592 | tf_op jit(solution)/shard_map/reduce_scatter | solution.py:199
  3565.8 41.3 %reduce-scatter.81.cloned.1.call-done = f32[256,3,256]{2,0,1:T(8,128)} async-done(((f32[1024,3,256]{2,0,1:T(8,128)}), f32[256,3,256]{2,0,1:T(8,128)}) %reduce-scatter.81.cloned.1.call-update) | async-done | bytes 786448 | tf_op jit(solution)/shard_map/reduce_scatter | solution.py:337
  (1761 shorter events, 2336.5 us)
Async XLA Ops:
  11.1 172.4 %reduce-scatter.33.cloned.1.call-start = ((), (), s32[]{:S(2)}) async-start(), calls=%async_computation.31 | async-start | bytes 5242880 | tf_op jit(solution)/shard_map/reduce_scatter | solution.py:151
  189.9 172.9 %reduce-scatter.35.cloned.1.call-start = ((), (), s32[]{:S(2)}) async-start(), calls=%async_computation.35 | async-start | bytes 5242880 | tf_op jit(solution)/shard_map/reduce_scatter | solution.py:162
  757.1 182.8 %reduce-scatter.41.cloned.1.call-start = ((), (), s32[]{:S(2)}) async-start(), calls=%async_computation.41 | async-start | bytes 5242880 | tf_op jit(solution)/shard_map/reduce_scatter | solution.py:151
  810.7 183.8 %all-gather.59.cloned.1.call-start = ((), (), s32[]{:S(2)}) async-start(), calls=%async_computation.58 | async-start | bytes 2621440 | tf_op jit(solution)/shard_map/all_gather | solution.py:206
  1068.8 187.9 %all-gather.61.cloned.1.call-start = ((), (), s32[]{:S(2)}) async-start(), calls=%async_computation.60 | async-start | bytes 2621440 | tf_op jit(solution)/shard_map/all_gather | solution.py:192
  1277.2 183.8 %reduce-scatter.45.cloned.1.call-start = ((), (), s32[]{:S(2)}) async-start(), calls=%async_computation.45 | async-start | bytes 5242880 | tf_op jit(solution)/shard_map/reduce_scatter | solution.py:151
  1331.5 184.1 %all-gather.63.cloned.1.call-start = ((), (), s32[]{:S(2)}) async-start(), calls=%async_computation.62 | async-start | bytes 2621440 | tf_op jit(solution)/shard_map/all_gather | solution.py:206
  1476.1 163.3 %reduce-scatter.63.cloned.1.call-start = ((), (), s32[]{:S(2)}) async-start(), calls=%async_computation.63 | async-start | bytes 5242880 | tf_op jit(solution)/shard_map/reduce_scatter | solution.py:214
  1590.0 187.2 %all-gather.65.cloned.1.call-start = ((), (), s32[]{:S(2)}) async-start(), calls=%async_computation.64 | async-start | bytes 2621440 | tf_op jit(solution)/shard_map/all_gather | solution.py:192
  1797.7 183.6 %reduce-scatter.49.cloned.1.call-start = ((), (), s32[]{:S(2)}) async-start(), calls=%async_computation.49 | async-start | bytes 5242880 | tf_op jit(solution)/shard_map/reduce_scatter | solution.py:151
  1851.6 184.2 %all-gather.67.cloned.1.call-start = ((), (), s32[]{:S(2)}) async-start(), calls=%async_computation.66 | async-start | bytes 2621440 | tf_op jit(solution)/shard_map/all_gather | solution.py:206
  1996.5 163.9 %reduce-scatter.67.cloned.1.call-start = ((), (), s32[]{:S(2)}) async-start(), calls=%async_computation.67 | async-start | bytes 5242880 | tf_op jit(solution)/shard_map/reduce_scatter | solution.py:214
  2080.6 159.4 %reduce-scatter.51.cloned.1.call-start = ((), (), s32[]{:S(2)}) async-start(), calls=%async_computation.51 | async-start | bytes 5242880 | tf_op jit(solution)/shard_map/reduce_scatter | solution.py:162
  2109.9 188.3 %all-gather.69.cloned.1.call-start = ((), (), s32[]{:S(2)}) async-start(), calls=%async_computation.68 | async-start | bytes 2621440 | tf_op jit(solution)/shard_map/all_gather | solution.py:192
  2318.8 183.4 %reduce-scatter.53.cloned.1.call-start = ((), (), s32[]{:S(2)}) async-start(), calls=%async_computation.53 | async-start | bytes 5242880 | tf_op jit(solution)/shard_map/reduce_scatter | solution.py:151
  2372.9 183.9 %all-gather.71.cloned.1.call-start = ((), (), s32[]{:S(2)}) async-start(), calls=%async_computation.70 | async-start | bytes 2621440 | tf_op jit(solution)/shard_map/all_gather | solution.py:206
  2516.9 164.0 %reduce-scatter.71.cloned.1.call-start = ((), (), s32[]{:S(2)}) async-start(), calls=%async_computation.71 | async-start | bytes 5242880 | tf_op jit(solution)/shard_map/reduce_scatter | solution.py:214
  2631.1 183.5 %all-gather.73.cloned.1.call-start = ((), (), s32[]{:S(2)}) async-start(), calls=%async_computation.72 | async-start | bytes 2621440 | tf_op jit(solution)/shard_map/all_gather | solution.py:192
  2917.7 167.1 %reduce-scatter.75.cloned.1.call-start = ((), (), s32[]{:S(2)}) async-start(), calls=%async_computation.75 | async-start | bytes 5242880 | tf_op jit(solution)/shard_map/reduce_scatter | solution.py:214
  3255.8 275.1 %reduce-scatter.91.cloned.1.call-start = ((), (), s32[]{:S(2)}) async-start(), calls=%async_computation.86 | async-start | bytes 655360
  3273.6 258.2 %reduce-scatter.89.cloned.1.call-start = ((), (), s32[]{:S(2)}) async-start(), calls=%async_computation.85 | async-start | bytes 40960 | tf_op jit(solution)/shard_map/reduce_scatter | solution.py:342
  3344.2 206.0 %reduce-scatter.79.cloned.1.call-start = ((), (), s32[]{:S(2)}) async-start(), calls=%async_computation.79 | async-start | bytes 5242880 | tf_op jit(solution)/shard_map/reduce_scatter | solution.py:214
  3349.8 203.0 %reduce-scatter.85.cloned.1.call-start = ((), (), s32[]{:S(2)}) async-start(), calls=%async_computation.83 | async-start | bytes 5242880 | tf_op jit(solution)/shard_map/reduce_scatter | solution.py:339
  3387.7 165.2 %reduce-scatter.87.cloned.1.call-start = ((), (), s32[]{:S(2)}) async-start(), calls=%async_computation.84 | async-start | bytes 5242880 | tf_op jit(solution)/shard_map/reduce_scatter | solution.py:340
  (441 other events, 15360.8 us)
Sparse Core Ops, SparseCore 0:
  108.0 75.4 reduce-scatter.32
  286.0 76.7 reduce-scatter.34
  456.3 75.4 reduce-scatter.36
  603.3 75.4 reduce-scatter.38
  784.8 75.5 reduce-scatter.56
  862.6 77.2 reduce-scatter.40
  1043.3 75.4 reduce-scatter.58
  1121.2 77.2 reduce-scatter.42
  1305.8 75.4 reduce-scatter.60
  1383.7 77.2 reduce-scatter.44
  1564.0 75.4 reduce-scatter.62
  1641.7 77.2 reduce-scatter.46
  1826.1 75.4 reduce-scatter.64
  1904.1 77.2 reduce-scatter.48
  2084.9 75.4 reduce-scatter.66
  2162.7 77.2 reduce-scatter.50
  2347.2 75.4 reduce-scatter.68
  2424.9 77.2 reduce-scatter.52
  2605.4 75.4 reduce-scatter.70
  2683.2 77.2 reduce-scatter.54
  2835.3 75.4 reduce-scatter.72
  3009.4 75.4 reduce-scatter.74
  3174.4 75.4 reduce-scatter.76
  3364.8 76.7 reduce-scatter.78
  (33 shorter events, 1358.0 us)
where the time goes:
time: 3630 us; the launch traced here: 3610 us
  waiting for transfers between devices  2260 us (62%)
  matrix products  580 us (16%)
  other arithmetic  333 us (9%)
  local copies, waits for them, and re-layouts  331 us (9%)
  blocking collectives  56.7 us (2%)
    reduce_scatter x6, waiting for transfers between devices, layer_forward(): lax.psum_scatter(matmul(active, w_back), 'tensor', scatter_dimension=0, t...  451 us
    reduce_scatter x6, waiting for transfers between devices, layer_forward(): lax.psum_scatter(matmul(context, w_out), 'tensor', scatter_dimension=0, t...  450 us
    reduce_scatter x6, waiting for transfers between devices, layer_backward(): lax.psum_scatter(rhs_inner(hidden_low, w_in), 'tensor', scatter_dimension...  297 us
    reduce_scatter x6, waiting for transfers between devices, layer_backward(): lax.psum_scatter(rhs_inner(packed_low, projection), 'tensor', scatter_dim...  243 us
    all_gather x6, waiting for transfers between devices, layer_backward(): lax.all_gather(first_grad.astype(jnp.bfloat16), 'tensor', axis=0, tiled=T...  220 us
    all_gather x6, waiting for transfers between devices, layer_forward(): gathered = lax.all_gather(row_block, 'tensor', axis=0, tiled=True)  194 us
    all_gather x6, waiting for transfers between devices, layer_backward(): lax.all_gather(second_grad.astype(jnp.bfloat16), 'tensor', axis=0, tiled=...  191 us
    dot_general x24, matrix products, rhs_inner(): lax.dot_general(lhs_mat, rhs_mat, (((1,), (1,)), ((), ())), preferred_ele...  158 us
  transfers between devices with their start and end apart: 67, of which 54 were waited for; matrix products, arithmetic and copies ran while one was open for 26% of the time, Pallas kernels for 0%

commit v1 on v0

v1 whole, which is shorter than its diff:
```python
import jax
import jax.numpy as jnp
from jax import lax
from jax.experimental import pallas as pl
from jax.experimental.pallas import tpu as pltpu
from jax.sharding import PartitionSpec as P

HEAD_DIM = 64
AXES = ("section", "dp", "tensor")
LOW = jnp.bfloat16
WIDE = jnp.float32


def move(value, target):
    sections, copies, ranks = (lax.axis_size(axis) for axis in AXES)
    pairs = []
    for s in range(sections):
        for d in range(copies):
            for t in range(ranks):
                goal = target(s, d, t)
                if goal is not None:
                    pairs.append(
                        ((s * copies + d) * ranks + t, (goal[0] * copies + goal[1]) * ranks + goal[2])
                    )
    return lax.ppermute(value, AXES, pairs)


def to_other_core(value):
    return move(value, lambda s, d, t: (s, d ^ 1, t))


def by_core(core, kept, received, axis):
    first = jnp.where(core == 0, kept, received)
    second = jnp.where(core == 0, received, kept)
    return jnp.stack([first, second], axis=axis)


def matmul(lhs_mat, rhs_mat):
    return jnp.dot(lhs_mat, rhs_mat, preferred_element_type=WIDE)


def lhs_inner(lhs_mat, rhs_mat):
    return lax.dot_general(
        lhs_mat, rhs_mat, (((0,), (0,)), ((), ())), preferred_element_type=WIDE
    )


def rhs_inner(lhs_mat, rhs_mat):
    return lax.dot_general(
        lhs_mat, rhs_mat, (((1,), (1,)), ((), ())), preferred_element_type=WIDE
    )


def core_sum(partial):
    low = partial.astype(LOW)
    return low.astype(WIDE) + to_other_core(low).astype(WIDE)


def norm_parts(summed):
    centered = summed - jnp.mean(summed, axis=-1, keepdims=True)
    variance = jnp.mean(centered * centered, axis=-1, keepdims=True)
    scale = lax.rsqrt(variance + 1e-05)
    return centered * scale, scale


def norm_backward(summed, gain_row, grad):
    unit, scale = norm_parts(summed)
    gain_grad = jnp.sum(grad * unit, axis=0)
    bias_grad = jnp.sum(grad, axis=0)
    inner = grad * gain_row
    result = scale * (
        inner
        - jnp.mean(inner, axis=-1, keepdims=True)
        - unit * jnp.mean(inner * unit, axis=-1, keepdims=True)
    )
    return result, gain_grad, bias_grad


def gelu_pair(values):
    below = 0.5 * (1.0 + lax.erf(values * (0.5**0.5)))
    density = jnp.exp(-0.5 * values * values) * (0.3989422804014327)
    return values * below, below + values * density


def segment_ids(seq_lens, row_count):
    seq_ends = jnp.cumsum(seq_lens)
    positions = jnp.arange(row_count, dtype=jnp.int32)
    return jnp.sum((positions[:, None] >= seq_ends[None, :]).astype(jnp.int32), axis=1)


def flash_params(flops, transcendentals, moved):
    return dict(
        cost_estimate=pl.CostEstimate(
            flops=flops, transcendentals=transcendentals, bytes_accessed=moved
        ),
        compiler_params=pltpu.CompilerParams(vmem_limit_bytes=48 * 1024 * 1024),
    )


def head_lanes(values, head):
    lane = lax.broadcasted_iota(jnp.int32, values.shape, 1)
    return jnp.where((lane // HEAD_DIM) == head, values, jnp.zeros_like(values))


def keys_by_queries(keys, queries):
    return lax.dot_general(keys, queries, (((1,), (1,)), ((), ())), preferred_element_type=WIDE)


def forward_kernel(query_ref, key_ref, value_ref, seg_key_ref, seg_query_ref, out_ref, logsum_ref):
    allowed = seg_key_ref[...] == seg_query_ref[...]
    queries = query_ref[...] * jnp.asarray(HEAD_DIM ** (-0.5), LOW)
    heads = queries.shape[1] // HEAD_DIM
    parts = []
    for head in range(heads):
        scores = keys_by_queries(key_ref[...], head_lanes(queries, head))
        scores = jnp.where(allowed, scores, -1000000000.0)
        highest = jnp.max(scores, axis=0, keepdims=True)
        raised = jnp.exp(scores - highest)
        totals = jnp.sum(raised, axis=0, keepdims=True)
        context = lhs_inner(value_ref[...], raised.astype(LOW))
        rows = slice(head * HEAD_DIM, (head + 1) * HEAD_DIM)
        parts.append(context[rows] / totals)
        logsum_ref[0, head : head + 1, :] = highest + jnp.log(totals)
    out_ref[...] = jnp.concatenate(parts, axis=0).T.astype(LOW)


def backward_kernel(
    query_ref, key_ref, value_ref, seg_key_ref, seg_query_ref, logsum_ref, grad_ref,
    out_ref, sum_ref, key_grad, value_grad,
):
    block = pl.program_id(1)
    size, lanes = query_ref.shape
    heads = lanes // HEAD_DIM
    factor = HEAD_DIM ** (-0.5)

    @pl.when(block == 0)
    def _():
        key_grad[...] = jnp.zeros_like(key_grad)
        value_grad[...] = jnp.zeros_like(value_grad)
        sum_ref[...] = jnp.zeros_like(sum_ref)

    allowed = seg_key_ref[...] == seg_query_ref[...]
    queries = query_ref[...] * jnp.asarray(factor, LOW)
    grads = grad_ref[...]
    weight_low, score_low, query_heads, grad_heads, query_parts = [], [], [], [], []
    for head in range(heads):
        query_head, grad_head = head_lanes(queries, head), head_lanes(grads, head)
        scores = jnp.where(allowed, keys_by_queries(key_ref[...], query_head), -1000000000.0)
        weights = jnp.exp(scores - logsum_ref[0, head : head + 1, :])
        weight_grad = keys_by_queries(value_ref[...], grad_head)
        centre = jnp.sum(weight_grad * weights, axis=0, keepdims=True)
        score_grad = (weights * (weight_grad - centre)).astype(LOW)
        rows = slice(head * HEAD_DIM, (head + 1) * HEAD_DIM)
        query_parts.append(lhs_inner(key_ref[...], score_grad)[rows] * factor)
        weight_low.append(weights.astype(LOW))
        score_low.append(score_grad)
        query_heads.append(query_head)
        grad_heads.append(grad_head)
    key_grad[...] += matmul(jnp.concatenate(score_low, axis=1), jnp.concatenate(query_heads, axis=0))
    value_grad[...] += matmul(jnp.concatenate(weight_low, axis=1), jnp.concatenate(grad_heads, axis=0))
    query_grad = jnp.concatenate(query_parts, axis=0).T
    out_ref[pl.ds(pl.multiple_of(block * size, size), size), :lanes] = query_grad.astype(LOW)
    sum_ref[0, 0:1, :] += jnp.sum(query_grad, axis=0, keepdims=True)

    @pl.when(block == pl.num_programs(1) - 1)
    def _():
        out_ref[:, lanes : 2 * lanes] = key_grad[...].astype(LOW)
        out_ref[:, 2 * lanes :] = value_grad[...].astype(LOW)
        sum_ref[0, 1:2, :] = jnp.sum(value_grad[...], axis=0, keepdims=True)


def attention_specs(rows, lanes, size):
    return [
        pl.BlockSpec((size, lanes), lambda pair, block: (block, 3 * pair)),
        pl.BlockSpec((rows, lanes), lambda pair, block: (0, 3 * pair + 1)),
        pl.BlockSpec((rows, lanes), lambda pair, block: (0, 3 * pair + 2)),
        pl.BlockSpec((rows, 1), lambda pair, block: (0, 0)),
        pl.BlockSpec((1, size), lambda pair, block: (0, block)),
    ]


def attend_forward(packed, segments, lanes):
    rows = packed.shape[0]
    pairs = packed.shape[1] // (3 * lanes)
    heads = lanes // HEAD_DIM
    size = min(256, rows)
    squares = pairs * heads * rows * rows
    return pl.pallas_call(
        forward_kernel,
        grid=(pairs, rows // size),
        in_specs=attention_specs(rows, lanes, size),
        out_specs=[
            pl.BlockSpec((size, lanes), lambda pair, block: (block, pair)),
            pl.BlockSpec((1, heads, size), lambda pair, block: (pair, 0, block)),
        ],
        out_shape=[
            jax.ShapeDtypeStruct((rows, pairs * lanes), LOW),
            jax.ShapeDtypeStruct((pairs, heads, rows), WIDE),
        ],
        **flash_params(8 * squares * HEAD_DIM, squares, 4 * rows * pairs * lanes * 2),
    )(packed, packed, packed, segments[:, None], segments[None, :])


def attend_backward(packed, segments, logsums, context_grad, lanes):
    rows = packed.shape[0]
    pairs = packed.shape[1] // (3 * lanes)
    heads = lanes // HEAD_DIM
    size = min(256, rows)
    squares = pairs * heads * rows * rows
    return pl.pallas_call(
        backward_kernel,
        grid=(pairs, rows // size),
        in_specs=attention_specs(rows, lanes, size)
        + [
            pl.BlockSpec((1, heads, size), lambda pair, block: (pair, 0, block)),
            pl.BlockSpec((size, lanes), lambda pair, block: (block, pair)),
        ],
        out_specs=[
            pl.BlockSpec((rows, 3 * lanes), lambda pair, block: (0, pair)),
            pl.BlockSpec((1, 2, lanes), lambda pair, block: (pair, 0, 0)),
        ],
        out_shape=[
            jax.ShapeDtypeStruct((rows, pairs * 3 * lanes), LOW),
            jax.ShapeDtypeStruct((pairs, 2, lanes), WIDE),
        ],
        scratch_shapes=[pltpu.VMEM((rows, lanes), WIDE), pltpu.VMEM((rows, lanes), WIDE)],
        **flash_params(20 * squares * HEAD_DIM, squares, 8 * rows * pairs * lanes * 2),
    )(packed, packed, packed, segments[:, None], segments[None, :], logsums, context_grad)


def pair_columns(packed, head_half, lanes, back=False):
    ranks = lanes // head_half
    if ranks == 1:
        return packed
    order = (3, ranks) if back else (ranks, 3)
    shaped = packed.reshape(packed.shape[0], -1, order[0], order[1], head_half)
    return jnp.swapaxes(shaped, 2, 3).reshape(packed.shape)


def layer_forward(rows, segments, weights, small):
    w_qkv, w_out, w_in, w_back = weights
    gains, biases, offset, inner_bias, head_half = small
    lanes = max(head_half, 128)
    packed = (rhs_inner(rows, w_qkv) + offset).astype(LOW)
    packed = pair_columns(packed, head_half, lanes)
    context, logsums = attend_forward(packed, segments, lanes)
    first_sum = rows.astype(WIDE) + core_sum(matmul(context, w_out)) + biases[2]
    middle = (norm_parts(first_sum)[0] * gains[0] + biases[3]).astype(LOW)
    active, slope = gelu_pair(rhs_inner(middle, w_in) + inner_bias)
    active, slope = active.astype(LOW), slope.astype(LOW)
    second_sum = middle.astype(WIDE) + core_sum(matmul(active, w_back)) + biases[4]
    result = norm_parts(second_sum)[0] * gains[1] + biases[5]
    return result, (rows, packed, logsums, context, first_sum, middle, active, slope, second_sum)


def slab_grads(hidden, features, chips):
    cut = features.shape[1] // chips
    return [lhs_inner(hidden, features[:, k * cut : (k + 1) * cut]).astype(LOW) for k in range(chips)]


def layer_backward(saved, segments, grad_rows, weights, small, chips):
    w_qkv, w_out, w_in, w_back = weights
    gains, biases, _, _, head_half = small
    lanes = max(head_half, 128)
    rows, packed, logsums, context, first_sum, middle, active, slope, second_sum = saved
    second_grad, gain_two, bias_two = norm_backward(second_sum, gains[1], grad_rows.astype(WIDE))
    branch_grad = second_grad.astype(LOW)
    hidden_grad = rhs_inner(branch_grad, w_back) * slope.astype(WIDE)
    hidden_low = hidden_grad.astype(LOW)
    middle_grad = second_grad + core_sum(matmul(hidden_low, w_in))
    back_grad = slab_grads(active, branch_grad, chips)
    in_grad = slab_grads(hidden_low, middle, chips)
    first_grad, gain_one, bias_one = norm_backward(first_sum, gains[0], middle_grad)
    attended_grad = first_grad.astype(LOW)
    context_grad = rhs_inner(attended_grad, w_out).astype(LOW)
    packed_low, sums = attend_backward(packed, segments, logsums, context_grad, lanes)
    packed_low = pair_columns(packed_low, head_half, lanes, back=True)
    input_grad = first_grad + core_sum(matmul(packed_low, w_qkv))
    out_grad = slab_grads(context, attended_grad, chips)
    qkv_grad = slab_grads(packed_low, rows, chips)
    shared = (gain_one, gain_two, jnp.sum(first_grad, axis=0), bias_one, jnp.sum(second_grad, axis=0), bias_two)
    own = (sums[:, 0].reshape(-1), sums[:, 1].reshape(-1), jnp.sum(hidden_grad, axis=0))
    return input_grad, (qkv_grad, out_grad, in_grad, back_grad), shared, own


def on_device(
    block_input, seq_lengths, w_qkv, w_out, w_in, w_back, gains, biases, ffn_bias, out_grad
):
    ranks = lax.axis_size("tensor")
    copies = lax.axis_size("dp")
    chips = copies // 2
    section = lax.axis_index("section")
    copy_at = lax.axis_index("dp")
    rank = lax.axis_index("tensor")
    core = copy_at % 2
    chip = copy_at // 2
    micro_count, own_rows, width = block_input.shape
    repeats = ranks // micro_count
    local = gains.shape[-1]
    counted = (rank % repeats) == 0

    def relative(value):
        parts = value.reshape(value.shape[:-1] + (chips, width // chips))
        axis = parts.ndim - 2
        ordered = [lax.dynamic_index_in_dim(parts, chip ^ k, axis, keepdims=False) for k in range(chips)]
        return jnp.concatenate(ordered, axis=-1)

    def fetch_rows(block):
        parts = block.reshape(micro_count, 2, own_rows // 2, width)
        kept = lax.dynamic_index_in_dim(parts, core, 1, keepdims=False)
        given = lax.dynamic_index_in_dim(parts, 1 - core, 1, keepdims=False)
        received = move(given, lambda s, d, t: (s, d ^ 1, t) if d % 2 == s else None)
        mine = jnp.where(core == section, kept, received)
        mine = jnp.repeat(mine, repeats, axis=0) if repeats > 1 else mine
        mine = lax.all_to_all(mine, "tensor", split_axis=0, concat_axis=0, tiled=True)
        whole = by_core(core, mine, to_other_core(mine), 1)
        return relative(whole.reshape(ranks * own_rows, width))

    def return_rows(first, second):
        chosen = relative(jnp.where(core == 0, first, second).astype(LOW))
        chosen = chosen.reshape(ranks, own_rows, width)
        spread = lax.all_to_all(chosen, "tensor", split_axis=0, concat_axis=0, tiled=True)
        spread = spread.reshape(micro_count, repeats, own_rows, width)[:, 0]
        placed = move(spread, lambda s, d, t: (d % 2, (d // 2) * 2 + s, t))
        return placed.astype(WIDE)[None]

    def gather_weight(halves):
        kept = lax.dynamic_index_in_dim(halves, core, 0, keepdims=False)
        given = lax.dynamic_index_in_dim(halves, 1 - core, 0, keepdims=False)
        received = to_other_core(given)
        own = jnp.where(
            core == 0,
            jnp.concatenate([kept, received], axis=1),
            jnp.concatenate([received, kept], axis=1),
        )
        upward, downward = [own], [own]
        for _ in range(1, ranks):
            upward.append(move(upward[-1], lambda s, d, t: (s, d, t + 1) if t + 1 < ranks else None))
            downward.append(move(downward[-1], lambda s, d, t: (s, d, t - 1) if t > 0 else None))
        item = jnp.zeros((ranks,) + own.shape, LOW)
        item = lax.dynamic_update_index_in_dim(item, own, rank, 0)
        for j in range(1, ranks):
            arrived = jnp.where(rank >= j, upward[j], downward[ranks - j])
            item = lax.dynamic_update_index_in_dim(item, arrived, (rank + ranks - j) % ranks, 0)
        across = move(item, lambda s, d, t: (1 - s, d, t))
        along = [move(item, lambda s, d, t: (s, d ^ (2 * k), t)) for k in range(1, chips)]
        cut = ranks // 2
        far = []
        for k in range(1, chips):
            upper = move(across[:cut], lambda s, d, t: (s, d ^ (2 * k), t))
            lower = move(along[k - 1][cut:], lambda s, d, t: (1 - s, d, t))
            far.append(jnp.concatenate([upper, lower], axis=0))
        mine, other = [item] + along, [across] + far
        result = []
        for layer in range(2):
            slabs = [jnp.where(section == layer, m, o) for m, o in zip(mine, other)]
            result.append(jnp.concatenate(slabs, axis=2))
        return result

    def fold(parts, layer):
        cut = ranks // 4
        off = lambda s: s != layer
        near = parts[0][cut:].astype(WIDE)
        uppers = []
        for k in range(1, chips):
            sent = move(parts[k][:cut], lambda s, d, t: (layer, d, t) if off(s) else None)
            uppers.append((parts[k][:cut].astype(WIDE) + sent.astype(WIDE)).astype(LOW))
            got = move(parts[k][cut:], lambda s, d, t: (s, d ^ (2 * k), t) if off(s) else None)
            near = near + got.astype(WIDE)
        near = jnp.concatenate([parts[0][:cut], near.astype(LOW)], axis=0)
        total = near.astype(WIDE)
        total = total + move(near, lambda s, d, t: (layer, d, t) if off(s) else None).astype(WIDE)
        for k in range(1, chips):
            whole = jnp.concatenate([uppers[k - 1], parts[k][cut:]], axis=0)
            got = move(whole, lambda s, d, t: (s, d ^ (2 * k), t) if not off(s) else None)
            total = total + got.astype(WIDE)
        return total.astype(LOW)

    def reduce_grad(first, second):
        folded = []
        for layer, slabs in enumerate((first, second)):
            slabs = [slab.reshape(ranks, -1, slab.shape[1]) for slab in slabs]
            if repeats > 1:
                slabs = [jnp.where(counted, slab, jnp.zeros((), LOW)) for slab in slabs]
            folded.append(fold(slabs, layer))
        chosen = jnp.where(section == 0, folded[0], folded[1])
        shard = lax.psum_scatter(chosen, "tensor", scatter_dimension=0, tiled=False).astype(LOW)
        shard = shard.reshape(shard.shape[0], 2, local)
        kept = lax.dynamic_index_in_dim(shard, core, 1, keepdims=False)
        given = lax.dynamic_index_in_dim(shard, 1 - core, 1, keepdims=False)
        return by_core(core, kept, to_other_core(given), 0).astype(WIDE)

    rows = fetch_rows(block_input)
    head_half = w_qkv.shape[-1] // 2
    hidden_half = w_in.shape[-1] // 2
    in_first = jnp.moveaxis(w_in[0].reshape(local, 2, hidden_half), 0, 2)
    qkv_first = jnp.transpose(w_qkv[0].reshape(local, 3, 2, head_half), (2, 1, 3, 0))
    qkv_first = qkv_first.reshape(2, 3 * head_half, local)
    out_first = w_out[0].reshape(2, head_half, local)
    attention_all = gather_weight(jnp.concatenate([qkv_first, out_first], axis=1))
    in_all = gather_weight(in_first)
    back_all = gather_weight(w_back[0].reshape(2, hidden_half, local))
    weights = [
        (
            attention_all[layer][:, : 3 * head_half].reshape(-1, width),
            attention_all[layer][:, 3 * head_half :].reshape(-1, width),
            in_all[layer].reshape(-1, width),
            back_all[layer].reshape(-1, width),
        )
        for layer in range(2)
    ]

    gain_count, bias_count = gains.shape[1], biases.shape[1]
    packed_small = jnp.concatenate([gains, biases, ffn_bias.reshape(1, -1, local)], axis=1)
    small_all = lax.all_gather(packed_small, ("section", "dp"), axis=0, tiled=True).astype(WIDE)
    small_all = small_all.reshape(2, copies, -1, local)

    def head_columns(row):
        return lax.dynamic_index_in_dim(row.reshape(ranks, 2, -1), core, 1, keepdims=False).reshape(-1)

    small = []
    for layer in range(2):
        table = jnp.moveaxis(small_all[layer, :, : gain_count + bias_count], 0, 1).reshape(-1, width)
        query_bias = head_columns(table[gain_count])
        value_bias = head_columns(table[gain_count + 1])
        query_bias, value_bias = query_bias.reshape(ranks, 1, -1), value_bias.reshape(ranks, 1, -1)
        offset = jnp.concatenate([query_bias, jnp.zeros_like(query_bias), value_bias], axis=1).reshape(-1)
        inner_bias = head_columns(small_all[layer, :, gain_count + bias_count :].reshape(-1))
        table = relative(table)
        small.append((table[:gain_count], table[gain_count:], offset, inner_bias, head_half))

    lengths = lax.all_gather(seq_lengths, "dp", axis=1, tiled=True)
    group_at = chip * 2 + section
    lengths = lengths[rank // repeats, group_at]
    segments = segment_ids(lengths, ranks * own_rows)
    cotangent = fetch_rows(out_grad)
    cotangent = jnp.where((segments < lengths.shape[0])[:, None], cotangent, jnp.zeros((), LOW))

    first_out, first_saved = layer_forward(rows, segments, weights[0], small[0])
    second_out, second_saved = layer_forward(first_out.astype(LOW), segments, weights[1], small[1])
    outputs = return_rows(first_out, second_out)
    second_in, second_grads, second_shared, second_own = layer_backward(
        second_saved, segments, cotangent, weights[1], small[1], chips
    )
    first_in, first_grads, first_shared, first_own = layer_backward(
        first_saved, segments, second_in.astype(LOW), weights[0], small[0], chips
    )
    input_grads = return_rows(first_in, second_in)

    back_shard, in_shard, out_shard, qkv_shard = [
        reduce_grad(first_grads[at], second_grads[at]) for at in (3, 2, 1, 0)
    ]
    qkv_grad = jnp.transpose(qkv_shard.reshape(2, 3, head_half, local), (3, 1, 0, 2)).reshape(local, 3, -1)
    out_grad_w = out_shard.reshape(-1, local)
    in_grad = jnp.transpose(in_shard.reshape(-1, local))
    back_grad = back_shard.reshape(-1, local)

    def spread_columns(row):
        blocks = row.reshape(ranks, 1, -1)
        both = jnp.where(jnp.arange(2)[None, :, None] == core, blocks, 0.0)
        return both.reshape(-1, width)

    tables = []
    for shared, own in ((first_shared, first_own), (second_shared, second_own)):
        common = jnp.where(core == 0, relative(jnp.stack(shared)), 0.0)
        tables.append(
            jnp.concatenate(
                [common[:2], spread_columns(own[0]), spread_columns(own[1]), common[2:], spread_columns(own[2])]
            )
        )
    table = jnp.stack(tables)
    table = jnp.where(counted, table, 0.0) if repeats > 1 else table
    table = lax.dynamic_index_in_dim(lax.psum(table, AXES), section, 0, keepdims=False)
    sliced = lax.dynamic_slice_in_dim(table[: gain_count + bias_count], copy_at * local, local, 1)
    inner = lax.dynamic_index_in_dim(
        table[gain_count + bias_count :].reshape(copies, -1), copy_at, 0, keepdims=False
    )
    return (
        outputs,
        input_grads,
        qkv_grad[None],
        out_grad_w[None],
        in_grad[None],
        back_grad[None],
        sliced[None, :gain_count],
        sliced[None, gain_count:],
        inner[None],
    )


def solution(mesh):
    return jax.shard_map(
        on_device,
        mesh=mesh,
        in_specs=(
            P(None, ("dp", "tensor"), None),
            P(None, "dp", None),
            P("section", "dp", None, "tensor"),
            P("section", "tensor", "dp"),
            P("section", "dp", "tensor"),
            P("section", "tensor", "dp"),
            P("section", None, "dp"),
            P("section", None, "dp"),
            P("section", "dp"),
            P(None, ("dp", "tensor"), None),
        ),
        out_specs=(
            P("section", None, ("dp", "tensor"), None),
            P("section", None, ("dp", "tensor"), None),
            P("section", "dp", None, "tensor"),
            P("section", "tensor", "dp"),
            P("section", "dp", "tensor"),
            P("section", "tensor", "dp"),
            P("section", None, "dp"),
            P("section", None, "dp"),
            P("section", "dp"),
        ),
        check_vma=False,
    )
```

time: 3630 us -> 1320 us (0.36)
  waiting for transfers between devices: 2260 us -> 274 us
  matrix products: 580 us -> 131 us
  starting transfers between devices: 30.8 us -> 245 us
  local copies, waits for them, and re-layouts: 331 us -> 181 us
  Pallas kernels: 0 us -> 128 us
  other arithmetic: 333 us -> 211 us
  blocking collectives: 56.7 us -> 122 us
    reduce_scatter x29 -> x4, waiting for transfers between devices: 1500 us -> 0.06 us  [reduce_grad(): lax.psum_scatter(chosen, 'tensor', scatter_dimension=0, tiled=False)]
    all_gather x27 -> x0, waiting for transfers between devices: 714 us -> none  [the longest x6 220 us: layer_backward(): lax.all_gather(first_grad.astype(jnp.bfloat16), 'tensor', axis=0, tiled=T...]
    dot_general x108 -> x8, matrix products: 327 us -> 43.1 us  [matmul(): return jnp.dot(lhs_mat, rhs_mat, preferred_element_type=WIDE)]
    ppermute x10 -> x83, starting transfers between devices: 24.2 us -> 224 us  [move(): return lax.ppermute(value, AXES, pairs)]
    pallas_call x0 -> x4, Pallas kernels: none -> 128 us  [the longest x2 74.8 us: attend_backward(): pl.pallas_call(backward_kernel, grid=(pairs, rows // size), in_specs=atte...]
    ppermute x10 -> x83, waiting for transfers between devices: 49 us -> 176 us  [move(): return lax.ppermute(value, AXES, pairs)]
    unnamed x724 -> x277, local copies, waits for them, and re-layouts: 156 us -> 40.2 us
    reduce_sum x86 -> x11, other arithmetic: 142 us -> 27.3 us  [the longest x4 12.1 us: norm_parts(): centered = summed - jnp.mean(summed, axis=-1, keepdims=True)]
  transfers between devices with their start and end apart: 67 -> 92, of which waited for: 54 -> 20; matrix products, arithmetic and copies ran while one was open for 26% -> 31% of each run, Pallas kernels for 0% -> 8%
where the time goes in v1:
time: 1320 us; the launch traced here: 1310 us
  waiting for transfers between devices  274 us (21%)
  starting transfers between devices  245 us (19%)
  other arithmetic  211 us (16%)
  local copies, waits for them, and re-layouts  181 us (14%)
  matrix products  131 us (10%)
  Pallas kernels  128 us (10%)
  blocking collectives  122 us (9%)
  between operations  18.8 us (1%)
    ppermute x83, starting transfers between devices, move(): return lax.ppermute(value, AXES, pairs)  224 us
    ppermute x83, waiting for transfers between devices, move(): return lax.ppermute(value, AXES, pairs)  176 us
    all_gather x1, blocking collectives, on_device(): lengths = lax.all_gather(seq_lengths, 'dp', axis=1, tiled=True)  112 us
    all_to_all x2, waiting for transfers between devices, return_rows(): lax.all_to_all(chosen, 'tensor', split_axis=0, concat_axis=0, tiled=True)  98.2 us
    pallas_call x2, Pallas kernels, attend_backward(): pl.pallas_call(backward_kernel, grid=(pairs, rows // size), in_specs=atte...  74.8 us
    pallas_call x2, Pallas kernels, attend_forward(): pl.pallas_call(forward_kernel, grid=(pairs, rows // size), in_specs=atten...  53.1 us
    dot_general x8, matrix products, rhs_inner(): lax.dot_general(lhs_mat, rhs_mat, (((1,), (1,)), ((), ())), preferred_ele...  47.1 us
    dynamic_slice x13, local copies, waits for them, and re-layouts, relative(): lax.dynamic_index_in_dim(parts, chip ^ k, axis, keepdims=False)  44.1 us
  transfers between devices with their start and end apart: 92, of which 20 were waited for; matrix products, arithmetic and copies ran while one was open for 31% of the time, Pallas kernels for 8%

profile of v1, /device:TPU:0, one launch (start us, length us, event | category | flops | bytes accessed | tf_op | source)
XLA Modules:
  0.0 1311.0 jit_solution(6949535603238813515)
XLA Ops:
  35.4 9.6 all_gather.6
  97.2 30.2 %collective-permute-done.8 = bf16[512,512]{1,0:T(8,128)(2,1)S(1)} collective-permute-done((bf16[512,512]{1,0:T(8,128)(2,1)}, bf16[512,512]{1,0:T(8,128)(2,1)S(1)}, u32[]{:S(2)}, u32[]{:S(2)}) %collective-permute-start.8) | collective-permute-done | bytes 524320 | tf_op jit(solution)/shard_map/ppermute | solution.py:25
  137.7 10.1 collective-permute-start.31
  178.9 112.3 %all_gather.7 = s32[4,4,4]{2,0,1:T(4,128)S(1)} all-gather(s32[4,1,4]{2,0,1:T(4,128)S(1)} %bitcast.502), channel_id=1, replica_groups=mesh['section'=2,'dp'=4,'tensor'=4] {'dp'}, dimensions={1}, use_global_device_ids=true | all-gather | bytes 320 | tf_op jit(solution)/shard_map/all_gather | solution.py:432
  352.2 26.7 %shard_map.169 = (bf16[1024,512]{1,0:T(8,128)(2,1)S(1)}, f32[4,2,1024]{2,1,0:T(2,128)S(1)}) custom-call(bf16[1024,1536]{1,0:T(8,128)(2,1)S(1)} %add_convert_fusion.1.query_ref.key_ref.value_ref, bf16[1024,1536]{1,0:T(8,128)(2,1)S(1)} %add_convert_fusion.1.query_ref.key_ref.value_ref, bf16[1024,1536]{1,0:T(8,128)(2,1)S(1)} %add_convert_fusion.1.query_ref.key_ref.value_ref, ...), custom_call_target="tpu_custom_call" | custom-call | flops 4294967296 | bytes 4194304 | tf_op jit(solution)/shard_map/pallas_call | solution.py:188
  402.5 7.5 multiply_convert_fusion.1
  430.7 26.5 %shard_map.170 = (bf16[1024,512]{1,0:T(8,128)(2,1)S(1)}, f32[4,2,1024]{2,1,0:T(2,128)S(1)}) custom-call(bf16[1024,1536]{1,0:T(8,128)(2,1)S(1)} %add_convert_fusion.query_ref.key_ref.value_ref, bf16[1024,1536]{1,0:T(8,128)(2,1)S(1)} %add_convert_fusion.query_ref.key_ref.value_ref, bf16[1024,1536]{1,0:T(8,128)(2,1)S(1)} %add_convert_fusion.query_ref.key_ref.value_ref, ...), custom_call_target="tpu_custom_call" | custom-call | flops 4294967296 | bytes 4194304 | tf_op jit(solution)/shard_map/pallas_call | solution.py:188
  511.4 8.5 constant_dynamic-slice_fusion.12
  546.6 10.5 fusion.16
  563.1 9.5 convolution_convert_fusion.15
  619.0 8.1 collective-permute-done.69
  630.5 29.6 %collective-permute-done.78 = bf16[3,512,512]{2,1,0:T(8,128)(2,1)S(1)} collective-permute-done((bf16[3,512,512]{2,1,0:T(8,128)(2,1)S(1)}, bf16[3,512,512]{2,1,0:T(8,128)(2,1)S(1)}, u32[]{:S(2)}, u32[]{:S(2)}) %collective-permute-start.78) | collective-permute-done | bytes 1572896 | tf_op jit(solution)/shard_map/ppermute | solution.py:25
  675.7 37.5 %shard_map.171 = (bf16[1024,1536]{1,0:T(8,128)(2,1)S(1)}, f32[4,2,128]{2,1,0:T(2,128)S(1)}) custom-call(bf16[1024,1536]{1,0:T(8,128)(2,1)} %copy-done.5, bf16[1024,1536]{1,0:T(8,128)(2,1)} %copy-done.5, bf16[1024,1536]{1,0:T(8,128)(2,1)} %copy-done.5, s32[1024,1]{1,0:T(8,128)S(1)} %copy.285.seg_key_ref, s32[1,1024]{1,0:T(1,128)S(1)} %bitcast.360, ...), custom_call_target="tpu_custom_call" | custom-call | flops 10737418240 | bytes 8388608 | tf_op jit(solution)/shard_map/pallas_call | solution.py:210
  774.3 11.6 fusion.18
  791.9 9.6 convolution_convert_fusion.13
  814.3 9.4 collective-permute-done.67
  849.0 37.3 %shard_map.172 = (bf16[1024,1536]{1,0:T(8,128)(2,1)S(1)}, f32[4,2,128]{2,1,0:T(2,128)S(1)}) custom-call(bf16[1024,1536]{1,0:T(8,128)(2,1)} %copy-done.4, bf16[1024,1536]{1,0:T(8,128)(2,1)} %copy-done.4, bf16[1024,1536]{1,0:T(8,128)(2,1)} %copy-done.4, s32[1024,1]{1,0:T(8,128)S(1)} %copy.285.seg_key_ref, s32[1,1024]{1,0:T(1,128)S(1)} %bitcast.361, ...), custom_call_target="tpu_custom_call" | custom-call | flops 10737418240 | bytes 8388608 | tf_op jit(solution)/shard_map/pallas_call | solution.py:210
  909.6 50.2 %collective-permute-done.57 = bf16[4,128,512]{1,2,0:T(8,128)(2,1)S(1)} collective-permute-done((bf16[4,128,512]{1,2,0:T(8,128)(2,1)S(1)}, bf16[4,128,512]{1,2,0:T(8,128)(2,1)S(1)}, u32[]{:S(2)}, u32[]{:S(2)}) %collective-permute-start.57) | collective-permute-done | bytes 524320 | tf_op jit(solution)/shard_map/ppermute | solution.py:25
  1023.3 49.7 %collective-permute-start.52 = (bf16[4,384,512]{1,2,0:T(8,128)(2,1)}, bf16[4,384,512]{1,2,0:T(8,128)(2,1)}, u32[]{:S(2)}, u32[]{:S(2)}) collective-permute-start(bf16[4,384,512]{1,2,0:T(8,128)(2,1)} %pad_maximum_fusion.19), channel_id=1, source_target_pairs={{0,16},{1,17},{2,18},{3,19},{4,20},{5,21},{6,22},{7,23},{8,24},{9,... | collective-permute-start | bytes 4718600 | tf_op jit(solution)/shard_map/ppermute | solution.py:25
  1074.7 15.3 %collective-permute-done.75 = bf16[4,512,512]{2,1,0:T(8,128)(2,1)} collective-permute-done((bf16[4,512,512]{2,1,0:T(8,128)(2,1)}, bf16[4,512,512]{2,1,0:T(8,128)(2,1)}, u32[]{:S(2)}, u32[]{:S(2)}) %collective-permute-start.75) | collective-permute-done | bytes 2097184 | tf_op jit(solution)/shard_map/ppermute | solution.py:25
  1097.8 8.3 select_convert_fusion
  1144.2 44.4 %all-to-all-done.3 = bf16[4,256,1024]{2,1,0:T(8,128)(2,1)} async-done(((bf16[4,256,1024]{2,1,0:T(8,128)(2,1)}), bf16[4,256,1024]{2,1,0:T(8,128)(2,1)}, u32[]{:S(2)}, u32[]{:S(2)}) %all-to-all-start.3) | async-done | bytes 2097184 | tf_op jit(solution)/shard_map/all_to_all | solution.py:322
  1212.5 53.8 %all-to-all-done.1 = bf16[4,256,1024]{2,1,0:T(8,128)(2,1)} async-done(((bf16[4,256,1024]{2,1,0:T(8,128)(2,1)}), bf16[4,256,1024]{2,1,0:T(8,128)(2,1)}, u32[]{:S(2)}, u32[]{:S(2)}) %all-to-all-start.1) | async-done | bytes 2097184 | tf_op jit(solution)/shard_map/all_to_all | solution.py:322
  1266.4 17.1 %collective-permute-start.39 = (bf16[4,256,1024]{2,1,0:T(8,128)(2,1)}, bf16[4,256,1024]{2,1,0:T(8,128)(2,1)}, u32[]{:S(2)}, u32[]{:S(2)}) collective-permute-start(bf16[4,256,1024]{2,1,0:T(8,128)(2,1)} %all-to-all-done.1), channel_id=1, source_target_pairs={{0,0},{1,1},{2,2},{3,3},{4,16},{5,17},{6,18},{7,19},{8,8},{9,9},{1... | collective-permute-start | bytes 6291464 | tf_op jit(solution)/shard_map/ppermute | solution.py:25
  (766 shorter events, 659.0 us)
Async XLA Ops:
  65.8 94.1 %all-to-all-start = ((bf16[4,128,1024]{2,1,0:T(8,128)(2,1)}), bf16[4,128,1024]{2,1,0:T(8,128)(2,1)S(1)}, u32[]{:S(2)}, u32[]{:S(2)}) async-start(bf16[4,128,1024]{2,1,0:T(8,128)(2,1)} %bitcast_select_fusion.1), calls=%async_computation | async-start | bytes 2097152 | tf_op jit(solution)/shard_map/all_to_all | solution.py:315
  154.5 146.1 %collective-permute-start.10 = (bf16[4,512,512]{2,1,0:T(8,128)(2,1)}, bf16[4,512,512]{2,1,0:T(8,128)(2,1)}, u32[]{:S(2)}, u32[]{:S(2)}) collective-permute-start(bf16[4,512,512]{2,1,0:T(8,128)(2,1)} %bitcast_dynamic-update-slice_fusion.6), channel_id=1, source_target_pairs={{0,8},{1,9},{2,10},{3,11},{4,12},{5,13},{6,14},{7,15},{8,0},{9,1},... | collective-permute-start | bytes 6291464 | tf_op jit(solution)/shard_map/ppermute | solution.py:25
  162.5 141.9 %collective-permute-start.32 = (bf16[4,512,512]{2,1,0:T(8,128)(2,1)}, bf16[4,512,512]{2,1,0:T(8,128)(2,1)}, u32[]{:S(2)}, u32[]{:S(2)}) collective-permute-start(bf16[4,512,512]{2,1,0:T(8,128)(2,1)} %bitcast_dynamic-update-slice_fusion), channel_id=1, source_target_pairs={{0,16},{1,17},{2,18},{3,19},{4,20},{5,21},{6,22},{7,23},{8,24},{9,... | collective-permute-start | bytes 6291464 | tf_op jit(solution)/shard_map/ppermute | solution.py:25
  168.8 154.9 %collective-permute-start.33 = (bf16[4,512,512]{2,1,0:T(8,128)(2,1)}, bf16[4,512,512]{2,1,0:T(8,128)(2,1)}, u32[]{:S(2)}, u32[]{:S(2)}) collective-permute-start(bf16[4,512,512]{2,1,0:T(8,128)(2,1)} %bitcast_dynamic-update-slice_fusion), channel_id=1, source_target_pairs={{0,8},{1,9},{2,10},{3,11},{4,12},{5,13},{6,14},{7,15},{8,0},{9,1},... | collective-permute-start | bytes 6291464 | tf_op jit(solution)/shard_map/ppermute | solution.py:25
  172.3 155.2 %collective-permute-start.21 = (bf16[4,512,512]{2,1,0:T(8,128)(2,1)}, bf16[4,512,512]{2,1,0:T(8,128)(2,1)}, u32[]{:S(2)}, u32[]{:S(2)}) collective-permute-start(bf16[4,512,512]{2,1,0:T(8,128)(2,1)} %bitcast_dynamic-update-slice_fusion.3), channel_id=1, source_target_pairs={{0,16},{1,17},{2,18},{3,19},{4,20},{5,21},{6,22},{7,23},{8,24},{9,... | collective-permute-start | bytes 6291464 | tf_op jit(solution)/shard_map/ppermute | solution.py:25
  178.1 152.2 %collective-permute-start.22 = (bf16[4,512,512]{2,1,0:T(8,128)(2,1)}, bf16[4,512,512]{2,1,0:T(8,128)(2,1)}, u32[]{:S(2)}, u32[]{:S(2)}) collective-permute-start(bf16[4,512,512]{2,1,0:T(8,128)(2,1)} %bitcast_dynamic-update-slice_fusion.3), channel_id=1, source_target_pairs={{0,8},{1,9},{2,10},{3,11},{4,12},{5,13},{6,14},{7,15},{8,0},{9,1},... | collective-permute-start | bytes 6291464 | tf_op jit(solution)/shard_map/ppermute | solution.py:25
  471.1 727.3 %all-reduce.2.cloned.1.call-start = ((), (), s32[]{:S(2)}) async-start(), calls=%async_computation.12 | async-start | bytes 196608 | tf_op jit(solution)/shard_map/psum | solution.py:473
  610.1 359.7 %collective-permute-start.72 = (bf16[4,512,512]{2,1,0:T(8,128)(2,1)}, bf16[4,512,512]{2,1,0:T(8,128)(2,1)}, u32[]{:S(2)}, u32[]{:S(2)}) collective-permute-start(bf16[4,512,512]{2,1,0:T(8,128)(2,1)} %pad_maximum_fusion.12), channel_id=1, source_target_pairs={{16,24},{17,25},{18,26},{19,27},{20,28},{21,29},{22,30},{23,31},{2... | collective-permute-start | bytes 6291464 | tf_op jit(solution)/shard_map/ppermute | solution.py:25
  755.2 137.4 %collective-permute-start.63 = (bf16[4,128,512]{1,2,0:T(8,128)(2,1)}, bf16[4,128,512]{1,2,0:T(8,128)(2,1)}, u32[]{:S(2)}, u32[]{:S(2)}) collective-permute-start(bf16[4,128,512]{1,2,0:T(8,128)(2,1)} %pad_maximum_fusion.27), channel_id=1, source_target_pairs={{16,24},{17,25},{18,26},{19,27},{20,28},{21,29},{22,30},{23,31},{2... | collective-permute-start | bytes 1572872 | tf_op jit(solution)/shard_map/ppermute | solution.py:25
  892.6 81.7 %collective-permute-start.70 = (bf16[4,512,512]{2,1,0:T(8,128)(2,1)}, bf16[4,512,512]{2,1,0:T(8,128)(2,1)}, u32[]{:S(2)}, u32[]{:S(2)}) collective-permute-start(bf16[4,512,512]{2,1,0:T(8,128)(2,1)} %pad_maximum_fusion.11), channel_id=1, source_target_pairs={{0,16},{1,17},{2,18},{3,19},{4,20},{5,21},{6,22},{7,23},{8,24},{9,... | collective-permute-start | bytes 6291464 | tf_op jit(solution)/shard_map/ppermute | solution.py:25
  897.6 79.3 %collective-permute-start.68 = (bf16[4,512,512]{2,1,0:T(8,128)(2,1)}, bf16[4,512,512]{2,1,0:T(8,128)(2,1)}, u32[]{:S(2)}, u32[]{:S(2)}) collective-permute-start(bf16[4,512,512]{2,1,0:T(8,128)(2,1)} %pad_maximum_fusion.10), channel_id=1, source_target_pairs={{0,8},{1,9},{2,10},{3,11},{4,12},{5,13},{6,14},{7,15},{8,0},{9,1},... | collective-permute-start | bytes 6291464 | tf_op jit(solution)/shard_map/ppermute | solution.py:25
  900.0 78.7 %collective-permute-start.66 = (bf16[4,512,512]{2,1,0:T(8,128)(2,1)}, bf16[4,512,512]{2,1,0:T(8,128)(2,1)}, u32[]{:S(2)}, u32[]{:S(2)}) collective-permute-start(bf16[4,512,512]{2,1,0:T(8,128)(2,1)} %pad_maximum_fusion.9), channel_id=1, source_target_pairs={{16,0},{17,1},{18,2},{19,3},{20,4},{21,5},{22,6},{23,7},{24,8},{25... | collective-permute-start | bytes 6291464 | tf_op jit(solution)/shard_map/ppermute | solution.py:25
  909.6 291.5 %reduce-scatter.7.cloned.1.call-start = ((), (), s32[]{:S(2)}) async-start(), calls=%async_computation.9 | async-start | bytes 655360 | tf_op jit(solution)/shard_map/reduce_scatter | solution.py:387
  964.4 241.6 %reduce-scatter.9.cloned.1.call-start = ((), (), s32[]{:S(2)}) async-start(), calls=%async_computation.10 | async-start | bytes 2621440 | tf_op jit(solution)/shard_map/reduce_scatter | solution.py:387
  985.3 222.0 %reduce-scatter.11.cloned.1.call-start = ((), (), s32[]{:S(2)}) async-start(), calls=%async_computation.11 | async-start | bytes 2621440 | tf_op jit(solution)/shard_map/reduce_scatter | solution.py:387
  993.9 79.0 %collective-permute-start.77 = (bf16[4,512,512]{2,1,0:T(8,128)(2,1)}, bf16[4,512,512]{2,1,0:T(8,128)(2,1)}, u32[]{:S(2)}, u32[]{:S(2)}) collective-permute-start(bf16[4,512,512]{2,1,0:T(8,128)(2,1)} %pad_maximum_fusion.14), channel_id=1, source_target_pairs={{0,8},{1,9},{2,10},{3,11},{4,12},{5,13},{6,14},{7,15},{8,0},{9,1},... | collective-permute-start | bytes 6291464 | tf_op jit(solution)/shard_map/ppermute | solution.py:25
  1002.0 88.0 %collective-permute-start.75 = (bf16[4,512,512]{2,1,0:T(8,128)(2,1)}, bf16[4,512,512]{2,1,0:T(8,128)(2,1)}, u32[]{:S(2)}, u32[]{:S(2)}) collective-permute-start(bf16[4,512,512]{2,1,0:T(8,128)(2,1)} %pad_maximum_fusion.13), channel_id=1, source_target_pairs={{16,0},{17,1},{18,2},{19,3},{20,4},{21,5},{22,6},{23,7},{24,8},{25... | collective-permute-start | bytes 6291464 | tf_op jit(solution)/shard_map/ppermute | solution.py:25
  1008.5 89.3 %collective-permute-start.45 = (bf16[1024,1024]{0,1:T(8,128)(2,1)}, bf16[1024,1024]{0,1:T(8,128)(2,1)}, u32[]{:S(2)}, u32[]{:S(2)}) collective-permute-start(bf16[1024,1024]{0,1:T(8,128)(2,1)} %convolution_convert_fusion.12), channel_id=1, source_target_pairs={{0,4},{1,5},{2,6},{3,7},{4,0},{5,1},{6,2},{7,3},{8,12},{9,13},{10,... | collective-permute-start | bytes 6291464 | tf_op jit(solution)/shard_map/ppermute | solution.py:25
  1021.5 171.6 %collective-permute-start.54 = (bf16[4,384,512]{1,2,0:T(8,128)(2,1)}, bf16[4,384,512]{1,2,0:T(8,128)(2,1)}, u32[]{:S(2)}, u32[]{:S(2)}) collective-permute-start(bf16[4,384,512]{1,2,0:T(8,128)(2,1)} %pad_maximum_fusion.20), channel_id=1, source_target_pairs={{16,24},{17,25},{18,26},{19,27},{20,28},{21,29},{22,30},{23,31},{2... | collective-permute-start | bytes 4718600 | tf_op jit(solution)/shard_map/ppermute | solution.py:25
  1023.3 169.8 %collective-permute-start.52 = (bf16[4,384,512]{1,2,0:T(8,128)(2,1)}, bf16[4,384,512]{1,2,0:T(8,128)(2,1)}, u32[]{:S(2)}, u32[]{:S(2)}) collective-permute-start(bf16[4,384,512]{1,2,0:T(8,128)(2,1)} %pad_maximum_fusion.19), channel_id=1, source_target_pairs={{0,16},{1,17},{2,18},{3,19},{4,20},{5,21},{6,22},{7,23},{8,24},{9,... | collective-permute-start | bytes 4718600 | tf_op jit(solution)/shard_map/ppermute | solution.py:25
  1188.6 77.8 %all-to-all-start.1 = ((bf16[4,256,1024]{2,1,0:T(8,128)(2,1)}), bf16[4,256,1024]{2,1,0:T(8,128)(2,1)}, u32[]{:S(2)}, u32[]{:S(2)}) async-start(bf16[4,256,1024]{2,1,0:T(8,128)(2,1)} %pad_maximum_fusion.6), calls=%async_computation.1 | async-start | bytes 4194304 | tf_op jit(solution)/shard_map/all_to_all | solution.py:322
  1193.0 93.5 %reduce-scatter.5.cloned.1.call-start = ((), (), s32[]{:S(2)}) async-start(), calls=%async_computation.8 | async-start | bytes 1966080 | tf_op jit(solution)/shard_map/reduce_scatter | solution.py:387
  1203.7 93.0 %collective-permute-start.46 = (bf16[4,256,1024]{2,1,0:T(8,128)(2,1)}, bf16[4,256,1024]{2,1,0:T(8,128)(2,1)S(1)}, u32[]{:S(2)}, u32[]{:S(2)}) collective-permute-start(bf16[4,256,1024]{2,1,0:T(8,128)(2,1)} %all-to-all-done.3), channel_id=1, source_target_pairs={{0,0},{1,1},{2,2},{3,3},{4,16},{5,17},{6,18},{7,19},{8,8},{9,9},{1... | collective-permute-start | bytes 6291464 | tf_op jit(solution)/shard_map/ppermute | solution.py:25
  1210.5 79.2 %collective-permute-start.73 = (bf16[512,256]{1,0:T(8,128)(2,1)S(1)}, bf16[512,256]{1,0:T(8,128)(2,1)}, u32[]{:S(2)}, u32[]{:S(2)}) collective-permute-start(bf16[512,256]{1,0:T(8,128)(2,1)S(1)} %bitcast.435), channel_id=1, source_target_pairs={{0,4},{1,5},{2,6},{3,7},{4,0},{5,1},{6,2},{7,3},{8,12},{9,13},{10,... | collective-permute-start | bytes 786440 | tf_op jit(solution)/shard_map/ppermute | solution.py:25
  (201 other events, 4197.9 us)
Sparse Core Ops, SparseCore 0:
  909.7 148.2 all-reduce.1
Sparse Core Ops, SparseCore 1:
  964.5 21.8 reduce-scatter.6
  988.5 42.8 reduce-scatter.8
  1097.8 67.2 reduce-scatter.10
  1198.4 64.7 reduce-scatter.4

commit v2 on v1

--- a/solution.py
+++ b/solution.py
@@ -30,9 +30,22 @@
 
 
 def by_core(core, kept, received, axis):
-    first = jnp.where(core == 0, kept, received)
-    second = jnp.where(core == 0, received, kept)
-    return jnp.stack([first, second], axis=axis)
+    return jnp.where(
+        core == 0,
+        jnp.concatenate([kept, received], axis=axis),
+        jnp.concatenate([received, kept], axis=axis),
+    )
+
+
+def choose(place, options):
+    chosen = options[0]
+    for at, option in enumerate(options[1:], 1):
+        chosen = jnp.where(place == at, option, chosen)
+    return chosen
+
+
+def after(value, *others):
+    return lax.optimization_barrier((value,) + others)[0]
 
 
 def matmul(lhs_mat, rhs_mat):
@@ -258,29 +271,33 @@
     return [lhs_inner(hidden, features[:, k * cut : (k + 1) * cut]).astype(LOW) for k in range(chips)]
 
 
-def layer_backward(saved, segments, grad_rows, weights, small, chips):
-    w_qkv, w_out, w_in, w_back = weights
-    gains, biases, _, _, head_half = small
-    lanes = max(head_half, 128)
-    rows, packed, logsums, context, first_sum, middle, active, slope, second_sum = saved
+def backward_hidden(saved, grad_rows, weights, small):
+    _, _, w_in, w_back = weights
+    gains = small[0]
+    middle, active, slope, second_sum = saved[5:]
     second_grad, gain_two, bias_two = norm_backward(second_sum, gains[1], grad_rows.astype(WIDE))
     branch_grad = second_grad.astype(LOW)
     hidden_grad = rhs_inner(branch_grad, w_back) * slope.astype(WIDE)
     hidden_low = hidden_grad.astype(LOW)
     middle_grad = second_grad + core_sum(matmul(hidden_low, w_in))
-    back_grad = slab_grads(active, branch_grad, chips)
-    in_grad = slab_grads(hidden_low, middle, chips)
+    sums = (gain_two, jnp.sum(second_grad, axis=0), bias_two, jnp.sum(hidden_grad, axis=0))
+    return middle_grad, branch_grad, hidden_low, sums
+
+
+def backward_attention(saved, segments, middle_grad, weights, small):
+    _, w_out, _, _ = weights
+    gains, head_half = small[0], small[4]
+    _, packed, logsums, _, first_sum = saved[:5]
     first_grad, gain_one, bias_one = norm_backward(first_sum, gains[0], middle_grad)
     attended_grad = first_grad.astype(LOW)
     context_grad = rhs_inner(attended_grad, w_out).astype(LOW)
-    packed_low, sums = attend_backward(packed, segments, logsums, context_grad, lanes)
+    lanes = max(head_half, 128)
+    packed_low, column_sums = attend_backward(packed, segments, logsums, context_grad, lanes)
     packed_low = pair_columns(packed_low, head_half, lanes, back=True)
-    input_grad = first_grad + core_sum(matmul(packed_low, w_qkv))
-    out_grad = slab_grads(context, attended_grad, chips)
-    qkv_grad = slab_grads(packed_low, rows, chips)
-    shared = (gain_one, gain_two, jnp.sum(first_grad, axis=0), bias_one, jnp.sum(second_grad, axis=0), bias_two)
-    own = (sums[:, 0].reshape(-1), sums[:, 1].reshape(-1), jnp.sum(hidden_grad, axis=0))
-    return input_grad, (qkv_grad, out_grad, in_grad, back_grad), shared, own
+    sums = (gain_one, jnp.sum(first_grad, axis=0), bias_one) + tuple(
+        column_sums[:, at].reshape(-1) for at in range(2)
+    )
+    return first_grad, attended_grad, packed_low, sums
 
 
 def on_device(
@@ -300,15 +317,13 @@
     counted = (rank % repeats) == 0
 
     def relative(value):
-        parts = value.reshape(value.shape[:-1] + (chips, width // chips))
-        axis = parts.ndim - 2
-        ordered = [lax.dynamic_index_in_dim(parts, chip ^ k, axis, keepdims=False) for k in range(chips)]
-        return jnp.concatenate(ordered, axis=-1)
+        slabs = jnp.split(value, chips, axis=-1)
+        return jnp.concatenate([choose(chip ^ k, slabs) for k in range(chips)], axis=-1)
 
     def fetch_rows(block):
         parts = block.reshape(micro_count, 2, own_rows // 2, width)
-        kept = lax.dynamic_index_in_dim(parts, core, 1, keepdims=False)
-        given = lax.dynamic_index_in_dim(parts, 1 - core, 1, keepdims=False)
+        kept = choose(core, (parts[:, 0], parts[:, 1]))
+        given = choose(core, (parts[:, 1], parts[:, 0]))
         received = move(given, lambda s, d, t: (s, d ^ 1, t) if d % 2 == s else None)
         mine = jnp.where(core == section, kept, received)
         mine = jnp.repeat(mine, repeats, axis=0) if repeats > 1 else mine
@@ -324,15 +339,12 @@
         placed = move(spread, lambda s, d, t: (d % 2, (d // 2) * 2 + s, t))
         return placed.astype(WIDE)[None]
 
-    def gather_weight(halves):
-        kept = lax.dynamic_index_in_dim(halves, core, 0, keepdims=False)
-        given = lax.dynamic_index_in_dim(halves, 1 - core, 0, keepdims=False)
-        received = to_other_core(given)
-        own = jnp.where(
-            core == 0,
-            jnp.concatenate([kept, received], axis=1),
-            jnp.concatenate([received, kept], axis=1),
-        )
+    def own_half(halves):
+        kept = choose(core, (halves[0], halves[1]))
+        given = choose(core, (halves[1], halves[0]))
+        return by_core(core, kept, to_other_core(given), 1)
+
+    def over_ranks(own):
         upward, downward = [own], [own]
         for _ in range(1, ranks):
             upward.append(move(upward[-1], lambda s, d, t: (s, d, t + 1) if t + 1 < ranks else None))
@@ -342,53 +354,60 @@
         for j in range(1, ranks):
             arrived = jnp.where(rank >= j, upward[j], downward[ranks - j])
             item = lax.dynamic_update_index_in_dim(item, arrived, (rank + ranks - j) % ranks, 0)
+        return item
+
+    def over_chips(item):
+        part = item.shape[0] // 2
         across = move(item, lambda s, d, t: (1 - s, d, t))
         along = [move(item, lambda s, d, t: (s, d ^ (2 * k), t)) for k in range(1, chips)]
-        cut = ranks // 2
         far = []
         for k in range(1, chips):
-            upper = move(across[:cut], lambda s, d, t: (s, d ^ (2 * k), t))
-            lower = move(along[k - 1][cut:], lambda s, d, t: (1 - s, d, t))
+            upper = move(across[:part], lambda s, d, t: (s, d ^ (2 * k), t))
+            lower = move(along[k - 1][part:], lambda s, d, t: (1 - s, d, t))
             far.append(jnp.concatenate([upper, lower], axis=0))
         mine, other = [item] + along, [across] + far
         result = []
         for layer in range(2):
             slabs = [jnp.where(section == layer, m, o) for m, o in zip(mine, other)]
-            result.append(jnp.concatenate(slabs, axis=2))
+            result.append(jnp.concatenate(slabs, axis=-1))
         return result
 
-    def fold(parts, layer):
-        cut = ranks // 4
-        off = lambda s: s != layer
-        near = parts[0][cut:].astype(WIDE)
-        uppers = []
+    def gather_weight(own):
+        return over_chips(over_ranks(own))
+
+    def gather_weight_late(own):
+        both = over_ranks(jnp.stack(over_chips(own)))
+        return [both[:, layer] for layer in range(2)]
+
+    def along_x(parts):
+        slabs = jnp.split(parts, chips, axis=-1)
+        total = slabs[0].astype(WIDE)
         for k in range(1, chips):
-            sent = move(parts[k][:cut], lambda s, d, t: (layer, d, t) if off(s) else None)
-            uppers.append((parts[k][:cut].astype(WIDE) + sent.astype(WIDE)).astype(LOW))
-            got = move(parts[k][cut:], lambda s, d, t: (s, d ^ (2 * k), t) if off(s) else None)
-            near = near + got.astype(WIDE)
-        near = jnp.concatenate([parts[0][:cut], near.astype(LOW)], axis=0)
-        total = near.astype(WIDE)
-        total = total + move(near, lambda s, d, t: (layer, d, t) if off(s) else None).astype(WIDE)
+            total = total + move(slabs[k], lambda s, d, t: (s, d ^ (2 * k), t)).astype(WIDE)
+        return total.astype(LOW)
+
+    def slabs_along_x(slabs):
+        total = slabs[0].astype(WIDE)
         for k in range(1, chips):
-            whole = jnp.concatenate([uppers[k - 1], parts[k][cut:]], axis=0)
-            got = move(whole, lambda s, d, t: (s, d ^ (2 * k), t) if not off(s) else None)
-            total = total + got.astype(WIDE)
+            total = total + move(slabs[k], lambda s, d, t: (s, d ^ (2 * k), t)).astype(WIDE)
         return total.astype(LOW)
 
-    def reduce_grad(first, second):
-        folded = []
-        for layer, slabs in enumerate((first, second)):
-            slabs = [slab.reshape(ranks, -1, slab.shape[1]) for slab in slabs]
-            if repeats > 1:
-                slabs = [jnp.where(counted, slab, jnp.zeros((), LOW)) for slab in slabs]
-            folded.append(fold(slabs, layer))
-        chosen = jnp.where(section == 0, folded[0], folded[1])
-        shard = lax.psum_scatter(chosen, "tensor", scatter_dimension=0, tiled=False).astype(LOW)
-        shard = shard.reshape(shard.shape[0], 2, local)
-        kept = lax.dynamic_index_in_dim(shard, core, 1, keepdims=False)
-        given = lax.dynamic_index_in_dim(shard, 1 - core, 1, keepdims=False)
-        return by_core(core, kept, to_other_core(given), 0).astype(WIDE)
+    def to_layer(part, layer):
+        sent = move(part, lambda s, d, t: (layer, d, t) if s != layer else None)
+        return (part.astype(WIDE) + sent.astype(WIDE)).astype(LOW)
+
+    def over_z(parts):
+        parts = parts.reshape((ranks, -1) + parts.shape[1:])
+        return lax.psum_scatter(parts, "tensor", scatter_dimension=0, tiled=False).astype(LOW)
+
+    def counted_only(slabs):
+        return [jnp.where(counted, slab, jnp.zeros((), LOW)) for slab in slabs] if repeats > 1 else slabs
+
+    def finish(shard):
+        parts = jnp.split(shard, 2, axis=1)
+        kept = choose(core, parts)
+        given = choose(core, parts[::-1])
+        return by_core(core, kept[None], to_other_core(given)[None], 0).astype(WIDE)
 
     rows = fetch_rows(block_input)
     head_half = w_qkv.shape[-1] // 2
@@ -397,9 +416,14 @@
     qkv_first = jnp.transpose(w_qkv[0].reshape(local, 3, 2, head_half), (2, 1, 3, 0))
     qkv_first = qkv_first.reshape(2, 3 * head_half, local)
     out_first = w_out[0].reshape(2, head_half, local)
-    attention_all = gather_weight(jnp.concatenate([qkv_first, out_first], axis=1))
-    in_all = gather_weight(in_first)
-    back_all = gather_weight(w_back[0].reshape(2, hidden_half, local))
+    back_first = w_back[0].reshape(2, hidden_half, local)
+    later = hidden_half // 2
+    attention_all = gather_weight(own_half(jnp.concatenate([qkv_first, out_first], axis=1)))
+    back_own = own_half(back_first)
+    in_all = gather_weight(own_half(in_first))
+    back_one = gather_weight(back_own[:later])
+    back_two = gather_weight_late(back_own[later:])
+    back_all = [jnp.concatenate(pair, axis=1) for pair in zip(back_one, back_two)]
     weights = [
         (
             attention_all[layer][:, : 3 * head_half].reshape(-1, width),
@@ -412,11 +436,26 @@
 
     gain_count, bias_count = gains.shape[1], biases.shape[1]
     packed_small = jnp.concatenate([gains, biases, ffn_bias.reshape(1, -1, local)], axis=1)
-    small_all = lax.all_gather(packed_small, ("section", "dp"), axis=0, tiled=True).astype(WIDE)
-    small_all = small_all.reshape(2, copies, -1, local)
+    table_parts = [
+        [
+            packed_small
+            if a == 0 and b == 0
+            else move(packed_small, lambda s, d, t: (s ^ a, d ^ b, t))
+            for b in range(copies)
+        ]
+        for a in range(2)
+    ]
+    table_all = jnp.stack([jnp.stack(row) for row in table_parts])[:, :, 0].astype(WIDE)
+    small_all = jnp.stack([choose(section, (table_all[at], table_all[1 - at])) for at in range(2)])
+    order = [[at ^ b for b in range(copies)] for at in range(copies)]
+    small_all = jnp.stack(
+        [choose(copy_at, [small_all[:, order[at][b]] for b in range(copies)]) for at in range(copies)],
+        axis=1,
+    )
 
     def head_columns(row):
-        return lax.dynamic_index_in_dim(row.reshape(ranks, 2, -1), core, 1, keepdims=False).reshape(-1)
+        halves = row.reshape(ranks, 2, -1)
+        return choose(core, (halves[:, 0], halves[:, 1])).reshape(-1)
 
     small = []
     for layer in range(2):
@@ -429,9 +468,8 @@
         table = relative(table)
         small.append((table[:gain_count], table[gain_count:], offset, inner_bias, head_half))
 
-    lengths = lax.all_gather(seq_lengths, "dp", axis=1, tiled=True)
-    group_at = chip * 2 + section
-    lengths = lengths[rank // repeats, group_at]
+    lengths = jnp.where(core == section, seq_lengths, to_other_core(seq_lengths))[:, 0]
+    lengths = lax.dynamic_index_in_dim(lengths, rank // repeats, 0, keepdims=False)
     segments = segment_ids(lengths, ranks * own_rows)
     cotangent = fetch_rows(out_grad)
     cotangent = jnp.where((segments < lengths.shape[0])[:, None], cotangent, jnp.zeros((), LOW))
@@ -439,17 +477,59 @@
     first_out, first_saved = layer_forward(rows, segments, weights[0], small[0])
     second_out, second_saved = layer_forward(first_out.astype(LOW), segments, weights[1], small[1])
     outputs = return_rows(first_out, second_out)
-    second_in, second_grads, second_shared, second_own = layer_backward(
-        second_saved, segments, cotangent, weights[1], small[1], chips
-    )
-    first_in, first_grads, first_shared, first_own = layer_backward(
-        first_saved, segments, second_in.astype(LOW), weights[0], small[0], chips
-    )
+
+    def feed_forward_grads(saved, branch_grad, hidden_low):
+        back = counted_only(slab_grads(saved[6], branch_grad, chips))
+        inner = counted_only([lhs_inner(hidden_low, saved[5]).astype(LOW)])[0]
+        return back, inner
+
+    def attention_grads(saved, attended_grad, packed_low):
+        out = slab_grads(saved[3], attended_grad, chips)
+        qkv = slab_grads(packed_low, saved[0], chips)
+        return counted_only(out), counted_only(qkv)
+
+    middle_grad, branch_grad, hidden_low, second_sums = backward_hidden(
+        second_saved, cotangent, weights[1], small[1]
+    )
+    back_slabs, inner = feed_forward_grads(second_saved, branch_grad, hidden_low)
+    back_two = slabs_along_x(back_slabs)
+    in_two = over_z(inner)
+    first_grad, attended_grad, packed_low, more_sums = backward_attention(
+        second_saved, segments, middle_grad, weights[1], small[1]
+    )
+    second_sums += more_sums
+    packed_low = after(packed_low, back_two)
+    back_two = to_layer(back_two, 1)
+    second_in = first_grad + core_sum(matmul(packed_low, weights[1][0]))
+    out_slabs, qkv_slabs = attention_grads(second_saved, attended_grad, packed_low)
+    qkv_two, out_two = slabs_along_x(qkv_slabs), slabs_along_x(out_slabs)
+
+    middle_grad, branch_grad, hidden_low, first_sums = backward_hidden(
+        first_saved, second_in.astype(LOW), weights[0], small[0]
+    )
+    middle_grad = after(middle_grad, back_two, in_two, outputs)
+    in_two = along_x(in_two)
+    back_slabs, inner = feed_forward_grads(first_saved, branch_grad, hidden_low)
+    back_one = slabs_along_x(back_slabs)
+    in_one = over_z(inner)
+    first_grad, attended_grad, packed_low, more_sums = backward_attention(
+        first_saved, segments, middle_grad, weights[0], small[0]
+    )
+    first_sums += more_sums
+    packed_low = after(packed_low, qkv_two, out_two, in_two)
+    in_two, qkv_two, out_two = to_layer(in_two, 1), to_layer(qkv_two, 1), to_layer(out_two, 1)
+    first_in = first_grad + core_sum(matmul(packed_low, weights[0][0]))
+    out_slabs, qkv_slabs = attention_grads(first_saved, attended_grad, packed_low)
+    back_one = to_layer(back_one, 0)
+    qkv_one, out_one = slabs_along_x(qkv_slabs), slabs_along_x(out_slabs)
     input_grads = return_rows(first_in, second_in)
-
-    back_shard, in_shard, out_shard, qkv_shard = [
-        reduce_grad(first_grads[at], second_grads[at]) for at in (3, 2, 1, 0)
-    ]
+    back_shard = over_z(jnp.where(section == 0, back_one, back_two))
+    in_one = to_layer(along_x(in_one), 0)
+    in_shard = finish(jnp.where(section == 0, in_one, in_two))
+    qkv_one, out_one = to_layer(qkv_one, 0), to_layer(out_one, 0)
+    back_shard = finish(back_shard)
+    out_shard = finish(over_z(jnp.where(section == 0, out_one, out_two)))
+    qkv_shard = finish(over_z(jnp.where(section == 0, qkv_one, qkv_two)))
     qkv_grad = jnp.transpose(qkv_shard.reshape(2, 3, head_half, local), (3, 1, 0, 2)).reshape(local, 3, -1)
     out_grad_w = out_shard.reshape(-1, local)
     in_grad = jnp.transpose(in_shard.reshape(-1, local))
@@ -461,11 +541,13 @@
         return both.reshape(-1, width)
 
     tables = []
-    for shared, own in ((first_shared, first_own), (second_shared, second_own)):
-        common = jnp.where(core == 0, relative(jnp.stack(shared)), 0.0)
+    for sums in (first_sums, second_sums):
+        gain_two, bias_four, bias_five, inner_sum, gain_one, bias_two, bias_three, query_sum, value_sum = sums
+        common = jnp.stack([gain_one, gain_two, bias_two, bias_three, bias_four, bias_five])
+        common = jnp.where(core == 0, relative(common), 0.0)
         tables.append(
             jnp.concatenate(
-                [common[:2], spread_columns(own[0]), spread_columns(own[1]), common[2:], spread_columns(own[2])]
+                [common[:2], spread_columns(query_sum), spread_columns(value_sum), common[2:], spread_columns(inner_sum)]
             )
         )
     table = jnp.stack(tables)

time: 1320 us -> 1140 us (0.86)
  waiting for transfers between devices: 274 us -> 428 us
  blocking collectives: 122 us -> 0 us
  local copies, waits for them, and re-layouts: 181 us -> 63.5 us
  starting transfers between devices: 245 us -> 174 us
  other arithmetic: 211 us -> 147 us
  matrix products: 131 us -> 173 us
    all_gather x2 -> x0, blocking collectives: 122 us -> none  [the longest x1 112 us: on_device(): lengths = lax.all_gather(seq_lengths, 'dp', axis=1, tiled=True)]
    reduce_scatter x4 -> x5, waiting for transfers between devices: 0.06 us -> 89.5 us  [over_z(): lax.psum_scatter(parts, 'tensor', scatter_dimension=0, tiled=False)]
    ppermute x83 -> x85, waiting for transfers between devices: 176 us -> 254 us  [move(): return lax.ppermute(value, AXES, pairs)]
    ppermute x83 -> x85, starting transfers between devices: 224 us -> 155 us  [move(): return lax.ppermute(value, AXES, pairs)]
    dynamic_slice x31 -> x0, local copies, waits for them, and re-layouts: 55 us -> none  [the longest x13 44.1 us: relative(): lax.dynamic_index_in_dim(parts, chip ^ k, axis, keepdims=False)]
    all_to_all x2, waiting for transfers between devices: 98.2 us -> 54.6 us  [return_rows(): lax.all_to_all(chosen, 'tensor', split_axis=0, concat_axis=0, tiled=True)]
    slice x45 -> x11, local copies, waits for them, and re-layouts: 40.4 us -> 5.66 us  [the longest x4 3.43 us: over_chips(): lower = move(along[k - 1][part:], lambda s, d, t: (1 - s, d, t))]
    dot_general x16 -> x14, matrix products: 41.1 us -> 75.4 us  [lhs_inner(): lax.dot_general(lhs_mat, rhs_mat, (((0,), (0,)), ((), ())), preferred_ele...]
  transfers between devices with their start and end apart: 92 -> 95, of which waited for: 20 -> 31; matrix products, arithmetic and copies ran while one was open for 31% -> 25% of each run, Pallas kernels for 8% -> 9%
where the time goes in v2:
time: 1140 us; the launch traced here: 1130 us
  waiting for transfers between devices  428 us (38%)
  starting transfers between devices  174 us (15%)
  matrix products  173 us (15%)
  other arithmetic  147 us (13%)
  Pallas kernels  128 us (11%)
  local copies, waits for them, and re-layouts  63.5 us (6%)
  between operations  17.1 us (2%)
    ppermute x85, waiting for transfers between devices, move(): return lax.ppermute(value, AXES, pairs)  254 us
    ppermute x85, starting transfers between devices, move(): return lax.ppermute(value, AXES, pairs)  155 us
    reduce_scatter x5, waiting for transfers between devices, over_z(): lax.psum_scatter(parts, 'tensor', scatter_dimension=0, tiled=False)  89.5 us
    dot_general x14, matrix products, lhs_inner(): lax.dot_general(lhs_mat, rhs_mat, (((0,), (0,)), ((), ())), preferred_ele...  75.4 us
    pallas_call x2, Pallas kernels, attend_backward(): pl.pallas_call(backward_kernel, grid=(pairs, rows // size), in_specs=atte...  74.6 us
    all_to_all x2, waiting for transfers between devices, return_rows(): lax.all_to_all(chosen, 'tensor', split_axis=0, concat_axis=0, tiled=True)  54.6 us
    dot_general x8, matrix products, rhs_inner(): lax.dot_general(lhs_mat, rhs_mat, (((1,), (1,)), ((), ())), preferred_ele...  54.4 us
    pallas_call x2, Pallas kernels, attend_forward(): pl.pallas_call(forward_kernel, grid=(pairs, rows // size), in_specs=atten...  52.9 us
  transfers between devices with their start and end apart: 95, of which 31 were waited for; matrix products, arithmetic and copies ran while one was open for 25% of the time, Pallas kernels for 9%

profile of v2, /device:TPU:0, one launch (start us, length us, event | category | flops | bytes accessed | tf_op | source)
XLA Modules:
  0.0 1130.1 jit_solution(15106418891266930113)
XLA Ops:
  119.6 10.4 collective-permute-done.7
  131.2 22.7 %collective-permute-done.25 = bf16[512,512]{1,0:T(8,128)(2,1)S(1)} collective-permute-done((bf16[512,512]{1,0:T(8,128)(2,1)}, bf16[512,512]{1,0:T(8,128)(2,1)S(1)}, u32[]{:S(2)}, u32[]{:S(2)}) %collective-permute-start.25) | collective-permute-done | bytes 524320 | tf_op jit(solution)/shard_map/ppermute | solution.py:25
  222.2 30.8 %collective-permute-done.42 = bf16[2,256,512]{2,1,0:T(8,128)(2,1)S(1)} collective-permute-done((bf16[2,256,512]{2,1,0:T(8,128)(2,1)}, bf16[2,256,512]{2,1,0:T(8,128)(2,1)S(1)}, u32[]{:S(2)}, u32[]{:S(2)}) %collective-permute-start.42) | collective-permute-done | bytes 524320 | tf_op jit(solution)/shard_map/ppermute | solution.py:25
  293.1 33.0 %collective-permute-done.12 = bf16[2,512,512]{2,1,0:T(8,128)(2,1)S(1)} collective-permute-done((bf16[2,512,512]{2,1,0:T(8,128)(2,1)S(1)}, bf16[2,512,512]{2,1,0:T(8,128)(2,1)S(1)}, u32[]{:S(2)}, u32[]{:S(2)}) %collective-permute-start.12) | collective-permute-done | bytes 1048608 | tf_op jit(solution)/shard_map/ppermute | solution.py:25
  334.7 26.4 %shard_map.169 = (bf16[1024,512]{1,0:T(8,128)(2,1)S(1)}, f32[4,2,1024]{2,1,0:T(2,128)S(1)}) custom-call(bf16[1024,1536]{1,0:T(8,128)(2,1)S(1)} %add_convert_fusion.1.query_ref.key_ref.value_ref, bf16[1024,1536]{1,0:T(8,128)(2,1)S(1)} %add_convert_fusion.1.query_ref.key_ref.value_ref, bf16[1024,1536]{1,0:T(8,128)(2,1)S(1)} %add_convert_fusion.1.query_ref.key_ref.value_ref, ...), custom_call_target="tpu_custom_call" | custom-call | flops 4294967296 | bytes 4194304 | tf_op jit(solution)/shard_map/pallas_call | solution.py:201
  378.1 12.7 %collective-permute-done.31 = bf16[2,512,512]{2,1,0:T(8,128)(2,1)S(1)} collective-permute-done((bf16[2,512,512]{2,1,0:T(8,128)(2,1)S(1)}, bf16[2,512,512]{2,1,0:T(8,128)(2,1)S(1)}, u32[]{:S(2)}, u32[]{:S(2)}) %collective-permute-start.31) | collective-permute-done | bytes 1048608 | tf_op jit(solution)/shard_map/ppermute | solution.py:25
  426.9 26.5 %shard_map.170 = (bf16[1024,512]{1,0:T(8,128)(2,1)S(1)}, f32[4,2,1024]{2,1,0:T(2,128)S(1)}) custom-call(bf16[1024,1536]{1,0:T(8,128)(2,1)S(1)} %add_convert_fusion.query_ref.key_ref.value_ref, bf16[1024,1536]{1,0:T(8,128)(2,1)S(1)} %add_convert_fusion.query_ref.key_ref.value_ref, bf16[1024,1536]{1,0:T(8,128)(2,1)S(1)} %add_convert_fusion.query_ref.key_ref.value_ref, ...), custom_call_target="tpu_custom_call" | custom-call | flops 4294967296 | bytes 4194304 | tf_op jit(solution)/shard_map/pallas_call | solution.py:201
  517.0 12.1 %fusion.16 = (f32[2048]{0:T(1024)S(1)}, bf16[1024,2048]{1,0:T(8,128)(2,1)}, f32[1024,2048]{1,0:T(8,128)}) fusion(f32[1024,2048]{1,0:T(8,128)} %get-tuple-element.213, f32[2048]{0:T(1024)S(1)} %bitcast.404, bf16[1024,1024]{0,1:T(8,128)(2,1)S(1)} %convert_element_type.411, bf16[2048,1024]{1,0:T(8,128)(2,1)S(1)} %bitcast.310), kind=kOutput, calls=%fused_computation.32 | convolution fusion | flops 4322228224 | bytes 27279360 | tf_op jit(solution)/shard_map/dot_general | solution.py:62
  529.1 10.5 convolution_convert_fusion.13
  555.3 37.4 %shard_map.171 = (bf16[1024,1536]{1,0:T(8,128)(2,1)S(1)}, f32[4,2,128]{2,1,0:T(2,128)S(1)}) custom-call(bf16[1024,1536]{1,0:T(8,128)(2,1)} %copy-done.8, bf16[1024,1536]{1,0:T(8,128)(2,1)} %copy-done.8, bf16[1024,1536]{1,0:T(8,128)(2,1)} %copy-done.8, s32[1024,1]{1,0:T(8,128)S(1)} %copy.134.seg_key_ref, s32[1,1024]{1,0:T(1,128)S(1)} %bitcast.293, ...), custom_call_target="tpu_custom_call" | custom-call | flops 10737418240 | bytes 8388608 | tf_op jit(solution)/shard_map/pallas_call | solution.py:223
  605.3 12.5 %convolution_convert_fusion.1 = bf16[2048,1024]{1,0:T(8,128)(2,1)} fusion(f32[1024,2048]{1,0:T(8,128)} %get-tuple-element.214, bf16[1024,2048]{1,0:T(8,128)(2,1)} %get-tuple-element.98, f32[1024,1024]{0,1:T(8,128)S(1)} %copy-done.18, f32[1024]{0:T(1024)S(1)} %bitcast.384, f32[1024]{0:T(1024)S(1)} %bitcast.366, f32[1024]{0:T(1024)S(1)} %add_rsqrt_fusion.1, ...), kind=kOutput, calls=%fused_computation.83 | convolution fusion | flops 4308598784 | bytes 20987904 | tf_op jit(solution)/shard_map/dot_general | solution.py:56
  626.7 12.1 %fusion.18 = (f32[2048]{0:T(1024)S(1)}, bf16[1024,2048]{1,0:T(8,128)(2,1)}, f32[1024,2048]{1,0:T(8,128)}) fusion(f32[1024,2048]{1,0:T(8,128)} %get-tuple-element.211, f32[2048]{0:T(1024)S(1)} %bitcast.402, bf16[1024,1024]{0,1:T(8,128)(2,1)S(1)} %fusion.72, bf16[2048,1024]{1,0:T(8,128)(2,1)S(1)} %bitcast.305), kind=kOutput, calls=%fused_computation.34 | convolution fusion | flops 4322228224 | bytes 27279360 | tf_op jit(solution)/shard_map/dot_general | solution.py:62
  638.9 10.5 convolution_convert_fusion.11
  669.2 13.2 %convolution_convert_fusion = bf16[2048,1024]{1,0:T(8,128)(2,1)} fusion(f32[1024,2048]{1,0:T(8,128)} %get-tuple-element.215, bf16[1024,2048]{1,0:T(8,128)(2,1)} %get-tuple-element.94, f32[1024,1024]{0,1:T(8,128)} %copy-done.12, f32[1024]{0:T(1024)S(1)} %bitcast.372, f32[1024]{0:T(1024)S(1)} %bitcast.353, f32[1024]{0:T(1024)S(1)} %copy-done.91, ...), kind=kOutput, calls=%fused_computation.82 | convolution fusion | flops 4308598784 | bytes 20987904 | tf_op jit(solution)/shard_map/dot_general | solution.py:56
  687.5 16.5 %collective-permute-done.82 = bf16[2048,512]{1,0:T(8,128)(2,1)} collective-permute-done((bf16[2048,512]{1,0:T(8,128)(2,1)}, bf16[2048,512]{1,0:T(8,128)(2,1)}, u32[]{:S(2)}, u32[]{:S(2)}) %collective-permute-start.82) | collective-permute-done | bytes 2097184 | tf_op jit(solution)/shard_map/ppermute | solution.py:25
  714.7 54.6 %all-to-all-done.1 = bf16[4,256,1024]{2,1,0:T(8,128)(2,1)} async-done(((bf16[4,256,1024]{2,1,0:T(8,128)(2,1)}), bf16[4,256,1024]{2,1,0:T(8,128)(2,1)}, u32[]{:S(2)}, u32[]{:S(2)}) %all-to-all-start.1) | async-done | bytes 2097184 | tf_op jit(solution)/shard_map/all_to_all | solution.py:337
  769.3 17.5 %collective-permute-start.57 = (bf16[4,256,1024]{2,1,0:T(8,128)(2,1)}, bf16[4,256,1024]{2,1,0:T(8,128)(2,1)}, u32[]{:S(2)}, u32[]{:S(2)}) collective-permute-start(bf16[4,256,1024]{2,1,0:T(8,128)(2,1)} %all-to-all-done.1), channel_id=1, source_target_pairs={{0,0},{1,1},{2,2},{3,3},{4,16},{5,17},{6,18},{7,19},{8,8},{9,9},{1... | collective-permute-start | bytes 6291464 | tf_op jit(solution)/shard_map/ppermute | solution.py:25
  818.9 37.2 %shard_map.172 = (bf16[1024,1536]{1,0:T(8,128)(2,1)S(1)}, f32[4,2,128]{2,1,0:T(2,128)S(1)}) custom-call(bf16[1024,1536]{1,0:T(8,128)(2,1)} %copy-done.7, bf16[1024,1536]{1,0:T(8,128)(2,1)} %copy-done.7, bf16[1024,1536]{1,0:T(8,128)(2,1)} %copy-done.7, s32[1024,1]{1,0:T(8,128)S(1)} %copy.134.seg_key_ref, s32[1,1024]{1,0:T(1,128)S(1)} %bitcast.294, ...), custom_call_target="tpu_custom_call" | custom-call | flops 10737418240 | bytes 8388608 | tf_op jit(solution)/shard_map/pallas_call | solution.py:223
  882.7 29.3 %collective-permute-done.74 = bf16[512,512]{1,0:T(8,128)(2,1)S(1)} collective-permute-done((bf16[512,512]{1,0:T(8,128)(2,1)S(1)}, bf16[512,512]{1,0:T(8,128)(2,1)S(1)}, u32[]{:S(2)}, u32[]{:S(2)}) %collective-permute-start.74) | collective-permute-done | bytes 524320 | tf_op jit(solution)/shard_map/ppermute | solution.py:25
  935.1 28.8 %collective-permute-done.71 = bf16[1536,512]{1,0:T(8,128)(2,1)} collective-permute-done((bf16[1536,512]{1,0:T(8,128)(2,1)}, bf16[1536,512]{1,0:T(8,128)(2,1)}, u32[]{:S(2)}, u32[]{:S(2)}) %collective-permute-start.71) | collective-permute-done | bytes 1572896 | tf_op jit(solution)/shard_map/ppermute | solution.py:25
  973.4 28.7 %all-reduce.2.cloned.1.call-done = f32[2,12,1024]{2,0,1:T(2,128)} async-done(((f32[2,12,1024]{2,0,1:T(2,128)}), f32[2,12,1024]{2,0,1:T(2,128)}) %all-reduce.2.cloned.1.call-update) | async-done | bytes 98320 | tf_op jit(solution)/shard_map/psum | solution.py:555
  1006.1 42.9 %reduce-scatter.14.cloned.1.call-done = bf16[1,512,512]{2,1,0:T(8,128)(2,1)} async-done(((bf16[4,512,512]{2,1,0:T(8,128)(2,1)}), bf16[1,512,512]{2,1,0:T(8,128)(2,1)}) %reduce-scatter.14.cloned.1.call-update) | async-done | bytes 524304 | tf_op jit(solution)/shard_map/reduce_scatter | solution.py:401
  1056.8 15.8 %reduce-scatter.10.cloned.1.call-done = bf16[1,128,512]{2,1,0:T(8,128)(2,1)} async-done(((bf16[4,128,512]{2,1,0:T(8,128)(2,1)}), bf16[1,128,512]{2,1,0:T(8,128)(2,1)}) %reduce-scatter.10.cloned.1.call-update) | async-done | bytes 131088 | tf_op jit(solution)/shard_map/reduce_scatter | solution.py:401
  1077.9 30.8 %reduce-scatter.8.cloned.1.call-done = bf16[1,384,512]{2,1,0:T(8,128)(2,1)} async-done(((bf16[4,384,512]{2,1,0:T(8,128)(2,1)}), bf16[1,384,512]{2,1,0:T(8,128)(2,1)}) %reduce-scatter.8.cloned.1.call-update) | async-done | bytes 393232 | tf_op jit(solution)/shard_map/reduce_scatter | solution.py:401
  (618 shorter events, 540.0 us)
Async XLA Ops:
  96.0 120.9 %all-to-all-start = ((bf16[4,128,1024]{1,2,0:T(8,128)(2,1)}), bf16[4,128,1024]{1,2,0:T(8,128)(2,1)}, u32[]{:S(2)}, u32[]{:S(2)}) async-start(bf16[4,128,1024]{1,2,0:T(8,128)(2,1)} %copy.131), calls=%async_computation | async-start | bytes 2097152 | tf_op jit(solution)/shard_map/all_to_all | solution.py:330
  100.5 74.3 %collective-permute-start.49 = (bf16[2,256,1024]{2,1,0:T(8,128)(2,1)}, bf16[2,256,1024]{2,1,0:T(8,128)(2,1)}, u32[]{:S(2)}, u32[]{:S(2)}) collective-permute-start(bf16[2,256,1024]{2,1,0:T(8,128)(2,1)} %pad_maximum_fusion.10), channel_id=1, source_target_pairs={{1,0},{2,1},{3,2},{5,4},{6,5},{7,6},{9,8},{10,9},{11,10},{13,12},{... | collective-permute-start | bytes 3145736 | tf_op jit(solution)/shard_map/ppermute | solution.py:25
  130.1 63.4 %collective-permute-start.40 = (bf16[4,256,512]{2,1,0:T(8,128)(2,1)}, bf16[4,256,512]{2,1,0:T(8,128)(2,1)S(1)}, u32[]{:S(2)}, u32[]{:S(2)}) collective-permute-start(bf16[4,256,512]{2,1,0:T(8,128)(2,1)} %bitcast_dynamic-update-slice_fusion.10), channel_id=1, source_target_pairs={{0,16},{1,17},{2,18},{3,19},{4,20},{5,21},{6,22},{7,23},{8,24},{9,... | collective-permute-start | bytes 3145736 | tf_op jit(solution)/shard_map/ppermute | solution.py:25
  187.4 78.1 %collective-permute-start.9 = (bf16[4,512,512]{2,1,0:T(8,128)(2,1)S(1)}, bf16[4,512,512]{2,1,0:T(8,128)(2,1)}, u32[]{:S(2)}, u32[]{:S(2)}) collective-permute-start(bf16[4,512,512]{2,1,0:T(8,128)(2,1)S(1)} %bitcast_dynamic-update-slice_fusion.7), channel_id=1, source_target_pairs={{0,16},{1,17},{2,18},{3,19},{4,20},{5,21},{6,22},{7,23},{8,24},{9,... | collective-permute-start | bytes 6291464 | tf_op jit(solution)/shard_map/ppermute | solution.py:25
  198.3 76.8 %collective-permute-start.10 = (bf16[4,512,512]{2,1,0:T(8,128)(2,1)S(1)}, bf16[4,512,512]{2,1,0:T(8,128)(2,1)}, u32[]{:S(2)}, u32[]{:S(2)}) collective-permute-start(bf16[4,512,512]{2,1,0:T(8,128)(2,1)S(1)} %bitcast_dynamic-update-slice_fusion.7), channel_id=1, source_target_pairs={{0,8},{1,9},{2,10},{3,11},{4,12},{5,13},{6,14},{7,15},{8,0},{9,1},... | collective-permute-start | bytes 6291464 | tf_op jit(solution)/shard_map/ppermute | solution.py:25
  261.5 103.6 %collective-permute-start.29 = (bf16[4,512,512]{2,1,0:T(8,128)(2,1)}, bf16[4,512,512]{2,1,0:T(8,128)(2,1)S(1)}, u32[]{:S(2)}, u32[]{:S(2)}) collective-permute-start(bf16[4,512,512]{2,1,0:T(8,128)(2,1)} %bitcast_dynamic-update-slice_fusion.4), channel_id=1, source_target_pairs={{0,16},{1,17},{2,18},{3,19},{4,20},{5,21},{6,22},{7,23},{8,24},{9,... | collective-permute-start | bytes 6291464 | tf_op jit(solution)/shard_map/ppermute | solution.py:25
  275.1 90.6 %collective-permute-start.30 = (bf16[4,512,512]{2,1,0:T(8,128)(2,1)}, bf16[4,512,512]{2,1,0:T(8,128)(2,1)}, u32[]{:S(2)}, u32[]{:S(2)}) collective-permute-start(bf16[4,512,512]{2,1,0:T(8,128)(2,1)} %bitcast_dynamic-update-slice_fusion.4), channel_id=1, source_target_pairs={{0,8},{1,9},{2,10},{3,11},{4,12},{5,13},{6,14},{7,15},{8,0},{9,1},... | collective-permute-start | bytes 6291464 | tf_op jit(solution)/shard_map/ppermute | solution.py:25
  275.1 87.4 %collective-permute-start.53 = (bf16[2,256,1024]{2,1,0:T(8,128)(2,1)}, bf16[2,256,1024]{2,1,0:T(8,128)(2,1)}, u32[]{:S(2)}, u32[]{:S(2)}) collective-permute-start(bf16[2,256,1024]{2,1,0:T(8,128)(2,1)} %collective-permute-done.52), channel_id=1, source_target_pairs={{0,1},{1,2},{2,3},{4,5},{5,6},{6,7},{8,9},{9,10},{10,11},{12,13},{... | collective-permute-start | bytes 3145736 | tf_op jit(solution)/shard_map/ppermute | solution.py:25
  469.1 332.0 %reduce-scatter.6.cloned.1.call-start = ((), (), s32[]{:S(2)}) async-start(), calls=%async_computation.9 | async-start | bytes 5242880 | tf_op jit(solution)/shard_map/reduce_scatter | solution.py:401
  664.0 105.3 %all-to-all-start.1 = ((bf16[4,256,1024]{2,1,0:T(8,128)(2,1)}), bf16[4,256,1024]{2,1,0:T(8,128)(2,1)}, u32[]{:S(2)}, u32[]{:S(2)}) async-start(bf16[4,256,1024]{2,1,0:T(8,128)(2,1)} %bitcast.94), calls=%async_computation.1 | async-start | bytes 4194304 | tf_op jit(solution)/shard_map/all_to_all | solution.py:337
  668.7 300.0 %reduce-scatter.12.cloned.1.call-start = ((), (), s32[]{:S(2)}) async-start(), calls=%async_computation.12 | async-start | bytes 5242880 | tf_op jit(solution)/shard_map/reduce_scatter | solution.py:401
  682.4 319.7 %all-reduce.2.cloned.1.call-start = ((), (), s32[]{:S(2)}) async-start(), calls=%async_computation.14 | async-start | bytes 196608 | tf_op jit(solution)/shard_map/psum | solution.py:555
  682.6 112.5 %collective-permute-start.64 = (bf16[2048,512]{1,0:T(8,128)(2,1)}, bf16[2048,512]{1,0:T(8,128)(2,1)}, u32[]{:S(2)}, u32[]{:S(2)}) collective-permute-start(bf16[2048,512]{1,0:T(8,128)(2,1)} %add_convert_fusion.5), channel_id=1, source_target_pairs={{0,16},{1,17},{2,18},{3,19},{4,20},{5,21},{6,22},{7,23},{8,24},{9,... | collective-permute-start | bytes 6291464 | tf_op jit(solution)/shard_map/ppermute | solution.py:25
  710.9 84.2 %collective-permute-start.83 = (bf16[2048,512]{1,0:T(8,128)(2,1)}, bf16[2048,512]{1,0:T(8,128)(2,1)}, u32[]{:S(2)}, u32[]{:S(2)}) collective-permute-start(bf16[2048,512]{1,0:T(8,128)(2,1)} %add_convert_fusion.3), channel_id=1, source_target_pairs={{16,0},{17,1},{18,2},{19,3},{20,4},{21,5},{22,6},{23,7},{24,8},{25... | collective-permute-start | bytes 6291464 | tf_op jit(solution)/shard_map/ppermute | solution.py:25
  714.4 79.1 %collective-permute-start.66 = (bf16[512,512]{1,0:T(8,128)(2,1)S(1)}, bf16[512,512]{1,0:T(8,128)(2,1)S(1)}, u32[]{:S(2)}, u32[]{:S(2)}) collective-permute-start(bf16[512,512]{1,0:T(8,128)(2,1)S(1)} %convolution_convert_fusion.22), channel_id=1, source_target_pairs={{0,8},{1,9},{2,10},{3,11},{4,12},{5,13},{6,14},{7,15},{8,0},{9,1},... | collective-permute-start | bytes 1572872 | tf_op jit(solution)/shard_map/ppermute | solution.py:25
  792.0 67.1 %collective-permute-start.65 = (bf16[1536,512]{1,0:T(8,128)(2,1)}, bf16[1536,512]{1,0:T(8,128)(2,1)}, u32[]{:S(2)}, u32[]{:S(2)}) collective-permute-start(bf16[1536,512]{1,0:T(8,128)(2,1)} %convolution_convert_fusion.8), channel_id=1, source_target_pairs={{0,8},{1,9},{2,10},{3,11},{4,12},{5,13},{6,14},{7,15},{8,0},{9,1},... | collective-permute-start | bytes 4718600 | tf_op jit(solution)/shard_map/ppermute | solution.py:25
  803.2 61.9 %collective-permute-start.67 = (bf16[512,512]{1,0:T(8,128)(2,1)}, bf16[512,512]{1,0:T(8,128)(2,1)}, u32[]{:S(2)}, u32[]{:S(2)}) collective-permute-start(bf16[512,512]{1,0:T(8,128)(2,1)} %split.123), channel_id=1, source_target_pairs={{0,8},{1,9},{2,10},{3,11},{4,12},{5,13},{6,14},{7,15},{8,0},{9,1},... | collective-permute-start | bytes 1572872 | tf_op jit(solution)/shard_map/ppermute | solution.py:25
  858.9 190.1 %reduce-scatter.14.cloned.1.call-start = ((), (), s32[]{:S(2)}) async-start(), calls=%async_computation.13 | async-start | bytes 2621440 | tf_op jit(solution)/shard_map/reduce_scatter | solution.py:401
  927.9 125.6 %all-to-all-start.3 = ((bf16[4,256,1024]{2,1,0:T(8,128)(2,1)}), bf16[4,256,1024]{2,1,0:T(8,128)(2,1)}, u32[]{:S(2)}, u32[]{:S(2)}) async-start(bf16[4,256,1024]{2,1,0:T(8,128)(2,1)} %bitcast.102), calls=%async_computation.4 | async-start | bytes 4194304 | tf_op jit(solution)/shard_map/all_to_all | solution.py:337
  932.3 140.3 %reduce-scatter.10.cloned.1.call-start = ((), (), s32[]{:S(2)}) async-start(), calls=%async_computation.11 | async-start | bytes 655360 | tf_op jit(solution)/shard_map/reduce_scatter | solution.py:401
  935.0 173.6 %reduce-scatter.8.cloned.1.call-start = ((), (), s32[]{:S(2)}) async-start(), calls=%async_computation.10 | async-start | bytes 1966080 | tf_op jit(solution)/shard_map/reduce_scatter | solution.py:401
  969.8 80.3 %collective-permute-start.78 = (bf16[512,512]{1,0:T(8,128)(2,1)S(1)}, bf16[512,512]{1,0:T(8,128)(2,1)S(1)}, u32[]{:S(2)}, u32[]{:S(2)}) collective-permute-start(bf16[512,512]{1,0:T(8,128)(2,1)S(1)} %split.131), channel_id=1, source_target_pairs={{0,8},{1,9},{2,10},{3,11},{4,12},{5,13},{6,14},{7,15},{8,0},{9,1},... | collective-permute-start | bytes 1572872 | tf_op jit(solution)/shard_map/ppermute | solution.py:25
  971.2 102.4 %collective-permute-start.80 = (bf16[512,512]{1,0:T(8,128)(2,1)S(1)}, bf16[512,512]{1,0:T(8,128)(2,1)}, u32[]{:S(2)}, u32[]{:S(2)}) collective-permute-start(bf16[512,512]{1,0:T(8,128)(2,1)S(1)} %copy-done.62), channel_id=1, source_target_pairs={{0,16},{1,17},{2,18},{3,19},{4,20},{5,21},{6,22},{7,23},{8,24},{9,... | collective-permute-start | bytes 1572872 | tf_op jit(solution)/shard_map/ppermute | solution.py:25
  1053.5 66.8 %collective-permute-start.69 = (bf16[4,256,1024]{2,1,0:T(8,128)(2,1)}, bf16[4,256,1024]{2,1,0:T(8,128)(2,1)S(1)}, u32[]{:S(2)}, u32[]{:S(2)}) collective-permute-start(bf16[4,256,1024]{2,1,0:T(8,128)(2,1)} %all-to-all-done.3), channel_id=1, source_target_pairs={{0,0},{1,1},{2,2},{3,3},{4,16},{5,17},{6,18},{7,19},{8,8},{9,9},{1... | collective-permute-start | bytes 6291464 | tf_op jit(solution)/shard_map/ppermute | solution.py:25
  (173 other events, 4814.7 us)
Sparse Core Ops, SparseCore 0:
  618.0 98.0 reduce-scatter.5
  718.5 88.0 reduce-scatter.11
  859.0 143.0 all-reduce.1
  1004.3 44.6 reduce-scatter.13
  1051.8 20.7 reduce-scatter.9
  1074.9 33.7 reduce-scatter.7

commit v3 on v2

--- a/solution.py
+++ b/solution.py
@@ -1,3 +1,5 @@
+import functools
+
 import jax
 import jax.numpy as jnp
 from jax import lax
@@ -119,26 +121,57 @@
     return lax.dot_general(keys, queries, (((1,), (1,)), ((), ())), preferred_element_type=WIDE)
 
 
-def forward_kernel(query_ref, key_ref, value_ref, seg_key_ref, seg_query_ref, out_ref, logsum_ref):
-    allowed = seg_key_ref[...] == seg_query_ref[...]
-    queries = query_ref[...] * jnp.asarray(HEAD_DIM ** (-0.5), LOW)
-    heads = queries.shape[1] // HEAD_DIM
-    parts = []
-    for head in range(heads):
-        scores = keys_by_queries(key_ref[...], head_lanes(queries, head))
-        scores = jnp.where(allowed, scores, -1000000000.0)
-        highest = jnp.max(scores, axis=0, keepdims=True)
-        raised = jnp.exp(scores - highest)
-        totals = jnp.sum(raised, axis=0, keepdims=True)
-        context = lhs_inner(value_ref[...], raised.astype(LOW))
-        rows = slice(head * HEAD_DIM, (head + 1) * HEAD_DIM)
-        parts.append(context[rows] / totals)
-        logsum_ref[0, head : head + 1, :] = highest + jnp.log(totals)
-    out_ref[...] = jnp.concatenate(parts, axis=0).T.astype(LOW)
+def key_windows(seq_lens, rows, size):
+    widths = tuple(sorted({min(rows, width) for width in (512, 640, 768, rows)}))
+    ends = jnp.cumsum(seq_lens)
+    first = jnp.arange(rows // size, dtype=jnp.int32)[:, None] * size
+    lowest = jnp.max(jnp.where(ends[None, :] <= first, ends[None, :], 0), axis=1)
+    highest = jnp.min(jnp.where(ends[None, :] >= first + size, ends[None, :], rows), axis=1)
+    start, kind = jnp.zeros_like(lowest), jnp.full_like(lowest, len(widths) - 1)
+    for at in range(len(widths) - 2, -1, -1):
+        begin = jnp.minimum(lowest // 128 * 128, rows - widths[at])
+        fits = highest - begin <= widths[at]
+        start = jnp.where(fits, begin, start)
+        kind = jnp.where(fits, at, kind)
+    return start.astype(jnp.int32), kind.astype(jnp.int32), widths
+
+
+def each_width(kind, widths, body):
+    for at, width in enumerate(widths):
+        @pl.when(kind == at)
+        def _(width=width):
+            body(width)
+
+
+def forward_kernel(
+    widths, start_ref, kind_ref, query_ref, key_ref, value_ref, seg_key_ref, seg_query_ref, out_ref, logsum_ref
+):
+    block = pl.program_id(1)
+    heads = query_ref.shape[1] // HEAD_DIM
+
+    def body(width):
+        window = pl.ds(pl.multiple_of(start_ref[block], 128), width)
+        allowed = seg_key_ref[window, :] == seg_query_ref[...]
+        queries = query_ref[...] * jnp.asarray(HEAD_DIM ** (-0.5), LOW)
+        keys, values = key_ref[window, :], value_ref[window, :]
+        parts = []
+        for head in range(heads):
+            scores = keys_by_queries(keys, head_lanes(queries, head))
+            scores = jnp.where(allowed, scores, -1000000000.0)
+            highest = jnp.max(scores, axis=0, keepdims=True)
+            raised = jnp.exp(scores - highest)
+            totals = jnp.sum(raised, axis=0, keepdims=True)
+            context = lhs_inner(values, raised.astype(LOW))
+            rows = slice(head * HEAD_DIM, (head + 1) * HEAD_DIM)
+            parts.append(context[rows] / totals)
+            logsum_ref[0, head : head + 1, :] = highest + jnp.log(totals)
+        out_ref[...] = jnp.concatenate(parts, axis=0).T.astype(LOW)
+
+    each_width(kind_ref[block], widths, body)
 
 
 def backward_kernel(
-    query_ref, key_ref, value_ref, seg_key_ref, seg_query_ref, logsum_ref, grad_ref,
+    widths, start_ref, kind_ref, query_ref, key_ref, value_ref, seg_key_ref, seg_query_ref, logsum_ref, grad_ref,
     out_ref, sum_ref, key_grad, value_grad,
 ):
     block = pl.program_id(1)
@@ -152,28 +185,37 @@
         value_grad[...] = jnp.zeros_like(value_grad)
         sum_ref[...] = jnp.zeros_like(sum_ref)
 
-    allowed = seg_key_ref[...] == seg_query_ref[...]
-    queries = query_ref[...] * jnp.asarray(factor, LOW)
-    grads = grad_ref[...]
-    weight_low, score_low, query_heads, grad_heads, query_parts = [], [], [], [], []
-    for head in range(heads):
-        query_head, grad_head = head_lanes(queries, head), head_lanes(grads, head)
-        scores = jnp.where(allowed, keys_by_queries(key_ref[...], query_head), -1000000000.0)
-        weights = jnp.exp(scores - logsum_ref[0, head : head + 1, :])
-        weight_grad = keys_by_queries(value_ref[...], grad_head)
-        centre = jnp.sum(weight_grad * weights, axis=0, keepdims=True)
-        score_grad = (weights * (weight_grad - centre)).astype(LOW)
-        rows = slice(head * HEAD_DIM, (head + 1) * HEAD_DIM)
-        query_parts.append(lhs_inner(key_ref[...], score_grad)[rows] * factor)
-        weight_low.append(weights.astype(LOW))
-        score_low.append(score_grad)
-        query_heads.append(query_head)
-        grad_heads.append(grad_head)
-    key_grad[...] += matmul(jnp.concatenate(score_low, axis=1), jnp.concatenate(query_heads, axis=0))
-    value_grad[...] += matmul(jnp.concatenate(weight_low, axis=1), jnp.concatenate(grad_heads, axis=0))
-    query_grad = jnp.concatenate(query_parts, axis=0).T
-    out_ref[pl.ds(pl.multiple_of(block * size, size), size), :lanes] = query_grad.astype(LOW)
-    sum_ref[0, 0:1, :] += jnp.sum(query_grad, axis=0, keepdims=True)
+    def body(width):
+        window = pl.ds(pl.multiple_of(start_ref[block], 128), width)
+        allowed = seg_key_ref[window, :] == seg_query_ref[...]
+        queries = query_ref[...] * jnp.asarray(factor, LOW)
+        grads = grad_ref[...]
+        keys, values = key_ref[window, :], value_ref[window, :]
+        weight_low, score_low, query_heads, grad_heads, query_parts = [], [], [], [], []
+        for head in range(heads):
+            query_head, grad_head = head_lanes(queries, head), head_lanes(grads, head)
+            scores = jnp.where(allowed, keys_by_queries(keys, query_head), -1000000000.0)
+            weights = jnp.exp(scores - logsum_ref[0, head : head + 1, :])
+            weight_grad = keys_by_queries(values, grad_head)
+            centre = jnp.sum(weight_grad * weights, axis=0, keepdims=True)
+            score_grad = (weights * (weight_grad - centre)).astype(LOW)
+            rows = slice(head * HEAD_DIM, (head + 1) * HEAD_DIM)
+            query_parts.append(lhs_inner(keys, score_grad)[rows] * factor)
+            weight_low.append(weights.astype(LOW))
+            score_low.append(score_grad)
+            query_heads.append(query_head)
+            grad_heads.append(grad_head)
+        key_grad[window, :] += matmul(
+            jnp.concatenate(score_low, axis=1), jnp.concatenate(query_heads, axis=0)
+        )
+        value_grad[window, :] += matmul(
+            jnp.concatenate(weight_low, axis=1), jnp.concatenate(grad_heads, axis=0)
+        )
+        query_grad = jnp.concatenate(query_parts, axis=0).T
+        out_ref[pl.ds(pl.multiple_of(block * size, size), size), :lanes] = query_grad.astype(LOW)
+        sum_ref[0, 0:1, :] += jnp.sum(query_grad, axis=0, keepdims=True)
+
+    each_width(kind_ref[block], widths, body)
 
     @pl.when(block == pl.num_programs(1) - 1)
     def _():
@@ -184,61 +226,69 @@
 
 def attention_specs(rows, lanes, size):
     return [
-        pl.BlockSpec((size, lanes), lambda pair, block: (block, 3 * pair)),
-        pl.BlockSpec((rows, lanes), lambda pair, block: (0, 3 * pair + 1)),
-        pl.BlockSpec((rows, lanes), lambda pair, block: (0, 3 * pair + 2)),
-        pl.BlockSpec((rows, 1), lambda pair, block: (0, 0)),
-        pl.BlockSpec((1, size), lambda pair, block: (0, block)),
+        pl.BlockSpec((size, lanes), lambda pair, block, *_: (block, 3 * pair)),
+        pl.BlockSpec((rows, lanes), lambda pair, block, *_: (0, 3 * pair + 1)),
+        pl.BlockSpec((rows, lanes), lambda pair, block, *_: (0, 3 * pair + 2)),
+        pl.BlockSpec((rows, 1), lambda pair, block, *_: (0, 0)),
+        pl.BlockSpec((1, size), lambda pair, block, *_: (0, block)),
     ]
 
 
-def attend_forward(packed, segments, lanes):
+def attend_forward(packed, segments, seq_lens, lanes):
     rows = packed.shape[0]
     pairs = packed.shape[1] // (3 * lanes)
     heads = lanes // HEAD_DIM
     size = min(256, rows)
     squares = pairs * heads * rows * rows
+    start, kind, widths = key_windows(seq_lens, rows, size)
     return pl.pallas_call(
-        forward_kernel,
-        grid=(pairs, rows // size),
-        in_specs=attention_specs(rows, lanes, size),
-        out_specs=[
-            pl.BlockSpec((size, lanes), lambda pair, block: (block, pair)),
-            pl.BlockSpec((1, heads, size), lambda pair, block: (pair, 0, block)),
-        ],
+        functools.partial(forward_kernel, widths),
+        grid_spec=pltpu.PrefetchScalarGridSpec(
+            num_scalar_prefetch=2,
+            grid=(pairs, rows // size),
+            in_specs=attention_specs(rows, lanes, size),
+            out_specs=[
+                pl.BlockSpec((size, lanes), lambda pair, block, *_: (block, pair)),
+                pl.BlockSpec((1, heads, size), lambda pair, block, *_: (pair, 0, block)),
+            ],
+        ),
         out_shape=[
             jax.ShapeDtypeStruct((rows, pairs * lanes), LOW),
             jax.ShapeDtypeStruct((pairs, heads, rows), WIDE),
         ],
         **flash_params(8 * squares * HEAD_DIM, squares, 4 * rows * pairs * lanes * 2),
-    )(packed, packed, packed, segments[:, None], segments[None, :])
-
-
-def attend_backward(packed, segments, logsums, context_grad, lanes):
+    )(start, kind, packed, packed, packed, segments[:, None], segments[None, :])
+
+
+def attend_backward(packed, segments, seq_lens, logsums, context_grad, lanes):
     rows = packed.shape[0]
     pairs = packed.shape[1] // (3 * lanes)
     heads = lanes // HEAD_DIM
     size = min(256, rows)
     squares = pairs * heads * rows * rows
+    start, kind, widths = key_windows(seq_lens, rows, size)
     return pl.pallas_call(
-        backward_kernel,
-        grid=(pairs, rows // size),
-        in_specs=attention_specs(rows, lanes, size)
-        + [
-            pl.BlockSpec((1, heads, size), lambda pair, block: (pair, 0, block)),
-            pl.BlockSpec((size, lanes), lambda pair, block: (block, pair)),
-        ],
-        out_specs=[
-            pl.BlockSpec((rows, 3 * lanes), lambda pair, block: (0, pair)),
-            pl.BlockSpec((1, 2, lanes), lambda pair, block: (pair, 0, 0)),
-        ],
+        functools.partial(backward_kernel, widths),
+        grid_spec=pltpu.PrefetchScalarGridSpec(
+            num_scalar_prefetch=2,
+            grid=(pairs, rows // size),
+            in_specs=attention_specs(rows, lanes, size)
+            + [
+                pl.BlockSpec((1, heads, size), lambda pair, block, *_: (pair, 0, block)),
+                pl.BlockSpec((size, lanes), lambda pair, block, *_: (block, pair)),
+            ],
+            out_specs=[
+                pl.BlockSpec((rows, 3 * lanes), lambda pair, block, *_: (0, pair)),
+                pl.BlockSpec((1, 2, lanes), lambda pair, block, *_: (pair, 0, 0)),
+            ],
+            scratch_shapes=[pltpu.VMEM((rows, lanes), WIDE), pltpu.VMEM((rows, lanes), WIDE)],
+        ),
         out_shape=[
             jax.ShapeDtypeStruct((rows, pairs * 3 * lanes), LOW),
             jax.ShapeDtypeStruct((pairs, 2, lanes), WIDE),
         ],
-        scratch_shapes=[pltpu.VMEM((rows, lanes), WIDE), pltpu.VMEM((rows, lanes), WIDE)],
         **flash_params(20 * squares * HEAD_DIM, squares, 8 * rows * pairs * lanes * 2),
-    )(packed, packed, packed, segments[:, None], segments[None, :], logsums, context_grad)
+    )(start, kind, packed, packed, packed, segments[:, None], segments[None, :], logsums, context_grad)
 
 
 def pair_columns(packed, head_half, lanes, back=False):
@@ -250,13 +300,13 @@
     return jnp.swapaxes(shaped, 2, 3).reshape(packed.shape)
 
 
-def layer_forward(rows, segments, weights, small):
+def layer_forward(rows, segments, seq_lens, weights, small):
     w_qkv, w_out, w_in, w_back = weights
     gains, biases, offset, inner_bias, head_half = small
     lanes = max(head_half, 128)
     packed = (rhs_inner(rows, w_qkv) + offset).astype(LOW)
     packed = pair_columns(packed, head_half, lanes)
-    context, logsums = attend_forward(packed, segments, lanes)
+    context, logsums = attend_forward(packed, segments, seq_lens, lanes)
     first_sum = rows.astype(WIDE) + core_sum(matmul(context, w_out)) + biases[2]
     middle = (norm_parts(first_sum)[0] * gains[0] + biases[3]).astype(LOW)
     active, slope = gelu_pair(rhs_inner(middle, w_in) + inner_bias)
@@ -284,7 +334,7 @@
     return middle_grad, branch_grad, hidden_low, sums
 
 
-def backward_attention(saved, segments, middle_grad, weights, small):
+def backward_attention(saved, segments, seq_lens, middle_grad, weights, small):
     _, w_out, _, _ = weights
     gains, head_half = small[0], small[4]
     _, packed, logsums, _, first_sum = saved[:5]
@@ -292,7 +342,7 @@
     attended_grad = first_grad.astype(LOW)
     context_grad = rhs_inner(attended_grad, w_out).astype(LOW)
     lanes = max(head_half, 128)
-    packed_low, column_sums = attend_backward(packed, segments, logsums, context_grad, lanes)
+    packed_low, column_sums = attend_backward(packed, segments, seq_lens, logsums, context_grad, lanes)
     packed_low = pair_columns(packed_low, head_half, lanes, back=True)
     sums = (gain_one, jnp.sum(first_grad, axis=0), bias_one) + tuple(
         column_sums[:, at].reshape(-1) for at in range(2)
@@ -320,24 +370,33 @@
         slabs = jnp.split(value, chips, axis=-1)
         return jnp.concatenate([choose(chip ^ k, slabs) for k in range(chips)], axis=-1)
 
-    def fetch_rows(block):
+    def fetch_rows(block, *before):
         parts = block.reshape(micro_count, 2, own_rows // 2, width)
         kept = choose(core, (parts[:, 0], parts[:, 1]))
         given = choose(core, (parts[:, 1], parts[:, 0]))
         received = move(given, lambda s, d, t: (s, d ^ 1, t) if d % 2 == s else None)
         mine = jnp.where(core == section, kept, received)
         mine = jnp.repeat(mine, repeats, axis=0) if repeats > 1 else mine
+        mine = after(mine, *before) if before else mine
         mine = lax.all_to_all(mine, "tensor", split_axis=0, concat_axis=0, tiled=True)
         whole = by_core(core, mine, to_other_core(mine), 1)
-        return relative(whole.reshape(ranks * own_rows, width))
-
-    def return_rows(first, second):
-        chosen = relative(jnp.where(core == 0, first, second).astype(LOW))
-        chosen = chosen.reshape(ranks, own_rows, width)
-        spread = lax.all_to_all(chosen, "tensor", split_axis=0, concat_axis=0, tiled=True)
-        spread = spread.reshape(micro_count, repeats, own_rows, width)[:, 0]
-        placed = move(spread, lambda s, d, t: (d % 2, (d // 2) * 2 + s, t))
-        return placed.astype(WIDE)[None]
+        return relative(whole.reshape(ranks * own_rows, width)), mine
+
+    def spread_rows(value):
+        parts = relative(value.astype(LOW)).reshape(ranks, 2, own_rows // 2, width)
+        mine = choose(core, (parts[:, 0], parts[:, 1]))
+        spread = lax.all_to_all(mine, "tensor", split_axis=0, concat_axis=0, tiled=True)
+        return spread.reshape((micro_count, repeats) + spread.shape[1:])[:, 0]
+
+    def place_rows(spread, layer):
+        halves = [
+            move(spread, lambda s, d, t: (layer, (d // 2) * 2 + s, t) if d % 2 == half else None)
+            for half in range(2)
+        ]
+        return jnp.concatenate(halves, axis=1)
+
+    def by_section(first, second):
+        return jnp.where(section == 0, first, second)
 
     def own_half(halves):
         kept = choose(core, (halves[0], halves[1]))
@@ -409,7 +468,6 @@
         given = choose(core, parts[::-1])
         return by_core(core, kept[None], to_other_core(given)[None], 0).astype(WIDE)
 
-    rows = fetch_rows(block_input)
     head_half = w_qkv.shape[-1] // 2
     hidden_half = w_in.shape[-1] // 2
     in_first = jnp.moveaxis(w_in[0].reshape(local, 2, hidden_half), 0, 2)
@@ -418,12 +476,19 @@
     out_first = w_out[0].reshape(2, head_half, local)
     back_first = w_back[0].reshape(2, hidden_half, local)
     later = hidden_half // 2
-    attention_all = gather_weight(own_half(jnp.concatenate([qkv_first, out_first], axis=1)))
+    attention_own = own_half(jnp.concatenate([qkv_first, out_first], axis=1))
     back_own = own_half(back_first)
-    in_all = gather_weight(own_half(in_first))
-    back_one = gather_weight(back_own[:later])
-    back_two = gather_weight_late(back_own[later:])
-    back_all = [jnp.concatenate(pair, axis=1) for pair in zip(back_one, back_two)]
+    in_own = own_half(in_first)
+    back_two = jnp.stack(over_chips(back_own[later:]))
+    attention_item = over_ranks(attention_own)
+    attention_all = over_chips(attention_item)
+    rows, rows_here = fetch_rows(block_input, attention_item)
+    in_item = over_ranks(after(in_own, rows_here))
+    in_all = over_chips(in_item)
+    back_item = over_ranks(after(back_own[:later], in_item))
+    back_one = over_chips(back_item)
+    back_two = over_ranks(after(back_two, back_item))
+    back_all = [jnp.concatenate([back_one[at], back_two[:, at]], axis=1) for at in range(2)]
     weights = [
         (
             attention_all[layer][:, : 3 * head_half].reshape(-1, width),
@@ -471,65 +536,71 @@
     lengths = jnp.where(core == section, seq_lengths, to_other_core(seq_lengths))[:, 0]
     lengths = lax.dynamic_index_in_dim(lengths, rank // repeats, 0, keepdims=False)
     segments = segment_ids(lengths, ranks * own_rows)
-    cotangent = fetch_rows(out_grad)
-    cotangent = jnp.where((segments < lengths.shape[0])[:, None], cotangent, jnp.zeros((), LOW))
-
-    first_out, first_saved = layer_forward(rows, segments, weights[0], small[0])
-    second_out, second_saved = layer_forward(first_out.astype(LOW), segments, weights[1], small[1])
-    outputs = return_rows(first_out, second_out)
-
-    def feed_forward_grads(saved, branch_grad, hidden_low):
-        back = counted_only(slab_grads(saved[6], branch_grad, chips))
-        inner = counted_only([lhs_inner(hidden_low, saved[5]).astype(LOW)])[0]
-        return back, inner
+    live = (segments < lengths.shape[0])[:, None]
+
+    first_out, first_saved = layer_forward(rows, segments, lengths, weights[0], small[0])
+    first_low = first_out.astype(LOW)
+    cotangent, cotangent_here = fetch_rows(out_grad, first_low, back_two)
+    cotangent = jnp.where(live, cotangent, jnp.zeros((), LOW))
+    second_out, second_saved = layer_forward(first_low, segments, lengths, weights[1], small[1])
+    first_spread = spread_rows(after(first_low, cotangent_here))
+    second_spread = spread_rows(second_out)
+
+    def matrix_grad(hidden, features):
+        return counted_only([lhs_inner(hidden, features).astype(LOW)])[0]
 
     def attention_grads(saved, attended_grad, packed_low):
-        out = slab_grads(saved[3], attended_grad, chips)
-        qkv = slab_grads(packed_low, saved[0], chips)
-        return counted_only(out), counted_only(qkv)
+        qkv = over_z(matrix_grad(packed_low, saved[0]))
+        return qkv, over_z(matrix_grad(saved[3], attended_grad))
 
     middle_grad, branch_grad, hidden_low, second_sums = backward_hidden(
         second_saved, cotangent, weights[1], small[1]
     )
-    back_slabs, inner = feed_forward_grads(second_saved, branch_grad, hidden_low)
-    back_two = slabs_along_x(back_slabs)
-    in_two = over_z(inner)
+    middle_grad = after(middle_grad, first_spread)
+    first_placed = place_rows(first_spread, 0)
+    back_two = slabs_along_x(counted_only(slab_grads(second_saved[6], branch_grad, chips)))
+    in_two = over_z(matrix_grad(hidden_low, second_saved[5]))
     first_grad, attended_grad, packed_low, more_sums = backward_attention(
-        second_saved, segments, middle_grad, weights[1], small[1]
+        second_saved, segments, lengths, middle_grad, weights[1], small[1]
     )
     second_sums += more_sums
-    packed_low = after(packed_low, back_two)
+    packed_low = after(packed_low, back_two, second_spread)
     back_two = to_layer(back_two, 1)
+    second_placed = place_rows(second_spread, 1)
     second_in = first_grad + core_sum(matmul(packed_low, weights[1][0]))
-    out_slabs, qkv_slabs = attention_grads(second_saved, attended_grad, packed_low)
-    qkv_two, out_two = slabs_along_x(qkv_slabs), slabs_along_x(out_slabs)
+    qkv_two, out_two = attention_grads(second_saved, attended_grad, packed_low)
+    second_low = second_in.astype(LOW)
+    second_in_spread = spread_rows(second_low)
 
     middle_grad, branch_grad, hidden_low, first_sums = backward_hidden(
-        first_saved, second_in.astype(LOW), weights[0], small[0]
-    )
-    middle_grad = after(middle_grad, back_two, in_two, outputs)
+        first_saved, second_low, weights[0], small[0]
+    )
+    middle_grad = after(middle_grad, back_two, in_two, first_placed, second_placed)
+    outputs = by_section(first_placed, second_placed).astype(WIDE)[None]
     in_two = along_x(in_two)
-    back_slabs, inner = feed_forward_grads(first_saved, branch_grad, hidden_low)
-    back_one = slabs_along_x(back_slabs)
-    in_one = over_z(inner)
+    back_one = slabs_along_x(counted_only(slab_grads(first_saved[6], branch_grad, chips)))
+    in_one = slabs_along_x(counted_only(slab_grads(hidden_low, first_saved[5], chips)))
     first_grad, attended_grad, packed_low, more_sums = backward_attention(
-        first_saved, segments, middle_grad, weights[0], small[0]
+        first_saved, segments, lengths, middle_grad, weights[0], small[0]
     )
     first_sums += more_sums
-    packed_low = after(packed_low, qkv_two, out_two, in_two)
-    in_two, qkv_two, out_two = to_layer(in_two, 1), to_layer(qkv_two, 1), to_layer(out_two, 1)
+    packed_low = after(packed_low, qkv_two, out_two, in_two, back_one)
+    in_two, back_one = to_layer(in_two, 1), to_layer(back_one, 0)
+    qkv_two, out_two = along_x(qkv_two), along_x(out_two)
+    qkv_one, out_one = attention_grads(first_saved, attended_grad, packed_low)
     first_in = first_grad + core_sum(matmul(packed_low, weights[0][0]))
-    out_slabs, qkv_slabs = attention_grads(first_saved, attended_grad, packed_low)
-    back_one = to_layer(back_one, 0)
-    qkv_one, out_one = slabs_along_x(qkv_slabs), slabs_along_x(out_slabs)
-    input_grads = return_rows(first_in, second_in)
-    back_shard = over_z(jnp.where(section == 0, back_one, back_two))
-    in_one = to_layer(along_x(in_one), 0)
-    in_shard = finish(jnp.where(section == 0, in_one, in_two))
-    qkv_one, out_one = to_layer(qkv_one, 0), to_layer(out_one, 0)
-    back_shard = finish(back_shard)
-    out_shard = finish(over_z(jnp.where(section == 0, out_one, out_two)))
-    qkv_shard = finish(over_z(jnp.where(section == 0, qkv_one, qkv_two)))
+    first_in = after(first_in, in_one, second_in_spread)
+    in_one = to_layer(in_one, 0)
+    second_in_placed = place_rows(second_in_spread, 1)
+    first_in_placed = place_rows(spread_rows(first_in), 0)
+    input_grads = by_section(first_in_placed, second_in_placed).astype(WIDE)[None]
+
+    back_shard = finish(over_z(by_section(back_one, back_two)))
+    in_shard = finish(by_section(over_z(in_one), in_two))
+    qkv_two, out_two = to_layer(qkv_two, 1), to_layer(out_two, 1)
+    qkv_one, out_one = to_layer(along_x(qkv_one), 0), to_layer(along_x(out_one), 0)
+    out_shard = finish(by_section(out_one, out_two))
+    qkv_shard = finish(by_section(qkv_one, qkv_two))
     qkv_grad = jnp.transpose(qkv_shard.reshape(2, 3, head_half, local), (3, 1, 0, 2)).reshape(local, 3, -1)
     out_grad_w = out_shard.reshape(-1, local)
     in_grad = jnp.transpose(in_shard.reshape(-1, local))

time: 1140 us -> 1210 us (1.061)
  local copies, waits for them, and re-layouts: 63.5 us -> 160 us
  waiting for transfers between devices: 428 us -> 369 us
  other arithmetic: 147 us -> 195 us
  Pallas kernels: 128 us -> 103 us
  starting transfers between devices: 174 us -> 188 us
    unnamed x212 -> x260, local copies, waits for them, and re-layouts: 22.5 us -> 84.8 us
    ppermute x85 -> x91, waiting for transfers between devices: 254 us -> 192 us  [move(): return lax.ppermute(value, AXES, pairs)]
    all_to_all x2 -> x4, waiting for transfers between devices: 54.6 us -> 12.5 us  [spread_rows(): lax.all_to_all(mine, 'tensor', split_axis=0, concat_axis=0, tiled=True)]
    reduce_scatter x5 -> x7, waiting for transfers between devices: 89.5 us -> 115 us  [over_z(): lax.psum_scatter(parts, 'tensor', scatter_dimension=0, tiled=False)]
    pallas_call x4, Pallas kernels: 128 us -> 103 us  [the longest x2 59.2 us: attend_backward(): pl.pallas_call(functools.partial(backward_kernel, widths), grid_spec=pltp...]
    slice x1 -> x5, local copies, waits for them, and re-layouts: 0.02 us -> 22.9 us  [the longest x4 22.2 us: spread_rows(): mine = choose(core, (parts[:, 0], parts[:, 1]))]
    convert_element_type x4 -> x7, other arithmetic: 6.52 us -> 25.5 us  [the longest x1 6.14 us: backward_hidden(): hidden_low = hidden_grad.astype(LOW)]
    all_to_all x2, waiting for transfers between devices: 1.39 us -> 19.3 us  [fetch_rows(): lax.all_to_all(mine, 'tensor', split_axis=0, concat_axis=0, tiled=True)]
  transfers between devices with their start and end apart: 95 -> 105, of which waited for: 31 -> 27; matrix products, arithmetic and copies ran while one was open for 25% -> 37% of each run, Pallas kernels for 9% -> 9%
where the time goes in v3:
time: 1210 us; the launch traced here: 1200 us
  waiting for transfers between devices  369 us (30%)
  other arithmetic  195 us (16%)
  starting transfers between devices  188 us (16%)
  matrix products  165 us (14%)
  local copies, waits for them, and re-layouts  160 us (13%)
  Pallas kernels  103 us (9%)
  between operations  17.3 us (1%)
    ppermute x91, waiting for transfers between devices, move(): return lax.ppermute(value, AXES, pairs)  192 us
    ppermute x91, starting transfers between devices, move(): return lax.ppermute(value, AXES, pairs)  158 us
    reduce_scatter x7, waiting for transfers between devices, over_z(): lax.psum_scatter(parts, 'tensor', scatter_dimension=0, tiled=False)  115 us
    unnamed x260, local copies, waits for them, and re-layouts  84.8 us
    dot_general x11, matrix products, lhs_inner(): lax.dot_general(lhs_mat, rhs_mat, (((0,), (0,)), ((), ())), preferred_ele...  64.1 us
    pallas_call x2, Pallas kernels, attend_backward(): pl.pallas_call(functools.partial(backward_kernel, widths), grid_spec=pltp...  59.2 us
    dot_general x8, matrix products, rhs_inner(): lax.dot_general(lhs_mat, rhs_mat, (((1,), (1,)), ((), ())), preferred_ele...  51.8 us
    dot_general x8, matrix products, matmul(): return jnp.dot(lhs_mat, rhs_mat, preferred_element_type=WIDE)  49.1 us
  transfers between devices with their start and end apart: 105, of which 27 were waited for; matrix products, arithmetic and copies ran while one was open for 37% of the time, Pallas kernels for 9%

profile of v3, /device:TPU:0, one launch (start us, length us, event | category | flops | bytes accessed | tf_op | source)
XLA Modules:
  0.0 1197.0 jit_solution(10730348854311355750)
XLA Ops:
  93.9 40.9 %collective-permute-done.44 = bf16[256,512]{1,0:T(8,128)(2,1)} collective-permute-done((bf16[256,512]{1,0:T(8,128)(2,1)}, bf16[256,512]{1,0:T(8,128)(2,1)}, u32[]{:S(2)}, u32[]{:S(2)}) %collective-permute-start.44) | collective-permute-done | bytes 262176 | tf_op jit(solution)/shard_map/ppermute | solution.py:27
  219.1 21.7 %shard_map.169 = (bf16[1024,512]{1,0:T(8,128)(2,1)S(1)}, f32[4,2,1024]{2,1,0:T(2,128)S(1)}) custom-call(s32[4]{0:T(128)S(1)} %compare_select_fusion.8.start_ref, s32[4]{0:T(128)S(1)} %get-tuple-element.119.kind_ref, bf16[1024,1536]{1,0:T(8,128)(2,1)S(1)} %add_convert_fusion.1.query_ref.key_ref.value_ref, ...), custom_call_target="tpu_custom_call" | custom-call | flops 4294967296 | bytes 4194304 | tf_op jit(solution)/shard_map/pallas_call | solution.py:244
  257.2 12.8 %collective-permute-done.40 = bf16[4,256,512]{2,1,0:T(8,128)(2,1)S(1)} collective-permute-done((bf16[4,256,512]{2,1,0:T(8,128)(2,1)S(1)}, bf16[4,256,512]{2,1,0:T(8,128)(2,1)S(1)}, u32[]{:S(2)}, u32[]{:S(2)}) %collective-permute-start.40) | collective-permute-done | bytes 1048608 | tf_op jit(solution)/shard_map/ppermute | solution.py:27
  331.0 7.7 multiply_convert_fusion.1
  370.3 21.7 %shard_map.170 = (bf16[1024,512]{1,0:T(8,128)(2,1)S(1)}, f32[4,2,1024]{2,1,0:T(2,128)S(1)}) custom-call(s32[4]{0:T(128)S(1)} %compare_select_fusion.8.start_ref, s32[4]{0:T(128)S(1)} %get-tuple-element.119.kind_ref, bf16[1024,1536]{1,0:T(8,128)(2,1)S(1)} %add_convert_fusion.query_ref.key_ref.value_ref, ...), custom_call_target="tpu_custom_call" | custom-call | flops 4294967296 | bytes 4194304 | tf_op jit(solution)/shard_map/pallas_call | solution.py:244
  408.4 19.3 %all-to-all-done.1 = bf16[4,128,1024]{2,1,0:T(8,128)(2,1)S(1)} async-done(((bf16[4,128,1024]{2,1,0:T(8,128)(2,1)}), bf16[4,128,1024]{2,1,0:T(8,128)(2,1)S(1)}, u32[]{:S(2)}, u32[]{:S(2)}) %all-to-all-start.1) | async-done | bytes 1048608 | tf_op jit(solution)/shard_map/all_to_all | solution.py:381
  435.9 9.1 multiply_convert_fusion
  501.7 12.0 %fusion.16 = (f32[2048]{0:T(1024)S(1)}, bf16[1024,2048]{1,0:T(8,128)(2,1)}, f32[1024,2048]{1,0:T(8,128)}) fusion(f32[1024,2048]{1,0:T(8,128)} %get-tuple-element.230, f32[2048]{0:T(1024)S(1)} %bitcast.422, bf16[1024,1024]{0,1:T(8,128)(2,1)S(1)} %convert_element_type.421, bf16[2048,1024]{1,0:T(8,128)(2,1)S(1)} %bitcast.327), kind=kOutput, calls=%fused_computation.32 | convolution fusion | flops 4322228224 | bytes 27279360 | tf_op jit(solution)/shard_map/dot_general | solution.py:64
  513.7 11.8 convolution_convert_fusion.2
  533.5 11.9 convolution_convert_fusion.12
  608.6 29.7 %shard_map.171 = (bf16[1024,1536]{1,0:T(8,128)(2,1)S(1)}, f32[4,2,128]{2,1,0:T(2,128)S(1)}) custom-call(s32[4]{0:T(128)S(1)} %compare_select_fusion.8.start_ref, s32[4]{0:T(128)S(1)} %get-tuple-element.119.kind_ref, bf16[1024,1536]{1,0:T(8,128)(2,1)} %copy-done.3, bf16[1024,1536]{1,0:T(8,128)(2,1)} %copy-done.3, bf16[1024,1536]{1,0:T(8,128)(2,1)} %copy-done.3, ...), custom_call_target="tpu_custom_call" | custom-call | flops 10737418240 | bytes 8388608 | tf_op jit(solution)/shard_map/pallas_call | solution.py:270
  645.0 7.6 convolution_convert_fusion.11
  659.4 7.7 convolution_convert_fusion.1
  679.9 10.7 fusion.18
  711.2 17.5 %collective-permute-done.69 = bf16[2048,512]{1,0:T(8,128)(2,1)} collective-permute-done((bf16[2048,512]{1,0:T(8,128)(2,1)}, bf16[2048,512]{1,0:T(8,128)(2,1)}, u32[]{:S(2)}, u32[]{:S(2)}) %collective-permute-start.69) | collective-permute-done | bytes 2097184 | tf_op jit(solution)/shard_map/ppermute | solution.py:27
  738.2 34.8 %collective-permute-done.71 = bf16[2048,512]{1,0:T(8,128)(2,1)} collective-permute-done((bf16[2048,512]{1,0:T(8,128)(2,1)}, bf16[2048,512]{1,0:T(8,128)(2,1)}, u32[]{:S(2)}, u32[]{:S(2)}) %collective-permute-start.71) | collective-permute-done | bytes 2097184 | tf_op jit(solution)/shard_map/ppermute | solution.py:27
  806.4 29.5 %shard_map.172 = (bf16[1024,1536]{1,0:T(8,128)(2,1)S(1)}, f32[4,2,128]{2,1,0:T(2,128)S(1)}) custom-call(s32[4]{0:T(128)S(1)} %compare_select_fusion.8.start_ref, s32[4]{0:T(128)S(1)} %get-tuple-element.119.kind_ref, bf16[1024,1536]{1,0:T(8,128)(2,1)} %copy-done.2, bf16[1024,1536]{1,0:T(8,128)(2,1)} %copy-done.2, bf16[1024,1536]{1,0:T(8,128)(2,1)} %copy-done.2, ...), custom_call_target="tpu_custom_call" | custom-call | flops 10737418240 | bytes 8388608 | tf_op jit(solution)/shard_map/pallas_call | solution.py:270
  844.5 13.1 %collective-permute-done.68 = bf16[512,512]{1,0:T(8,128)(2,1)S(1)} collective-permute-done((bf16[512,512]{1,0:T(8,128)(2,1)S(1)}, bf16[512,512]{1,0:T(8,128)(2,1)S(1)}, u32[]{:S(2)}, u32[]{:S(2)}) %collective-permute-start.68) | collective-permute-done | bytes 524320 | tf_op jit(solution)/shard_map/ppermute | solution.py:27
  858.9 7.8 convolution_convert_fusion
  866.7 9.6 collective-permute-start.56
  944.4 30.3 %all-reduce.2.cloned.1.call-done = f32[2,12,1024]{2,0,1:T(2,128)} async-done(((f32[2,12,1024]{2,0,1:T(2,128)}), f32[2,12,1024]{2,0,1:T(2,128)}) %all-reduce.2.cloned.1.call-update) | async-done | bytes 98320 | tf_op jit(solution)/shard_map/psum | solution.py:626
  1024.0 69.6 %reduce-scatter.14.cloned.1.call-done = bf16[1,384,1024]{2,1,0:T(8,128)(2,1)} async-done(((bf16[4,384,1024]{2,1,0:T(8,128)(2,1)}), bf16[1,384,1024]{2,1,0:T(8,128)(2,1)}) %reduce-scatter.14.cloned.1.call-update) | async-done | bytes 786448 | tf_op jit(solution)/shard_map/reduce_scatter | solution.py:460
  1096.9 43.1 %reduce-scatter.20.cloned.1.call-done = bf16[1,512,512]{2,1,0:T(8,128)(2,1)} async-done(((bf16[4,512,512]{2,1,0:T(8,128)(2,1)}), bf16[1,512,512]{2,1,0:T(8,128)(2,1)}) %reduce-scatter.20.cloned.1.call-update) | async-done | bytes 524304 | tf_op jit(solution)/shard_map/reduce_scatter | solution.py:460
  1153.2 24.3 %collective-permute-done.77 = bf16[384,512]{1,0:T(8,128)(2,1)} collective-permute-done((bf16[384,512]{1,0:T(8,128)(2,1)S(1)}, bf16[384,512]{1,0:T(8,128)(2,1)}, u32[]{:S(2)}, u32[]{:S(2)}) %collective-permute-start.77) | collective-permute-done | bytes 393248 | tf_op jit(solution)/shard_map/ppermute | solution.py:27
  (713 shorter events, 675.4 us)
Async XLA Ops:
  30.4 61.6 %collective-permute-start.22 = (bf16[512,256]{1,0:T(8,128)(2,1)}, bf16[512,256]{1,0:T(8,128)(2,1)}, u32[]{:S(2)}, u32[]{:S(2)}) collective-permute-start(bf16[512,256]{1,0:T(8,128)(2,1)} %get-tuple-element.173), channel_id=1, source_target_pairs={{0,4},{1,5},{2,6},{3,7},{4,0},{5,1},{6,2},{7,3},{8,12},{9,13},{10,... | collective-permute-start | bytes 786440 | tf_op jit(solution)/shard_map/ppermute | solution.py:27
  83.3 76.2 %collective-permute-start.10 = (bf16[4,512,512]{2,1,0:T(8,128)(2,1)S(1)}, bf16[4,512,512]{2,1,0:T(8,128)(2,1)}, u32[]{:S(2)}, u32[]{:S(2)}) collective-permute-start(bf16[4,512,512]{2,1,0:T(8,128)(2,1)S(1)} %bitcast_dynamic-update-slice_fusion.8), channel_id=1, source_target_pairs={{0,16},{1,17},{2,18},{3,19},{4,20},{5,21},{6,22},{7,23},{8,24},{9,... | collective-permute-start | bytes 6291464 | tf_op jit(solution)/shard_map/ppermute | solution.py:27
  85.7 77.5 %collective-permute-start.11 = (bf16[4,512,512]{2,1,0:T(8,128)(2,1)S(1)}, bf16[4,512,512]{2,1,0:T(8,128)(2,1)}, u32[]{:S(2)}, u32[]{:S(2)}) collective-permute-start(bf16[4,512,512]{2,1,0:T(8,128)(2,1)S(1)} %bitcast_dynamic-update-slice_fusion.8), channel_id=1, source_target_pairs={{0,8},{1,9},{2,10},{3,11},{4,12},{5,13},{6,14},{7,15},{8,0},{9,1},... | collective-permute-start | bytes 6291464 | tf_op jit(solution)/shard_map/ppermute | solution.py:27
  159.5 95.3 %collective-permute-start.47 = (bf16[128,512]{1,0:T(8,128)(2,1)S(1)}, bf16[128,512]{1,0:T(8,128)(2,1)S(1)}, u32[]{:S(2)}, u32[]{:S(2)}) collective-permute-start(bf16[128,512]{1,0:T(8,128)(2,1)S(1)} %slice.450), channel_id=1, source_target_pairs={{0,16},{1,17},{2,18},{3,19},{4,20},{5,21},{6,22},{7,23},{8,24},{9,... | collective-permute-start | bytes 393224 | tf_op jit(solution)/shard_map/ppermute | solution.py:27
  199.6 81.9 %collective-permute-start.29 = (bf16[4,512,512]{2,1,0:T(8,128)(2,1)}, bf16[4,512,512]{2,1,0:T(8,128)(2,1)}, u32[]{:S(2)}, u32[]{:S(2)}) collective-permute-start(bf16[4,512,512]{2,1,0:T(8,128)(2,1)} %bitcast_dynamic-update-slice_fusion.4), channel_id=1, source_target_pairs={{0,16},{1,17},{2,18},{3,19},{4,20},{5,21},{6,22},{7,23},{8,24},{9,... | collective-permute-start | bytes 6291464 | tf_op jit(solution)/shard_map/ppermute | solution.py:27
  202.3 93.0 %collective-permute-start.30 = (bf16[4,512,512]{2,1,0:T(8,128)(2,1)}, bf16[4,512,512]{2,1,0:T(8,128)(2,1)}, u32[]{:S(2)}, u32[]{:S(2)}) collective-permute-start(bf16[4,512,512]{2,1,0:T(8,128)(2,1)} %bitcast_dynamic-update-slice_fusion.4), channel_id=1, source_target_pairs={{0,8},{1,9},{2,10},{3,11},{4,12},{5,13},{6,14},{7,15},{8,0},{9,1},... | collective-permute-start | bytes 6291464 | tf_op jit(solution)/shard_map/ppermute | solution.py:27
  400.9 387.8 %reduce-scatter.8.cloned.1.call-start = ((), (), s32[]{:S(2)}) async-start(), calls=%async_computation.13 | async-start | bytes 5242880 | tf_op jit(solution)/shard_map/reduce_scatter | solution.py:460
  591.4 267.5 %reduce-scatter.12.cloned.1.call-start = ((), (), s32[]{:S(2)}) async-start(), calls=%async_computation.15 | async-start | bytes 1310720 | tf_op jit(solution)/shard_map/reduce_scatter | solution.py:460
  644.9 214.0 %reduce-scatter.10.cloned.1.call-start = ((), (), s32[]{:S(2)}) async-start(), calls=%async_computation.14 | async-start | bytes 3932160 | tf_op jit(solution)/shard_map/reduce_scatter | solution.py:460
  652.8 131.7 %collective-permute-start.67 = (bf16[2048,512]{1,0:T(8,128)(2,1)}, bf16[2048,512]{1,0:T(8,128)(2,1)}, u32[]{:S(2)}, u32[]{:S(2)}) collective-permute-start(bf16[2048,512]{1,0:T(8,128)(2,1)} %add_convert_fusion.8), channel_id=1, source_target_pairs={{0,16},{1,17},{2,18},{3,19},{4,20},{5,21},{6,22},{7,23},{8,24},{9,... | collective-permute-start | bytes 6291464 | tf_op jit(solution)/shard_map/ppermute | solution.py:27
  667.2 255.2 %reduce-scatter.16.cloned.1.call-start = ((), (), s32[]{:S(2)}) async-start(), calls=%async_computation.17 | async-start | bytes 1310720 | tf_op jit(solution)/shard_map/reduce_scatter | solution.py:460
  702.9 70.0 %collective-permute-start.71 = (bf16[2048,512]{1,0:T(8,128)(2,1)}, bf16[2048,512]{1,0:T(8,128)(2,1)}, u32[]{:S(2)}, u32[]{:S(2)}) collective-permute-start(bf16[2048,512]{1,0:T(8,128)(2,1)} %convolution_convert_fusion.3), channel_id=1, source_target_pairs={{0,8},{1,9},{2,10},{3,11},{4,12},{5,13},{6,14},{7,15},{8,0},{9,1},... | collective-permute-start | bytes 6291464 | tf_op jit(solution)/shard_map/ppermute | solution.py:27
  711.1 66.9 %collective-permute-start.66 = (bf16[1024,1024]{0,1:T(8,128)(2,1)}, bf16[1024,1024]{0,1:T(8,128)(2,1)}, u32[]{:S(2)}, u32[]{:S(2)}) collective-permute-start(bf16[1024,1024]{0,1:T(8,128)(2,1)} %convolution_convert_fusion.10), channel_id=1, source_target_pairs={{0,4},{1,5},{2,6},{3,7},{4,0},{5,1},{6,2},{7,3},{8,12},{9,13},{10,... | collective-permute-start | bytes 6291464 | tf_op jit(solution)/shard_map/ppermute | solution.py:27
  776.6 62.1 %collective-permute-start.86 = (bf16[2048,512]{1,0:T(8,128)(2,1)}, bf16[2048,512]{1,0:T(8,128)(2,1)}, u32[]{:S(2)}, u32[]{:S(2)}) collective-permute-start(bf16[2048,512]{1,0:T(8,128)(2,1)} %add_convert_fusion.4), channel_id=1, source_target_pairs={{16,0},{17,1},{18,2},{19,3},{20,4},{21,5},{22,6},{23,7},{24,8},{25... | collective-permute-start | bytes 6291464 | tf_op jit(solution)/shard_map/ppermute | solution.py:27
  802.7 172.0 %all-reduce.2.cloned.1.call-start = ((), (), s32[]{:S(2)}) async-start(), calls=%async_computation.20 | async-start | bytes 196608 | tf_op jit(solution)/shard_map/psum | solution.py:626
  838.6 183.9 %reduce-scatter.18.cloned.1.call-start = ((), (), s32[]{:S(2)}) async-start(), calls=%async_computation.18 | async-start | bytes 2621440 | tf_op jit(solution)/shard_map/reduce_scatter | solution.py:460
  843.0 250.6 %reduce-scatter.14.cloned.1.call-start = ((), (), s32[]{:S(2)}) async-start(), calls=%async_computation.16 | async-start | bytes 3932160 | tf_op jit(solution)/shard_map/reduce_scatter | solution.py:460
  909.5 230.5 %reduce-scatter.20.cloned.1.call-start = ((), (), s32[]{:S(2)}) async-start(), calls=%async_computation.19 | async-start | bytes 2621440 | tf_op jit(solution)/shard_map/reduce_scatter | solution.py:460
  915.9 69.7 %collective-permute-start.70 = (bf16[1024,1024]{0,1:T(8,128)(2,1)S(1)}, bf16[1024,1024]{0,1:T(8,128)(2,1)}, u32[]{:S(2)}, u32[]{:S(2)}) collective-permute-start(bf16[1024,1024]{0,1:T(8,128)(2,1)S(1)} %convolution_convert_fusion.9), channel_id=1, source_target_pairs={{0,4},{1,5},{2,6},{3,7},{4,0},{5,1},{6,2},{7,3},{8,12},{9,13},{10,... | collective-permute-start | bytes 6291464 | tf_op jit(solution)/shard_map/ppermute | solution.py:27
  936.8 244.0 %collective-permute-start.74 = (bf16[4,128,1024]{2,1,0:T(8,128)(2,1)}, bf16[4,128,1024]{2,1,0:T(8,128)(2,1)}, u32[]{:S(2)}, u32[]{:S(2)}) collective-permute-start(bf16[4,128,1024]{2,1,0:T(8,128)(2,1)} %all-to-all-done.4), channel_id=1, source_target_pairs={{0,16},{1,17},{2,18},{3,19},{8,24},{9,25},{10,26},{11,27},{16,20},... | collective-permute-start | bytes 3145736 | tf_op jit(solution)/shard_map/ppermute | solution.py:27
  939.0 241.8 %collective-permute-start.75 = (bf16[4,128,1024]{2,1,0:T(8,128)(2,1)}, bf16[4,128,1024]{2,1,0:T(8,128)(2,1)}, u32[]{:S(2)}, u32[]{:S(2)}) collective-permute-start(bf16[4,128,1024]{2,1,0:T(8,128)(2,1)} %all-to-all-done.4), channel_id=1, source_target_pairs={{4,16},{5,17},{6,18},{7,19},{12,24},{13,25},{14,26},{15,27},{20,20... | collective-permute-start | bytes 3145736 | tf_op jit(solution)/shard_map/ppermute | solution.py:27
  1011.4 130.6 %all-to-all-start.5 = ((bf16[4,128,1024]{2,1,0:T(8,128)(2,1)}), bf16[4,128,1024]{2,1,0:T(8,128)(2,1)}, u32[]{:S(2)}, u32[]{:S(2)}) async-start(bf16[4,128,1024]{2,1,0:T(8,128)(2,1)} %select_bitcast_fusion), calls=%async_computation.8 | async-start | bytes 2097152 | tf_op jit(solution)/shard_map/all_to_all | solution.py:388
  1017.8 128.1 %collective-permute-start.79 = (bf16[384,512]{1,0:T(8,128)(2,1)S(1)}, bf16[384,512]{1,0:T(8,128)(2,1)}, u32[]{:S(2)}, u32[]{:S(2)}) collective-permute-start(bf16[384,512]{1,0:T(8,128)(2,1)S(1)} %add_convert_fusion.16), channel_id=1, source_target_pairs={{0,16},{1,17},{2,18},{3,19},{4,20},{5,21},{6,22},{7,23},{8,24},{9,... | collective-permute-start | bytes 1179656 | tf_op jit(solution)/shard_map/ppermute | solution.py:27
  1023.9 117.9 %collective-permute-start.88 = (bf16[512,256]{1,0:T(8,128)(2,1)S(1)}, bf16[512,256]{1,0:T(8,128)(2,1)S(1)}, u32[]{:S(2)}, u32[]{:S(2)}) collective-permute-start(bf16[512,256]{1,0:T(8,128)(2,1)S(1)} %get-tuple-element.166), channel_id=1, source_target_pairs={{0,4},{1,5},{2,6},{3,7},{4,0},{5,1},{6,2},{7,3},{8,12},{9,13},{10,... | collective-permute-start | bytes 786440 | tf_op jit(solution)/shard_map/ppermute | solution.py:27
  (202 other events, 3752.5 us)
Sparse Core Ops, SparseCore 0:
  525.6 107.2 reduce-scatter.7
  645.0 29.3 reduce-scatter.11
  676.8 58.8 reduce-scatter.9
  802.8 30.2 reduce-scatter.15
  839.5 135.1 all-reduce.1
  976.9 45.5 reduce-scatter.17
  1024.8 68.7 reduce-scatter.13
  1095.9 44.1 reduce-scatter.19

commit v4 on v3

--- a/solution.py
+++ b/solution.py
@@ -48,6 +48,10 @@
 
 def after(value, *others):
     return lax.optimization_barrier((value,) + others)[0]
+
+
+def tie(*values):
+    return lax.optimization_barrier(values)
 
 
 def matmul(lhs_mat, rhs_mat):
@@ -327,10 +331,10 @@
     middle, active, slope, second_sum = saved[5:]
     second_grad, gain_two, bias_two = norm_backward(second_sum, gains[1], grad_rows.astype(WIDE))
     branch_grad = second_grad.astype(LOW)
-    hidden_grad = rhs_inner(branch_grad, w_back) * slope.astype(WIDE)
-    hidden_low = hidden_grad.astype(LOW)
+    hidden_low = (rhs_inner(branch_grad, w_back) * slope.astype(WIDE)).astype(LOW)
     middle_grad = second_grad + core_sum(matmul(hidden_low, w_in))
-    sums = (gain_two, jnp.sum(second_grad, axis=0), bias_two, jnp.sum(hidden_grad, axis=0))
+    inner_sum = matmul(jnp.ones((8, hidden_low.shape[0]), LOW), hidden_low)[0]
+    sums = (gain_two, jnp.sum(second_grad, axis=0), bias_two, inner_sum)
     return middle_grad, branch_grad, hidden_low, sums
 
 
@@ -371,20 +375,29 @@
         return jnp.concatenate([choose(chip ^ k, slabs) for k in range(chips)], axis=-1)
 
     def fetch_rows(block, *before):
-        parts = block.reshape(micro_count, 2, own_rows // 2, width)
-        kept = choose(core, (parts[:, 0], parts[:, 1]))
-        given = choose(core, (parts[:, 1], parts[:, 0]))
+        half = own_rows // 2
+        kept = choose(core, (block[:, :half], block[:, half:]))
+        given = choose(core, (block[:, half:], block[:, :half]))
         received = move(given, lambda s, d, t: (s, d ^ 1, t) if d % 2 == s else None)
         mine = jnp.where(core == section, kept, received)
         mine = jnp.repeat(mine, repeats, axis=0) if repeats > 1 else mine
         mine = after(mine, *before) if before else mine
         mine = lax.all_to_all(mine, "tensor", split_axis=0, concat_axis=0, tiled=True)
         whole = by_core(core, mine, to_other_core(mine), 1)
-        return relative(whole.reshape(ranks * own_rows, width)), mine
+        return relative(whole.reshape(ranks * own_rows, width))
+
+    def spread_both(first, second):
+        chosen = relative(jnp.where(core == 0, first, second)).reshape(ranks, own_rows, width)
+        spread = lax.all_to_all(chosen, "tensor", split_axis=0, concat_axis=0, tiled=True)
+        return spread.reshape(micro_count, repeats, own_rows, width)[:, 0]
+
+    def place_both(spread):
+        return move(spread, lambda s, d, t: (d % 2, (d // 2) * 2 + s, t))
 
     def spread_rows(value):
-        parts = relative(value.astype(LOW)).reshape(ranks, 2, own_rows // 2, width)
-        mine = choose(core, (parts[:, 0], parts[:, 1]))
+        parts = relative(value).reshape(ranks, own_rows, width)
+        half = own_rows // 2
+        mine = choose(core, (parts[:, :half], parts[:, half:]))
         spread = lax.all_to_all(mine, "tensor", split_axis=0, concat_axis=0, tiled=True)
         return spread.reshape((micro_count, repeats) + spread.shape[1:])[:, 0]
 
@@ -438,26 +451,26 @@
         both = over_ranks(jnp.stack(over_chips(own)))
         return [both[:, layer] for layer in range(2)]
 
-    def along_x(parts):
-        slabs = jnp.split(parts, chips, axis=-1)
-        total = slabs[0].astype(WIDE)
-        for k in range(1, chips):
-            total = total + move(slabs[k], lambda s, d, t: (s, d ^ (2 * k), t)).astype(WIDE)
+    def from_x(slabs):
+        return [move(slabs[k], lambda s, d, t: (s, d ^ (2 * k), t)) for k in range(1, chips)]
+
+    def from_section(part, layer):
+        return move(part, lambda s, d, t: (layer, d, t) if s != layer else None)
+
+    def add(part, received):
+        total = part.astype(WIDE)
+        for other in received:
+            total = total + other.astype(WIDE)
         return total.astype(LOW)
 
-    def slabs_along_x(slabs):
-        total = slabs[0].astype(WIDE)
-        for k in range(1, chips):
-            total = total + move(slabs[k], lambda s, d, t: (s, d ^ (2 * k), t)).astype(WIDE)
-        return total.astype(LOW)
-
-    def to_layer(part, layer):
-        sent = move(part, lambda s, d, t: (layer, d, t) if s != layer else None)
-        return (part.astype(WIDE) + sent.astype(WIDE)).astype(LOW)
-
-    def over_z(parts):
-        parts = parts.reshape((ranks, -1) + parts.shape[1:])
-        return lax.psum_scatter(parts, "tensor", scatter_dimension=0, tiled=False).astype(LOW)
+    def from_z(parts):
+        return lax.all_to_all(parts, "tensor", split_axis=0, concat_axis=0, tiled=True)
+
+    def add_ranks(parts):
+        return jnp.sum(parts.astype(WIDE), axis=0).astype(LOW)
+
+    def ranked(slab):
+        return slab.reshape((ranks, -1) + slab.shape[1:])
 
     def counted_only(slabs):
         return [jnp.where(counted, slab, jnp.zeros((), LOW)) for slab in slabs] if repeats > 1 else slabs
@@ -481,9 +494,10 @@
     in_own = own_half(in_first)
     back_two = jnp.stack(over_chips(back_own[later:]))
     attention_item = over_ranks(attention_own)
+    attention_item, back_two = tie(attention_item, back_two)
     attention_all = over_chips(attention_item)
-    rows, rows_here = fetch_rows(block_input, attention_item)
-    in_item = over_ranks(after(in_own, rows_here))
+    rows = fetch_rows(block_input, attention_item)
+    in_item = over_ranks(after(in_own, attention_item))
     in_all = over_chips(in_item)
     back_item = over_ranks(after(back_own[:later], in_item))
     back_one = over_chips(back_item)
@@ -501,6 +515,7 @@
 
     gain_count, bias_count = gains.shape[1], biases.shape[1]
     packed_small = jnp.concatenate([gains, biases, ffn_bias.reshape(1, -1, local)], axis=1)
+    packed_small, seq_lengths = tie(packed_small, seq_lengths, attention_item)[:2]
     table_parts = [
         [
             packed_small
@@ -540,67 +555,88 @@
 
     first_out, first_saved = layer_forward(rows, segments, lengths, weights[0], small[0])
     first_low = first_out.astype(LOW)
-    cotangent, cotangent_here = fetch_rows(out_grad, first_low, back_two)
+    cotangent = fetch_rows(out_grad, back_two)
     cotangent = jnp.where(live, cotangent, jnp.zeros((), LOW))
     second_out, second_saved = layer_forward(first_low, segments, lengths, weights[1], small[1])
-    first_spread = spread_rows(after(first_low, cotangent_here))
-    second_spread = spread_rows(second_out)
-
-    def matrix_grad(hidden, features):
-        return counted_only([lhs_inner(hidden, features).astype(LOW)])[0]
+    spread = spread_both(first_low, second_out.astype(LOW))
+
+    def hidden_grads(hidden, features):
+        return [ranked(slab) for slab in counted_only(slab_grads(hidden, features, chips))]
 
     def attention_grads(saved, attended_grad, packed_low):
-        qkv = over_z(matrix_grad(packed_low, saved[0]))
-        return qkv, over_z(matrix_grad(saved[3], attended_grad))
+        qkv = hidden_grads(packed_low, saved[0])
+        out = hidden_grads(saved[3], attended_grad)
+        return [jnp.concatenate(pair, axis=1) for pair in zip(qkv, out)]
 
     middle_grad, branch_grad, hidden_low, second_sums = backward_hidden(
         second_saved, cotangent, weights[1], small[1]
     )
-    middle_grad = after(middle_grad, first_spread)
-    first_placed = place_rows(first_spread, 0)
-    back_two = slabs_along_x(counted_only(slab_grads(second_saved[6], branch_grad, chips)))
-    in_two = over_z(matrix_grad(hidden_low, second_saved[5]))
+    back_slabs = hidden_grads(second_saved[6], branch_grad)
+    back_here = from_x(back_slabs)
+    inner = counted_only([lhs_inner(hidden_low, second_saved[5]).astype(LOW)])[0]
+    in_here = from_z(ranked(inner))
     first_grad, attended_grad, packed_low, more_sums = backward_attention(
         second_saved, segments, lengths, middle_grad, weights[1], small[1]
     )
     second_sums += more_sums
-    packed_low = after(packed_low, back_two, second_spread)
-    back_two = to_layer(back_two, 1)
-    second_placed = place_rows(second_spread, 1)
+    packed_low, spread, *back_here = tie(packed_low, spread, *back_here)
+    back_two = add(back_slabs[0], back_here)
+    back_sent = from_section(back_two, 1)
+    placed = place_both(spread)
     second_in = first_grad + core_sum(matmul(packed_low, weights[1][0]))
-    qkv_two, out_two = attention_grads(second_saved, attended_grad, packed_low)
+    attention_slabs = attention_grads(second_saved, attended_grad, packed_low)
+    attention_here = from_x(attention_slabs)
     second_low = second_in.astype(LOW)
-    second_in_spread = spread_rows(second_low)
 
     middle_grad, branch_grad, hidden_low, first_sums = backward_hidden(
         first_saved, second_low, weights[0], small[0]
     )
-    middle_grad = after(middle_grad, back_two, in_two, first_placed, second_placed)
-    outputs = by_section(first_placed, second_placed).astype(WIDE)[None]
-    in_two = along_x(in_two)
-    back_one = slabs_along_x(counted_only(slab_grads(first_saved[6], branch_grad, chips)))
-    in_one = slabs_along_x(counted_only(slab_grads(hidden_low, first_saved[5], chips)))
+    middle_grad, back_sent, placed = tie(middle_grad, back_sent, placed)
+    back_two = add(back_two, [back_sent])
+    outputs = placed.astype(WIDE)[None]
+    second_in_spread = spread_rows(second_low)
+    back_slabs = hidden_grads(first_saved[6], branch_grad)
+    back_here = from_x(back_slabs)
+    in_slabs = hidden_grads(hidden_low, first_saved[5])
+    in_one_here = from_x(in_slabs)
     first_grad, attended_grad, packed_low, more_sums = backward_attention(
         first_saved, segments, lengths, middle_grad, weights[0], small[0]
     )
     first_sums += more_sums
-    packed_low = after(packed_low, qkv_two, out_two, in_two, back_one)
-    in_two, back_one = to_layer(in_two, 1), to_layer(back_one, 0)
-    qkv_two, out_two = along_x(qkv_two), along_x(out_two)
-    qkv_one, out_one = attention_grads(first_saved, attended_grad, packed_low)
+    packed_low, in_here, *attention_here = tie(packed_low, in_here, *attention_here)
+    attention_two = add(attention_slabs[0], attention_here)
+    attention_sent = from_section(attention_two, 1)
+    in_two_slabs = jnp.split(add_ranks(in_here), chips, axis=-1)
+    in_two_here = from_x(in_two_slabs)
     first_in = first_grad + core_sum(matmul(packed_low, weights[0][0]))
-    first_in = after(first_in, in_one, second_in_spread)
-    in_one = to_layer(in_one, 0)
-    second_in_placed = place_rows(second_in_spread, 1)
-    first_in_placed = place_rows(spread_rows(first_in), 0)
-    input_grads = by_section(first_in_placed, second_in_placed).astype(WIDE)[None]
-
-    back_shard = finish(over_z(by_section(back_one, back_two)))
-    in_shard = finish(by_section(over_z(in_one), in_two))
-    qkv_two, out_two = to_layer(qkv_two, 1), to_layer(out_two, 1)
-    qkv_one, out_one = to_layer(along_x(qkv_one), 0), to_layer(along_x(out_one), 0)
-    out_shard = finish(by_section(out_one, out_two))
-    qkv_shard = finish(by_section(qkv_one, qkv_two))
+    attention_slabs = attention_grads(first_saved, attended_grad, packed_low)
+    attention_here = from_x(attention_slabs)
+    first_in, second_in_spread, *back_here = tie(first_in, second_in_spread, *back_here)
+    back_one = add(back_slabs[0], back_here)
+    back_sent = from_section(back_one, 0)
+    first_in_spread = spread_rows(first_in.astype(LOW))
+    second_placed = place_rows(second_in_spread, 1)
+
+    back_sent, *in_one_here = tie(back_sent, *in_one_here)
+    in_one = add(in_slabs[0], in_one_here)
+    in_one_sent = from_section(in_one, 0)
+    back_here = from_z(by_section(add(back_one, [back_sent]), back_two))
+    in_two = add(in_two_slabs[0], in_two_here)
+    in_two_sent = from_section(in_two, 1)
+    attention_two = add(attention_two, [attention_sent])
+    in_one_sent, *attention_here = tie(in_one_sent, *attention_here)
+    attention_one = add(attention_slabs[0], attention_here)
+    attention_one_sent = from_section(attention_one, 0)
+    in_one_here = from_z(add(in_one, [in_one_sent]))
+    in_two = add(in_two, [in_two_sent])
+    back_shard = finish(add_ranks(back_here))
+    first_placed = place_rows(first_in_spread, 0)
+    attention_one = add(attention_one, [attention_one_sent])
+    attention_here = from_z(by_section(attention_one, attention_two))
+    input_grads = by_section(first_placed, second_placed).astype(WIDE)[None]
+    in_shard = finish(by_section(add_ranks(in_one_here), in_two))
+    attention_shard = finish(add_ranks(attention_here))
+    qkv_shard, out_shard = attention_shard[:, : 3 * head_half], attention_shard[:, 3 * head_half :]
     qkv_grad = jnp.transpose(qkv_shard.reshape(2, 3, head_half, local), (3, 1, 0, 2)).reshape(local, 3, -1)
     out_grad_w = out_shard.reshape(-1, local)
     in_grad = jnp.transpose(in_shard.reshape(-1, local))

time: 1210 us -> 1170 us (0.967)
  local copies, waits for them, and re-layouts: 160 us -> 86 us
  waiting for transfers between devices: 369 us -> 403 us
  starting transfers between devices: 188 us -> 214 us
  matrix products: 165 us -> 144 us
  other arithmetic: 195 us -> 181 us
    reduce_scatter x7 -> x0, waiting for transfers between devices: 115 us -> none  [over_z(): lax.psum_scatter(parts, 'tensor', scatter_dimension=0, tiled=False)]
    psum x1, waiting for transfers between devices: 30.3 us -> 116 us  [on_device(): lax.psum(table, AXES)]
    ppermute x91 -> x83, waiting for transfers between devices: 192 us -> 274 us  [move(): return lax.ppermute(value, AXES, pairs)]
    unnamed x260 -> x244, local copies, waits for them, and re-layouts: 84.8 us -> 35.5 us
    all_to_all x0 -> x5, starting transfers between devices: none -> 24.4 us  [the longest x4 19.3 us: from_z(): lax.all_to_all(parts, 'tensor', split_axis=0, concat_axis=0, tiled=True)]
    slice x4 -> x2, local copies, waits for them, and re-layouts: 22.2 us -> 0.77 us  [the longest x1 0.72 us: on_device(): attention_shard[:, 3 * head_half:]]
    all_to_all x2, waiting for transfers between devices: 19.3 us -> 3.11 us  [fetch_rows(): lax.all_to_all(mine, 'tensor', split_axis=0, concat_axis=0, tiled=True)]
    dot_general x11 -> x15, matrix products: 64.1 us -> 50.1 us  [lhs_inner(): lax.dot_general(lhs_mat, rhs_mat, (((0,), (0,)), ((), ())), preferred_ele...]
  transfers between devices with their start and end apart: 105 -> 93, of which waited for: 27 -> 32; matrix products, arithmetic and copies ran while one was open for 37% -> 27% of each run, Pallas kernels for 9% -> 7%
where the time goes in v4:
time: 1170 us; the launch traced here: 1150 us
  waiting for transfers between devices  403 us (34%)
  starting transfers between devices  214 us (18%)
  other arithmetic  181 us (15%)
  matrix products  144 us (12%)
  Pallas kernels  107 us (9%)
  local copies, waits for them, and re-layouts  86 us (7%)
  between operations  17 us (1%)
    ppermute x83, waiting for transfers between devices, move(): return lax.ppermute(value, AXES, pairs)  274 us
    ppermute x83, starting transfers between devices, move(): return lax.ppermute(value, AXES, pairs)  170 us
    psum x1, waiting for transfers between devices, on_device(): lax.psum(table, AXES)  116 us
    pallas_call x2, Pallas kernels, attend_backward(): pl.pallas_call(functools.partial(backward_kernel, widths), grid_spec=pltp...  61.3 us
    dot_general x15, matrix products, lhs_inner(): lax.dot_general(lhs_mat, rhs_mat, (((0,), (0,)), ((), ())), preferred_ele...  50.1 us
    dot_general x10, matrix products, matmul(): return jnp.dot(lhs_mat, rhs_mat, preferred_element_type=WIDE)  47.7 us
    dot_general x8, matrix products, rhs_inner(): lax.dot_general(lhs_mat, rhs_mat, (((1,), (1,)), ((), ())), preferred_ele...  45.9 us
    pallas_call x2, Pallas kernels, attend_forward(): pl.pallas_call(functools.partial(forward_kernel, widths), grid_spec=pltpu...  45.4 us
  transfers between devices with their start and end apart: 93, of which 32 were waited for; matrix products, arithmetic and copies ran while one was open for 27% of the time, Pallas kernels for 7%

profile of v4, /device:TPU:0, one launch (start us, length us, event | category | flops | bytes accessed | tf_op | source)
XLA Modules:
  0.0 1151.5 jit_solution(12451781920695022217)
XLA Ops:
  103.8 16.8 %collective-permute-done.29 = bf16[512,512]{1,0:T(8,128)(2,1)S(1)} collective-permute-done((bf16[512,512]{1,0:T(8,128)(2,1)S(1)}, bf16[512,512]{1,0:T(8,128)(2,1)S(1)}, u32[]{:S(2)}, u32[]{:S(2)}) %collective-permute-start.29) | collective-permute-done | bytes 524320 | tf_op jit(solution)/shard_map/ppermute | solution.py:27
  122.5 9.8 collective-permute-start.32
  132.3 9.4 collective-permute-done.30
  221.2 23.5 %collective-permute-done.17 = bf16[2,512,512]{2,1,0:T(8,128)(2,1)} collective-permute-done((bf16[2,512,512]{2,1,0:T(8,128)(2,1)}, bf16[2,512,512]{2,1,0:T(8,128)(2,1)}, u32[]{:S(2)}, u32[]{:S(2)}) %collective-permute-start.17) | collective-permute-done | bytes 1048608 | tf_op jit(solution)/shard_map/ppermute | solution.py:27
  247.3 11.4 collective-permute-done.18
  274.0 8.2 collective-permute-done.44
  283.5 22.5 %shard_map.169 = (bf16[1024,512]{1,0:T(8,128)(2,1)S(1)}, f32[4,2,1024]{2,1,0:T(2,128)S(1)}) custom-call(s32[4]{0:T(128)S(1)} %compare_select_fusion.8.start_ref, s32[4]{0:T(128)S(1)} %get-tuple-element.142.kind_ref, bf16[1024,1536]{1,0:T(8,128)(2,1)S(1)} %add_convert_fusion.1.query_ref.key_ref.value_ref, ...), custom_call_target="tpu_custom_call" | custom-call | flops 4294967296 | bytes 4194304 | tf_op jit(solution)/shard_map/pallas_call | solution.py:248
  328.3 10.3 collective-permute-done.50
  399.2 22.9 %shard_map.170 = (bf16[1024,512]{1,0:T(8,128)(2,1)S(1)}, f32[4,2,1024]{2,1,0:T(2,128)S(1)}) custom-call(s32[4]{0:T(128)S(1)} %compare_select_fusion.8.start_ref, s32[4]{0:T(128)S(1)} %get-tuple-element.142.kind_ref, bf16[1024,1536]{1,0:T(8,128)(2,1)S(1)} %add_convert_fusion.query_ref.key_ref.value_ref, ...), custom_call_target="tpu_custom_call" | custom-call | flops 4294967296 | bytes 4194304 | tf_op jit(solution)/shard_map/pallas_call | solution.py:248
  445.7 9.1 multiply_convert_fusion.2
  488.6 9.5 multiply_convert_fusion.1
  529.4 30.5 %shard_map.171 = (bf16[1024,1536]{1,0:T(8,128)(2,1)S(1)}, f32[4,2,128]{2,1,0:T(2,128)S(1)}) custom-call(s32[4]{0:T(128)S(1)} %compare_select_fusion.8.start_ref, s32[4]{0:T(128)S(1)} %get-tuple-element.142.kind_ref, bf16[1024,1536]{1,0:T(8,128)(2,1)} %copy-done.11, bf16[1024,1536]{1,0:T(8,128)(2,1)} %copy-done.11, bf16[1024,1536]{1,0:T(8,128)(2,1)} %copy-done.11, ...), custom_call_target="tpu_custom_call" | custom-call | flops 10737418240 | bytes 8388608 | tf_op jit(solution)/shard_map/pallas_call | solution.py:274
  595.8 9.5 multiply_convert_fusion
  629.2 36.2 %collective-permute-done.63 = bf16[4,512,512]{2,1,0:T(8,128)(2,1)S(1)} collective-permute-done((bf16[4,512,512]{2,1,0:T(8,128)(2,1)S(1)}, bf16[4,512,512]{2,1,0:T(8,128)(2,1)S(1)}, u32[]{:S(2)}, u32[]{:S(2)}) %collective-permute-start.63) | collective-permute-done | bytes 2097184 | tf_op jit(solution)/shard_map/ppermute | solution.py:27
  672.6 30.7 %shard_map.172 = (bf16[1024,1536]{1,0:T(8,128)(2,1)S(1)}, f32[4,2,128]{2,1,0:T(2,128)S(1)}) custom-call(s32[4]{0:T(128)S(1)} %compare_select_fusion.8.start_ref, s32[4]{0:T(128)S(1)} %get-tuple-element.142.kind_ref, bf16[1024,1536]{1,0:T(8,128)(2,1)} %copy-done.10, bf16[1024,1536]{1,0:T(8,128)(2,1)} %copy-done.10, bf16[1024,1536]{1,0:T(8,128)(2,1)} %copy-done.10, ...), custom_call_target="tpu_custom_call" | custom-call | flops 10737418240 | bytes 8388608 | tf_op jit(solution)/shard_map/pallas_call | solution.py:274
  712.9 21.8 %collective-permute-start.66 = (bf16[1024,1024]{0,1:T(8,128)(2,1)}, bf16[1024,1024]{0,1:T(8,128)(2,1)}, u32[]{:S(2)}, u32[]{:S(2)}) collective-permute-start(bf16[1024,1024]{0,1:T(8,128)(2,1)} %convolution_convert_fusion.11), channel_id=1, source_target_pairs={{0,4},{1,5},{2,6},{3,7},{4,0},{5,1},{6,2},{7,3},{8,12},{9,13},{10,... | collective-permute-start | bytes 6291464 | tf_op jit(solution)/shard_map/ppermute | solution.py:27
  767.9 10.6 all-to-all-done.4
  778.5 8.8 collective-permute-done.67
  815.1 16.2 %collective-permute-done.73 = bf16[4,512,512]{2,1,0:T(8,128)(2,1)} collective-permute-done((bf16[4,512,512]{2,1,0:T(8,128)(2,1)}, bf16[4,512,512]{2,1,0:T(8,128)(2,1)}, u32[]{:S(2)}, u32[]{:S(2)}) %collective-permute-start.73) | collective-permute-done | bytes 2097184 | tf_op jit(solution)/shard_map/ppermute | solution.py:27
  831.3 9.8 collective-permute-done.72
  874.4 26.3 %collective-permute-done.75 = bf16[4,512,512]{2,1,0:T(8,128)(2,1)S(1)} collective-permute-done((bf16[4,512,512]{2,1,0:T(8,128)(2,1)S(1)}, bf16[4,512,512]{2,1,0:T(8,128)(2,1)S(1)}, u32[]{:S(2)}, u32[]{:S(2)}) %collective-permute-start.75) | collective-permute-done | bytes 2097184 | tf_op jit(solution)/shard_map/ppermute | solution.py:27
  923.7 39.3 %collective-permute-done.76 = bf16[4,512,512]{2,1,0:T(8,128)(2,1)} collective-permute-done((bf16[4,512,512]{2,1,0:T(8,128)(2,1)S(1)}, bf16[4,512,512]{2,1,0:T(8,128)(2,1)}, u32[]{:S(2)}, u32[]{:S(2)}) %collective-permute-start.76) | collective-permute-done | bytes 2097184 | tf_op jit(solution)/shard_map/ppermute | solution.py:27
  986.4 9.5 collective-permute-start.68
  1000.0 115.6 %all-reduce.2.cloned.1.call-done = f32[2,12,1024]{2,0,1:T(2,128)} async-done(((f32[2,12,1024]{2,0,1:T(2,128)}), f32[2,12,1024]{2,0,1:T(2,128)}) %all-reduce.2.cloned.1.call-update) | async-done | bytes 98320 | tf_op jit(solution)/shard_map/psum | solution.py:662
  (660 shorter events, 616.5 us)
Async XLA Ops:
  85.3 90.3 %all-to-all-start = ((bf16[4,128,1024]{2,1,0:T(8,128)(2,1)}), bf16[4,128,1024]{2,1,0:T(8,128)(2,1)}, u32[]{:S(2)}, u32[]{:S(2)}) async-start(bf16[4,128,1024]{2,1,0:T(8,128)(2,1)} %select_select_fusion.1), calls=%async_computation | async-start | bytes 2097152 | tf_op jit(solution)/shard_map/all_to_all | solution.py:385
  102.1 88.5 %collective-permute-start.16 = (bf16[4,512,512]{2,1,0:T(8,128)(2,1)}, bf16[4,512,512]{2,1,0:T(8,128)(2,1)}, u32[]{:S(2)}, u32[]{:S(2)}) collective-permute-start(bf16[4,512,512]{2,1,0:T(8,128)(2,1)} %bitcast_dynamic-update-slice_fusion.8), channel_id=1, source_target_pairs={{0,8},{1,9},{2,10},{3,11},{4,12},{5,13},{6,14},{7,15},{8,0},{9,1},... | collective-permute-start | bytes 6291464 | tf_op jit(solution)/shard_map/ppermute | solution.py:27
  102.8 80.1 %collective-permute-start.15 = (bf16[4,512,512]{2,1,0:T(8,128)(2,1)}, bf16[4,512,512]{2,1,0:T(8,128)(2,1)S(1)}, u32[]{:S(2)}, u32[]{:S(2)}) collective-permute-start(bf16[4,512,512]{2,1,0:T(8,128)(2,1)} %bitcast_dynamic-update-slice_fusion.8), channel_id=1, source_target_pairs={{0,16},{1,17},{2,18},{3,19},{4,20},{5,21},{6,22},{7,23},{8,24},{9,... | collective-permute-start | bytes 6291464 | tf_op jit(solution)/shard_map/ppermute | solution.py:27
  173.4 138.9 %collective-permute-start.35 = (bf16[4,512,512]{2,1,0:T(8,128)(2,1)}, bf16[4,512,512]{2,1,0:T(8,128)(2,1)}, u32[]{:S(2)}, u32[]{:S(2)}) collective-permute-start(bf16[4,512,512]{2,1,0:T(8,128)(2,1)} %bitcast_dynamic-update-slice_fusion.4), channel_id=1, source_target_pairs={{0,8},{1,9},{2,10},{3,11},{4,12},{5,13},{6,14},{7,15},{8,0},{9,1},... | collective-permute-start | bytes 6291464 | tf_op jit(solution)/shard_map/ppermute | solution.py:27
  190.7 117.4 %collective-permute-start.34 = (bf16[4,512,512]{2,1,0:T(8,128)(2,1)}, bf16[4,512,512]{2,1,0:T(8,128)(2,1)}, u32[]{:S(2)}, u32[]{:S(2)}) collective-permute-start(bf16[4,512,512]{2,1,0:T(8,128)(2,1)} %bitcast_dynamic-update-slice_fusion.4), channel_id=1, source_target_pairs={{0,16},{1,17},{2,18},{3,19},{4,20},{5,21},{6,22},{7,23},{8,24},{9,... | collective-permute-start | bytes 6291464 | tf_op jit(solution)/shard_map/ppermute | solution.py:27
  193.9 64.8 %collective-permute-start.18 = (bf16[2,512,512]{2,1,0:T(8,128)(2,1)}, bf16[2,512,512]{2,1,0:T(8,128)(2,1)}, u32[]{:S(2)}, u32[]{:S(2)}) collective-permute-start(bf16[2,512,512]{2,1,0:T(8,128)(2,1)} %slice.450), channel_id=1, source_target_pairs={{0,16},{1,17},{2,18},{3,19},{4,20},{5,21},{6,22},{7,23},{8,24},{9,... | collective-permute-start | bytes 3145736 | tf_op jit(solution)/shard_map/ppermute | solution.py:27
  209.4 54.6 %collective-permute-start.45 = (bf16[4,256,512]{2,1,0:T(8,128)(2,1)}, bf16[4,256,512]{2,1,0:T(8,128)(2,1)}, u32[]{:S(2)}, u32[]{:S(2)}) collective-permute-start(bf16[4,256,512]{2,1,0:T(8,128)(2,1)} %bitcast_dynamic-update-slice_fusion.11), channel_id=1, source_target_pairs={{0,8},{1,9},{2,10},{3,11},{4,12},{5,13},{6,14},{7,15},{8,0},{9,1},... | collective-permute-start | bytes 3145736 | tf_op jit(solution)/shard_map/ppermute | solution.py:27
  244.7 66.1 %collective-permute-start.49 = (bf16[2,256,1024]{2,1,0:T(8,128)(2,1)}, bf16[2,256,1024]{2,1,0:T(8,128)(2,1)}, u32[]{:S(2)}, u32[]{:S(2)}) collective-permute-start(bf16[2,256,1024]{2,1,0:T(8,128)(2,1)} %pad_maximum_fusion.13), channel_id=1, source_target_pairs={{1,0},{2,1},{3,2},{5,4},{6,5},{7,6},{9,8},{10,9},{11,10},{13,12},{... | collective-permute-start | bytes 3145736 | tf_op jit(solution)/shard_map/ppermute | solution.py:27
  508.6 57.9 %all-to-all-start.2 = ((bf16[4,256,1024]{2,1,0:T(8,128)(2,1)}), bf16[4,256,1024]{2,1,0:T(8,128)(2,1)}, u32[]{:S(2)}, u32[]{:S(2)}) async-start(bf16[4,256,1024]{2,1,0:T(8,128)(2,1)} %bitcast.90), calls=%async_computation.2 | async-start | bytes 4194304 | tf_op jit(solution)/shard_map/all_to_all | solution.py:391
  581.2 123.8 %all-to-all-start.3 = ((bf16[4,512,1024]{2,1,0:T(8,128)(2,1)}), bf16[4,512,1024]{2,1,0:T(8,128)(2,1)}, u32[]{:S(2)}, u32[]{:S(2)}) async-start(bf16[4,512,1024]{2,1,0:T(8,128)(2,1)} %bitcast.273), calls=%async_computation.3 | async-start | bytes 8388608 | tf_op jit(solution)/shard_map/all_to_all | solution.py:467
  615.7 49.7 %collective-permute-start.63 = (bf16[4,512,512]{2,1,0:T(8,128)(2,1)S(1)}, bf16[4,512,512]{2,1,0:T(8,128)(2,1)S(1)}, u32[]{:S(2)}, u32[]{:S(2)}) collective-permute-start(bf16[4,512,512]{2,1,0:T(8,128)(2,1)S(1)} %fusion.26), channel_id=1, source_target_pairs={{0,16},{1,17},{2,18},{3,19},{4,20},{5,21},{6,22},{7,23},{8,24},{9,... | collective-permute-start | bytes 6291464 | tf_op jit(solution)/shard_map/ppermute | solution.py:27
  625.1 80.0 %collective-permute-start.65 = (bf16[4,512,512]{2,1,0:T(8,128)(2,1)S(1)}, bf16[4,512,512]{2,1,0:T(8,128)(2,1)}, u32[]{:S(2)}, u32[]{:S(2)}) collective-permute-start(bf16[4,512,512]{2,1,0:T(8,128)(2,1)S(1)} %pad_maximum_fusion.6), channel_id=1, source_target_pairs={{0,8},{1,9},{2,10},{3,11},{4,12},{5,13},{6,14},{7,15},{8,0},{9,1},... | collective-permute-start | bytes 6291464 | tf_op jit(solution)/shard_map/ppermute | solution.py:27
  712.9 50.2 %collective-permute-start.66 = (bf16[1024,1024]{0,1:T(8,128)(2,1)}, bf16[1024,1024]{0,1:T(8,128)(2,1)}, u32[]{:S(2)}, u32[]{:S(2)}) collective-permute-start(bf16[1024,1024]{0,1:T(8,128)(2,1)} %convolution_convert_fusion.11), channel_id=1, source_target_pairs={{0,4},{1,5},{2,6},{3,7},{4,0},{5,1},{6,2},{7,3},{8,12},{9,13},{10,... | collective-permute-start | bytes 6291464 | tf_op jit(solution)/shard_map/ppermute | solution.py:27
  759.2 72.1 %collective-permute-start.73 = (bf16[4,512,512]{2,1,0:T(8,128)(2,1)}, bf16[4,512,512]{2,1,0:T(8,128)(2,1)}, u32[]{:S(2)}, u32[]{:S(2)}) collective-permute-start(bf16[4,512,512]{2,1,0:T(8,128)(2,1)} %bitcast.106), channel_id=1, source_target_pairs={{0,8},{1,9},{2,10},{3,11},{4,12},{5,13},{6,14},{7,15},{8,0},{9,1},... | collective-permute-start | bytes 6291464 | tf_op jit(solution)/shard_map/ppermute | solution.py:27
  846.0 61.3 %all-to-all-start.8 = ((bf16[4,512,512]{2,1,0:T(8,128)(2,1)}), bf16[4,512,512]{2,1,0:T(8,128)(2,1)}, u32[]{:S(2)}, u32[]{:S(2)}) async-start(bf16[4,512,512]{2,1,0:T(8,128)(2,1)} %fusion.31), calls=%async_computation.8 | async-start | bytes 4194304 | tf_op jit(solution)/shard_map/all_to_all | solution.py:467
  865.1 58.6 %collective-permute-start.77 = (bf16[4,512,512]{2,1,0:T(8,128)(2,1)}, bf16[4,512,512]{2,1,0:T(8,128)(2,1)}, u32[]{:S(2)}, u32[]{:S(2)}) collective-permute-start(bf16[4,512,512]{2,1,0:T(8,128)(2,1)} %add_convert_fusion.6), channel_id=1, source_target_pairs={{0,16},{1,17},{2,18},{3,19},{4,20},{5,21},{6,22},{7,23},{8,24},{9,... | collective-permute-start | bytes 6291464 | tf_op jit(solution)/shard_map/ppermute | solution.py:27
  907.3 61.1 %all-to-all-start.7 = ((bf16[4,512,512]{2,1,0:T(8,128)(2,1)}), bf16[4,512,512]{2,1,0:T(8,128)(2,1)}, u32[]{:S(2)}, u32[]{:S(2)}) async-start(bf16[4,512,512]{2,1,0:T(8,128)(2,1)} %add_convert_fusion.4), calls=%async_computation.7 | async-start | bytes 4194304 | tf_op jit(solution)/shard_map/all_to_all | solution.py:467
  968.4 170.5 %all-to-all-start.6 = ((bf16[4,512,512]{2,1,0:T(8,128)(2,1)}), bf16[4,512,512]{2,1,0:T(8,128)(2,1)S(1)}, u32[]{:S(2)}, u32[]{:S(2)}) async-start(bf16[4,512,512]{2,1,0:T(8,128)(2,1)} %fusion.30), calls=%async_computation.6 | async-start | bytes 4194304 | tf_op jit(solution)/shard_map/all_to_all | solution.py:467
  973.3 142.2 %all-reduce.2.cloned.1.call-start = ((), (), s32[]{:S(2)}) async-start(), calls=%async_computation.9 | async-start | bytes 196608 | tf_op jit(solution)/shard_map/psum | solution.py:662
  979.2 137.7 %collective-permute-start.79 = (bf16[512,512]{1,0:T(8,128)(2,1)S(1)}, bf16[512,512]{1,0:T(8,128)(2,1)S(1)}, u32[]{:S(2)}, u32[]{:S(2)}) collective-permute-start(bf16[512,512]{1,0:T(8,128)(2,1)S(1)} %split.121), channel_id=1, source_target_pairs={{0,8},{1,9},{2,10},{3,11},{4,12},{5,13},{6,14},{7,15},{8,0},{9,1},... | collective-permute-start | bytes 1572872 | tf_op jit(solution)/shard_map/ppermute | solution.py:27
  980.4 144.3 %collective-permute-start.71 = (bf16[4,128,1024]{2,1,0:T(8,128)(2,1)}, bf16[4,128,1024]{2,1,0:T(8,128)(2,1)}, u32[]{:S(2)}, u32[]{:S(2)}) collective-permute-start(bf16[4,128,1024]{2,1,0:T(8,128)(2,1)} %copy-done.84), channel_id=1, source_target_pairs={{4,16},{5,17},{6,18},{7,19},{12,24},{13,25},{14,26},{15,27},{20,20... | collective-permute-start | bytes 3145736 | tf_op jit(solution)/shard_map/ppermute | solution.py:27
  982.8 144.7 %collective-permute-start.70 = (bf16[4,128,1024]{2,1,0:T(8,128)(2,1)}, bf16[4,128,1024]{2,1,0:T(8,128)(2,1)}, u32[]{:S(2)}, u32[]{:S(2)}) collective-permute-start(bf16[4,128,1024]{2,1,0:T(8,128)(2,1)} %copy-done.84), channel_id=1, source_target_pairs={{0,16},{1,17},{2,18},{3,19},{8,24},{9,25},{10,26},{11,27},{16,20},... | collective-permute-start | bytes 3145736 | tf_op jit(solution)/shard_map/ppermute | solution.py:27
  985.2 142.4 %collective-permute-start.69 = (bf16[4,128,1024]{2,1,0:T(8,128)(2,1)}, bf16[4,128,1024]{2,1,0:T(8,128)(2,1)}, u32[]{:S(2)}, u32[]{:S(2)}) collective-permute-start(bf16[4,128,1024]{2,1,0:T(8,128)(2,1)} %all-to-all-done.5), channel_id=1, source_target_pairs={{4,0},{5,1},{6,2},{7,3},{12,8},{13,9},{14,10},{15,11},{20,4},{21,5... | collective-permute-start | bytes 3145736 | tf_op jit(solution)/shard_map/ppermute | solution.py:27
  986.4 141.1 %collective-permute-start.68 = (bf16[4,128,1024]{2,1,0:T(8,128)(2,1)}, bf16[4,128,1024]{2,1,0:T(8,128)(2,1)}, u32[]{:S(2)}, u32[]{:S(2)}) collective-permute-start(bf16[4,128,1024]{2,1,0:T(8,128)(2,1)} %all-to-all-done.5), channel_id=1, source_target_pairs={{0,0},{1,1},{2,2},{3,3},{8,8},{9,9},{10,10},{11,11},{16,4},{17,5},... | collective-permute-start | bytes 3145736 | tf_op jit(solution)/shard_map/ppermute | solution.py:27
  (185 other events, 2929.5 us)
Sparse Core Ops, SparseCore 0:
  983.0 132.5 all-reduce.1

commit v5 on v4

--- a/solution.py
+++ b/solution.py
@@ -107,11 +107,9 @@
     return jnp.sum((positions[:, None] >= seq_ends[None, :]).astype(jnp.int32), axis=1)
 
 
-def flash_params(flops, transcendentals, moved):
+def flash_params():
     return dict(
-        cost_estimate=pl.CostEstimate(
-            flops=flops, transcendentals=transcendentals, bytes_accessed=moved
-        ),
+        cost_estimate=pl.CostEstimate(flops=0, transcendentals=0, bytes_accessed=0),
         compiler_params=pltpu.CompilerParams(vmem_limit_bytes=48 * 1024 * 1024),
     )
 
@@ -243,7 +241,6 @@
     pairs = packed.shape[1] // (3 * lanes)
     heads = lanes // HEAD_DIM
     size = min(256, rows)
-    squares = pairs * heads * rows * rows
     start, kind, widths = key_windows(seq_lens, rows, size)
     return pl.pallas_call(
         functools.partial(forward_kernel, widths),
@@ -260,7 +257,7 @@
             jax.ShapeDtypeStruct((rows, pairs * lanes), LOW),
             jax.ShapeDtypeStruct((pairs, heads, rows), WIDE),
         ],
-        **flash_params(8 * squares * HEAD_DIM, squares, 4 * rows * pairs * lanes * 2),
+        **flash_params(),
     )(start, kind, packed, packed, packed, segments[:, None], segments[None, :])
 
 
@@ -269,7 +266,6 @@
     pairs = packed.shape[1] // (3 * lanes)
     heads = lanes // HEAD_DIM
     size = min(256, rows)
-    squares = pairs * heads * rows * rows
     start, kind, widths = key_windows(seq_lens, rows, size)
     return pl.pallas_call(
         functools.partial(backward_kernel, widths),
@@ -291,7 +287,7 @@
             jax.ShapeDtypeStruct((rows, pairs * 3 * lanes), LOW),
             jax.ShapeDtypeStruct((pairs, 2, lanes), WIDE),
         ],
-        **flash_params(20 * squares * HEAD_DIM, squares, 8 * rows * pairs * lanes * 2),
+        **flash_params(),
     )(start, kind, packed, packed, packed, segments[:, None], segments[None, :], logsums, context_grad)
 
 
@@ -304,8 +300,8 @@
     return jnp.swapaxes(shaped, 2, 3).reshape(packed.shape)
 
 
-def layer_forward(rows, segments, seq_lens, weights, small):
-    w_qkv, w_out, w_in, w_back = weights
+def layer_forward(rows, segments, seq_lens, weights, small, late_weights=None):
+    w_qkv, w_out, w_in = weights[:3]
     gains, biases, offset, inner_bias, head_half = small
     lanes = max(head_half, 128)
     packed = (rhs_inner(rows, w_qkv) + offset).astype(LOW)
@@ -315,9 +311,15 @@
     middle = (norm_parts(first_sum)[0] * gains[0] + biases[3]).astype(LOW)
     active, slope = gelu_pair(rhs_inner(middle, w_in) + inner_bias)
     active, slope = active.astype(LOW), slope.astype(LOW)
+    if late_weights is None:
+        w_back = weights[3]
+    else:
+        active, late = late_weights(active)
+        w_back = late[0]
     second_sum = middle.astype(WIDE) + core_sum(matmul(active, w_back)) + biases[4]
     result = norm_parts(second_sum)[0] * gains[1] + biases[5]
-    return result, (rows, packed, logsums, context, first_sum, middle, active, slope, second_sum)
+    saved = (rows, packed, logsums, context, first_sum, middle, active, slope, second_sum)
+    return result, saved, late if late_weights is not None else None
 
 
 def slab_grads(hidden, features, chips):
@@ -416,11 +418,12 @@
         given = choose(core, (halves[1], halves[0]))
         return by_core(core, kept, to_other_core(given), 1)
 
-    def over_ranks(own):
-        upward, downward = [own], [own]
-        for _ in range(1, ranks):
-            upward.append(move(upward[-1], lambda s, d, t: (s, d, t + 1) if t + 1 < ranks else None))
-            downward.append(move(downward[-1], lambda s, d, t: (s, d, t - 1) if t > 0 else None))
+    def relay(upward, downward):
+        upward.append(move(upward[-1], lambda s, d, t: (s, d, t + 1) if t + 1 < ranks else None))
+        downward.append(move(downward[-1], lambda s, d, t: (s, d, t - 1) if t > 0 else None))
+
+    def assemble(upward, downward):
+        own = upward[0]
         item = jnp.zeros((ranks,) + own.shape, LOW)
         item = lax.dynamic_update_index_in_dim(item, own, rank, 0)
         for j in range(1, ranks):
@@ -428,10 +431,19 @@
             item = lax.dynamic_update_index_in_dim(item, arrived, (rank + ranks - j) % ranks, 0)
         return item
 
-    def over_chips(item):
-        part = item.shape[0] // 2
+    def over_ranks(own):
+        upward, downward = [own], [own]
+        for _ in range(1, ranks):
+            relay(upward, downward)
+        return assemble(upward, downward)
+
+    def chips_once(item):
         across = move(item, lambda s, d, t: (1 - s, d, t))
         along = [move(item, lambda s, d, t: (s, d ^ (2 * k), t)) for k in range(1, chips)]
+        return across, along
+
+    def chips_twice(item, across, along):
+        part = item.shape[0] // 2
         far = []
         for k in range(1, chips):
             upper = move(across[:part], lambda s, d, t: (s, d ^ (2 * k), t))
@@ -444,12 +456,8 @@
             result.append(jnp.concatenate(slabs, axis=-1))
         return result
 
-    def gather_weight(own):
-        return over_chips(over_ranks(own))
-
-    def gather_weight_late(own):
-        both = over_ranks(jnp.stack(over_chips(own)))
-        return [both[:, layer] for layer in range(2)]
+    def over_chips(item):
+        return chips_twice(item, *chips_once(item))
 
     def from_x(slabs):
         return [move(slabs[k], lambda s, d, t: (s, d ^ (2 * k), t)) for k in range(1, chips)]
@@ -495,27 +503,44 @@
     back_two = jnp.stack(over_chips(back_own[later:]))
     attention_item = over_ranks(attention_own)
     attention_item, back_two = tie(attention_item, back_two)
-    attention_all = over_chips(attention_item)
+    across, along = chips_once(attention_item)
     rows = fetch_rows(block_input, attention_item)
-    in_item = over_ranks(after(in_own, attention_item))
+    in_own = after(in_own, attention_item)
+    upward, downward = [in_own], [in_own]
+    for at in range(1, ranks):
+        relay(upward, downward)
+        if at == ranks // 2:
+            upward[-1], downward[-1], across, *along = tie(upward[-1], downward[-1], across, *along)
+            attention_all = chips_twice(attention_item, across, along)
+    upward[-1], downward[-1], gains, seq_lengths = tie(upward[-1], downward[-1], gains, seq_lengths)
+    in_item = assemble(upward, downward)
     in_all = over_chips(in_item)
     back_item = over_ranks(after(back_own[:later], in_item))
-    back_one = over_chips(back_item)
-    back_two = over_ranks(after(back_two, back_item))
-    back_all = [jnp.concatenate([back_one[at], back_two[:, at]], axis=1) for at in range(2)]
+    across, along = chips_once(back_item)
+    back_two = after(back_two, back_item)
+    upward, downward = [back_two], [back_two]
+    for _ in range(1, ranks):
+        relay(upward, downward)
+
+    def late_weights(active):
+        tied = tie(active, across, upward[-1], downward[-1], *along)
+        halves = zip(
+            chips_twice(back_item, tied[1], list(tied[4:])),
+            jnp.moveaxis(assemble(upward[:-1] + [tied[2]], downward[:-1] + [tied[3]]), 1, 0),
+        )
+        return tied[0], [jnp.concatenate(pair, axis=1).reshape(-1, width) for pair in halves]
+
     weights = [
         (
             attention_all[layer][:, : 3 * head_half].reshape(-1, width),
             attention_all[layer][:, 3 * head_half :].reshape(-1, width),
             in_all[layer].reshape(-1, width),
-            back_all[layer].reshape(-1, width),
         )
         for layer in range(2)
     ]
 
     gain_count, bias_count = gains.shape[1], biases.shape[1]
     packed_small = jnp.concatenate([gains, biases, ffn_bias.reshape(1, -1, local)], axis=1)
-    packed_small, seq_lengths = tie(packed_small, seq_lengths, attention_item)[:2]
     table_parts = [
         [
             packed_small
@@ -553,11 +578,12 @@
     segments = segment_ids(lengths, ranks * own_rows)
     live = (segments < lengths.shape[0])[:, None]
 
-    first_out, first_saved = layer_forward(rows, segments, lengths, weights[0], small[0])
+    first_out, first_saved, late = layer_forward(rows, segments, lengths, weights[0], small[0], late_weights)
+    weights = [weights[layer] + (late[layer],) for layer in range(2)]
     first_low = first_out.astype(LOW)
     cotangent = fetch_rows(out_grad, back_two)
     cotangent = jnp.where(live, cotangent, jnp.zeros((), LOW))
-    second_out, second_saved = layer_forward(first_low, segments, lengths, weights[1], small[1])
+    second_out, second_saved, _ = layer_forward(first_low, segments, lengths, weights[1], small[1])
     spread = spread_both(first_low, second_out.astype(LOW))
 
     def hidden_grads(hidden, features):
@@ -573,8 +599,8 @@
     )
     back_slabs = hidden_grads(second_saved[6], branch_grad)
     back_here = from_x(back_slabs)
-    inner = counted_only([lhs_inner(hidden_low, second_saved[5]).astype(LOW)])[0]
-    in_here = from_z(ranked(inner))
+    in_slabs = hidden_grads(hidden_low, second_saved[5])
+    in_here = from_x(in_slabs)
     first_grad, attended_grad, packed_low, more_sums = backward_attention(
         second_saved, segments, lengths, middle_grad, weights[1], small[1]
     )
@@ -584,63 +610,60 @@
     back_sent = from_section(back_two, 1)
     placed = place_both(spread)
     second_in = first_grad + core_sum(matmul(packed_low, weights[1][0]))
-    attention_slabs = attention_grads(second_saved, attended_grad, packed_low)
-    attention_here = from_x(attention_slabs)
+    qkv, out = [
+        ranked(counted_only([lhs_inner(hidden, features).astype(LOW)])[0])
+        for hidden, features in ((packed_low, second_saved[0]), (second_saved[3], attended_grad))
+    ]
+    attention_here = from_z(jnp.concatenate([qkv, out], axis=1))
     second_low = second_in.astype(LOW)
 
     middle_grad, branch_grad, hidden_low, first_sums = backward_hidden(
         first_saved, second_low, weights[0], small[0]
     )
-    middle_grad, back_sent, placed = tie(middle_grad, back_sent, placed)
+    middle_grad, back_sent, placed, *in_here = tie(middle_grad, back_sent, placed, *in_here)
     back_two = add(back_two, [back_sent])
+    in_two = add(in_slabs[0], in_here)
+    in_sent = from_section(in_two, 1)
     outputs = placed.astype(WIDE)[None]
     second_in_spread = spread_rows(second_low)
     back_slabs = hidden_grads(first_saved[6], branch_grad)
     back_here = from_x(back_slabs)
     in_slabs = hidden_grads(hidden_low, first_saved[5])
-    in_one_here = from_x(in_slabs)
+    in_here = from_x(in_slabs)
     first_grad, attended_grad, packed_low, more_sums = backward_attention(
         first_saved, segments, lengths, middle_grad, weights[0], small[0]
     )
     first_sums += more_sums
-    packed_low, in_here, *attention_here = tie(packed_low, in_here, *attention_here)
-    attention_two = add(attention_slabs[0], attention_here)
-    attention_sent = from_section(attention_two, 1)
-    in_two_slabs = jnp.split(add_ranks(in_here), chips, axis=-1)
-    in_two_here = from_x(in_two_slabs)
+    packed_low, in_sent, second_in_spread, *back_here = tie(packed_low, in_sent, second_in_spread, *back_here)
+    in_two = add(in_two, [in_sent])
+    back_one = add(back_slabs[0], back_here)
+    back_sent = from_section(back_one, 0)
+    second_placed = place_rows(second_in_spread, 1)
     first_in = first_grad + core_sum(matmul(packed_low, weights[0][0]))
     attention_slabs = attention_grads(first_saved, attended_grad, packed_low)
-    attention_here = from_x(attention_slabs)
-    first_in, second_in_spread, *back_here = tie(first_in, second_in_spread, *back_here)
-    back_one = add(back_slabs[0], back_here)
-    back_sent = from_section(back_one, 0)
+    attention_one_here = from_x(attention_slabs)
+    first_in, attention_here, *in_here = tie(first_in, attention_here, *in_here)
     first_in_spread = spread_rows(first_in.astype(LOW))
-    second_placed = place_rows(second_in_spread, 1)
-
-    back_sent, *in_one_here = tie(back_sent, *in_one_here)
-    in_one = add(in_slabs[0], in_one_here)
-    in_one_sent = from_section(in_one, 0)
+    in_one = add(in_slabs[0], in_here)
+    in_sent = from_section(in_one, 0)
+    attention_two_slabs = jnp.split(add_ranks(attention_here), chips, axis=-1)
+    attention_two_here = from_x(attention_two_slabs)
+
+    back_sent, *attention_one_here = tie(back_sent, *attention_one_here)
     back_here = from_z(by_section(add(back_one, [back_sent]), back_two))
-    in_two = add(in_two_slabs[0], in_two_here)
-    in_two_sent = from_section(in_two, 1)
-    attention_two = add(attention_two, [attention_sent])
-    in_one_sent, *attention_here = tie(in_one_sent, *attention_here)
-    attention_one = add(attention_slabs[0], attention_here)
+    attention_one = add(attention_slabs[0], attention_one_here)
     attention_one_sent = from_section(attention_one, 0)
-    in_one_here = from_z(add(in_one, [in_one_sent]))
-    in_two = add(in_two, [in_two_sent])
+    attention_two = add(attention_two_slabs[0], attention_two_here)
+    attention_two_sent = from_section(attention_two, 1)
+    in_here = from_z(by_section(add(in_one, [in_sent]), in_two))
+    first_placed = place_rows(first_in_spread, 0)
+    attention_one_sent, attention_two_sent, back_here = tie(attention_one_sent, attention_two_sent, back_here)
+    attention_one = add(attention_one, [attention_one_sent])
+    attention_two = add(attention_two, [attention_two_sent])
     back_shard = finish(add_ranks(back_here))
-    first_placed = place_rows(first_in_spread, 0)
-    attention_one = add(attention_one, [attention_one_sent])
-    attention_here = from_z(by_section(attention_one, attention_two))
     input_grads = by_section(first_placed, second_placed).astype(WIDE)[None]
-    in_shard = finish(by_section(add_ranks(in_one_here), in_two))
-    attention_shard = finish(add_ranks(attention_here))
-    qkv_shard, out_shard = attention_shard[:, : 3 * head_half], attention_shard[:, 3 * head_half :]
-    qkv_grad = jnp.transpose(qkv_shard.reshape(2, 3, head_half, local), (3, 1, 0, 2)).reshape(local, 3, -1)
-    out_grad_w = out_shard.reshape(-1, local)
-    in_grad = jnp.transpose(in_shard.reshape(-1, local))
-    back_grad = back_shard.reshape(-1, local)
+    attention_here = from_z(attention_one)
+    in_shard = finish(add_ranks(in_here))
 
     def spread_columns(row):
         blocks = row.reshape(ranks, 1, -1)
@@ -659,7 +682,15 @@
         )
     table = jnp.stack(tables)
     table = jnp.where(counted, table, 0.0) if repeats > 1 else table
-    table = lax.dynamic_index_in_dim(lax.psum(table, AXES), section, 0, keepdims=False)
+    table = lax.psum(table, AXES)
+    attention_here, table = tie(attention_here, table)
+    attention_shard = finish(by_section(add_ranks(attention_here), attention_two))
+    qkv_shard, out_shard = attention_shard[:, : 3 * head_half], attention_shard[:, 3 * head_half :]
+    qkv_grad = jnp.transpose(qkv_shard.reshape(2, 3, head_half, local), (3, 1, 0, 2)).reshape(local, 3, -1)
+    out_grad_w = out_shard.reshape(-1, local)
+    in_grad = jnp.transpose(in_shard.reshape(-1, local))
+    back_grad = back_shard.reshape(-1, local)
+    table = choose(section, (table[0], table[1]))
     sliced = lax.dynamic_slice_in_dim(table[: gain_count + bias_count], copy_at * local, local, 1)
     inner = lax.dynamic_index_in_dim(
         table[gain_count + bias_count :].reshape(copies, -1), copy_at, 0, keepdims=False

time: 1170 us -> 1140 us (0.974)
  local copies, waits for them, and re-layouts: 86 us -> 74.1 us
    ppermute x83, waiting for transfers between devices: 274 us -> 291 us  [move(): return lax.ppermute(value, AXES, pairs)]
    psum x1, waiting for transfers between devices: 116 us -> 101 us  [on_device(): table = lax.psum(table, AXES)]
    dot_general x15 -> x14, matrix products: 50.1 us -> 41.9 us  [lhs_inner(): lax.dot_general(lhs_mat, rhs_mat, (((0,), (0,)), ((), ())), preferred_ele...]
    unnamed x244 -> x258, local copies, waits for them, and re-layouts: 35.5 us -> 36.3 us
  transfers between devices with their start and end apart: 93 -> 93, of which waited for: 32 -> 38; matrix products, arithmetic and copies ran while one was open for 27% -> 26% of each run, Pallas kernels for 7% -> 7%
where the time goes in v5:
time: 1140 us; the launch traced here: 1130 us
  waiting for transfers between devices  404 us (35%)
  starting transfers between devices  224 us (20%)
  other arithmetic  174 us (15%)
  matrix products  133 us (12%)
  Pallas kernels  102 us (9%)
  local copies, waits for them, and re-layouts  74.1 us (6%)
  between operations  17.1 us (2%)
    ppermute x83, waiting for transfers between devices, move(): return lax.ppermute(value, AXES, pairs)  291 us
    ppermute x83, starting transfers between devices, move(): return lax.ppermute(value, AXES, pairs)  180 us
    psum x1, waiting for transfers between devices, on_device(): table = lax.psum(table, AXES)  101 us
    pallas_call x2, Pallas kernels, attend_backward(): pl.pallas_call(functools.partial(backward_kernel, widths), grid_spec=pltp...  58.7 us
    dot_general x10, matrix products, matmul(): return jnp.dot(lhs_mat, rhs_mat, preferred_element_type=WIDE)  46.6 us
    dot_general x8, matrix products, rhs_inner(): lax.dot_general(lhs_mat, rhs_mat, (((1,), (1,)), ((), ())), preferred_ele...  44.2 us
    pallas_call x2, Pallas kernels, attend_forward(): pl.pallas_call(functools.partial(forward_kernel, widths), grid_spec=pltpu...  43.5 us
    dot_general x14, matrix products, lhs_inner(): lax.dot_general(lhs_mat, rhs_mat, (((0,), (0,)), ((), ())), preferred_ele...  41.9 us
  transfers between devices with their start and end apart: 93, of which 38 were waited for; matrix products, arithmetic and copies ran while one was open for 26% of the time, Pallas kernels for 7%

profile of v5, /device:TPU:0, one launch (start us, length us, event | category | flops | bytes accessed | tf_op | source)
XLA Modules:
  0.0 1127.1 jit_solution(8310732321901102711)
XLA Ops:
  92.7 19.2 %collective-permute-done.17 = bf16[512,512]{1,0:T(8,128)(2,1)} collective-permute-done((bf16[512,512]{1,0:T(8,128)(2,1)S(1)}, bf16[512,512]{1,0:T(8,128)(2,1)}, u32[]{:S(2)}, u32[]{:S(2)}) %collective-permute-start.17) | collective-permute-done | bytes 524320 | tf_op jit(solution)/shard_map/ppermute | solution.py:27
  113.2 10.5 collective-permute-start.16
  123.8 8.6 collective-permute-done.18
  191.2 11.8 %collective-permute-done.24 = bf16[2,512,512]{2,1,0:T(8,128)(2,1)} collective-permute-done((bf16[2,512,512]{2,1,0:T(8,128)(2,1)}, bf16[2,512,512]{2,1,0:T(8,128)(2,1)}, u32[]{:S(2)}, u32[]{:S(2)}) %collective-permute-start.24) | collective-permute-done | bytes 1048608 | tf_op jit(solution)/shard_map/ppermute | solution.py:27
  218.2 21.7 %shard_map.169 = (bf16[1024,512]{1,0:T(8,128)(2,1)S(1)}, f32[4,2,1024]{2,1,0:T(2,128)S(1)}) custom-call(s32[4]{0:T(128)S(1)} %compare_select_fusion.8.start_ref, s32[4]{0:T(128)S(1)} %get-tuple-element.174.kind_ref, bf16[1024,1536]{1,0:T(8,128)(2,1)S(1)} %add_convert_fusion.1.query_ref.key_ref.value_ref, ...), custom_call_target="tpu_custom_call" | custom-call | tf_op jit(solution)/shard_map/pallas_call | solution.py:245
  264.9 19.4 %collective-permute-done.48 = bf16[2,256,1024]{2,1,0:T(8,128)(2,1)} collective-permute-done((bf16[2,256,1024]{2,1,0:T(8,128)(2,1)S(1)}, bf16[2,256,1024]{2,1,0:T(8,128)(2,1)}, u32[]{:S(2)}, u32[]{:S(2)}) %collective-permute-start.48) | collective-permute-done | bytes 1048608 | tf_op jit(solution)/shard_map/ppermute | solution.py:27
  315.4 16.5 %collective-permute-done.36 = bf16[2,512,512]{2,1,0:T(8,128)(2,1)S(1)} collective-permute-done((bf16[2,512,512]{2,1,0:T(8,128)(2,1)S(1)}, bf16[2,512,512]{2,1,0:T(8,128)(2,1)S(1)}, u32[]{:S(2)}, u32[]{:S(2)}) %collective-permute-start.36) | collective-permute-done | bytes 1048608 | tf_op jit(solution)/shard_map/ppermute | solution.py:27
  339.8 7.7 multiply_convert_fusion.3
  347.5 8.5 collective-permute-done.47
  395.4 21.8 %shard_map.170 = (bf16[1024,512]{1,0:T(8,128)(2,1)S(1)}, f32[4,2,1024]{2,1,0:T(2,128)S(1)}) custom-call(s32[4]{0:T(128)S(1)} %compare_select_fusion.8.start_ref, s32[4]{0:T(128)S(1)} %get-tuple-element.174.kind_ref, bf16[1024,1536]{1,0:T(8,128)(2,1)S(1)} %add_convert_fusion.query_ref.key_ref.value_ref, ...), custom_call_target="tpu_custom_call" | custom-call | tf_op jit(solution)/shard_map/pallas_call | solution.py:245
  443.3 7.5 multiply_convert_fusion.2
  486.0 9.5 multiply_convert_fusion.1
  527.1 29.6 %shard_map.171 = (bf16[1024,1536]{1,0:T(8,128)(2,1)S(1)}, f32[4,2,128]{2,1,0:T(2,128)S(1)}) custom-call(s32[4]{0:T(128)S(1)} %compare_select_fusion.8.start_ref, s32[4]{0:T(128)S(1)} %get-tuple-element.174.kind_ref, bf16[1024,1536]{1,0:T(8,128)(2,1)} %copy-done.1, bf16[1024,1536]{1,0:T(8,128)(2,1)} %copy-done.1, bf16[1024,1536]{1,0:T(8,128)(2,1)} %copy-done.1, ...), custom_call_target="tpu_custom_call" | custom-call | tf_op jit(solution)/shard_map/pallas_call | solution.py:270
  591.0 17.1 %collective-permute-start.64 = (bf16[4,256,1024]{2,1,0:T(8,128)(2,1)}, bf16[4,256,1024]{2,1,0:T(8,128)(2,1)}, u32[]{:S(2)}, u32[]{:S(2)}) collective-permute-start(bf16[4,256,1024]{2,1,0:T(8,128)(2,1)} %all-to-all-done.2), channel_id=1, source_target_pairs={{0,0},{1,1},{2,2},{3,3},{4,16},{5,17},{6,18},{7,19},{8,8},{9,9},{1... | collective-permute-start | bytes 6291464 | tf_op jit(solution)/shard_map/ppermute | solution.py:27
  614.1 9.4 multiply_convert_fusion
  662.9 11.1 all-to-all-done.3
  694.1 29.2 %shard_map.172 = (bf16[1024,1536]{1,0:T(8,128)(2,1)S(1)}, f32[4,2,128]{2,1,0:T(2,128)S(1)}) custom-call(s32[4]{0:T(128)S(1)} %compare_select_fusion.8.start_ref, s32[4]{0:T(128)S(1)} %get-tuple-element.174.kind_ref, bf16[1024,1536]{1,0:T(8,128)(2,1)} %copy-done, bf16[1024,1536]{1,0:T(8,128)(2,1)} %copy-done, bf16[1024,1536]{1,0:T(8,128)(2,1)} %copy-done, ...), custom_call_target="tpu_custom_call" | custom-call | tf_op jit(solution)/shard_map/pallas_call | solution.py:270
  753.2 33.6 %collective-permute-done.69 = bf16[4,512,512]{2,1,0:T(8,128)(2,1)} collective-permute-done((bf16[4,512,512]{2,1,0:T(8,128)(2,1)S(1)}, bf16[4,512,512]{2,1,0:T(8,128)(2,1)}, u32[]{:S(2)}, u32[]{:S(2)}) %collective-permute-start.69) | collective-permute-done | bytes 2097184 | tf_op jit(solution)/shard_map/ppermute | solution.py:27
  797.3 34.1 %collective-permute-done.75 = bf16[4,512,512]{2,1,0:T(8,128)(2,1)} collective-permute-done((bf16[4,512,512]{2,1,0:T(8,128)(2,1)}, bf16[4,512,512]{2,1,0:T(8,128)(2,1)}, u32[]{:S(2)}, u32[]{:S(2)}) %collective-permute-start.75) | collective-permute-done | bytes 2097184 | tf_op jit(solution)/shard_map/ppermute | solution.py:27
  852.1 46.1 %collective-permute-done.80 = bf16[4,512,512]{2,1,0:T(8,128)(2,1)S(1)} collective-permute-done((bf16[4,512,512]{2,1,0:T(8,128)(2,1)S(1)}, bf16[4,512,512]{2,1,0:T(8,128)(2,1)S(1)}, u32[]{:S(2)}, u32[]{:S(2)}) %collective-permute-start.80) | collective-permute-done | bytes 2097184 | tf_op jit(solution)/shard_map/ppermute | solution.py:27
  923.3 11.3 %collective-permute-done.77 = bf16[512,512]{1,0:T(8,128)(2,1)} collective-permute-done((bf16[512,512]{1,0:T(8,128)(2,1)}, bf16[512,512]{1,0:T(8,128)(2,1)}, u32[]{:S(2)}, u32[]{:S(2)}) %collective-permute-start.77) | collective-permute-done | bytes 524320 | tf_op jit(solution)/shard_map/ppermute | solution.py:27
  951.0 10.3 collective-permute-done.76
  974.9 9.5 collective-permute-start.70
  1012.0 100.8 %all-reduce.2.cloned.1.call-done = f32[2,12,1024]{2,0,1:T(2,128)} async-done(((f32[2,12,1024]{2,0,1:T(2,128)}), f32[2,12,1024]{2,0,1:T(2,128)}) %all-reduce.2.cloned.1.call-update) | async-done | bytes 98320 | tf_op jit(solution)/shard_map/psum | solution.py:685
  (677 shorter events, 605.2 us)
Async XLA Ops:
  22.7 51.8 %collective-permute-start = (bf16[4,128,1024]{2,1,0:T(8,128)(2,1)}, bf16[4,128,1024]{2,1,0:T(8,128)(2,1)}, u32[]{:S(2)}, u32[]{:S(2)}) collective-permute-start(bf16[4,128,1024]{2,1,0:T(8,128)(2,1)} %broadcast_select_fusion.18), channel_id=1, source_target_pairs={{0,4},{1,5},{2,6},{3,7},{8,12},{9,13},{10,14},{11,15},{20,16},{21,... | collective-permute-start | bytes 3145736 | tf_op jit(solution)/shard_map/ppermute | solution.py:27
  67.8 65.8 %collective-permute-start.20 = (bf16[4,512,512]{2,1,0:T(8,128)(2,1)S(1)}, bf16[4,512,512]{2,1,0:T(8,128)(2,1)}, u32[]{:S(2)}, u32[]{:S(2)}) collective-permute-start(bf16[4,512,512]{2,1,0:T(8,128)(2,1)S(1)} %bitcast_dynamic-update-slice_fusion.8), channel_id=1, source_target_pairs={{0,8},{1,9},{2,10},{3,11},{4,12},{5,13},{6,14},{7,15},{8,0},{9,1},... | collective-permute-start | bytes 6291464 | tf_op jit(solution)/shard_map/ppermute | solution.py:27
  69.3 64.2 %collective-permute-start.19 = (bf16[4,512,512]{2,1,0:T(8,128)(2,1)S(1)}, bf16[4,512,512]{2,1,0:T(8,128)(2,1)}, u32[]{:S(2)}, u32[]{:S(2)}) collective-permute-start(bf16[4,512,512]{2,1,0:T(8,128)(2,1)S(1)} %bitcast_dynamic-update-slice_fusion.8), channel_id=1, source_target_pairs={{0,16},{1,17},{2,18},{3,19},{4,20},{5,21},{6,22},{7,23},{8,24},{9,... | collective-permute-start | bytes 6291464 | tf_op jit(solution)/shard_map/ppermute | solution.py:27
  145.8 62.0 %collective-permute-start.25 = (bf16[2,512,512]{2,1,0:T(8,128)(2,1)}, bf16[2,512,512]{2,1,0:T(8,128)(2,1)}, u32[]{:S(2)}, u32[]{:S(2)}) collective-permute-start(bf16[2,512,512]{2,1,0:T(8,128)(2,1)} %slice.350), channel_id=1, source_target_pairs={{0,16},{1,17},{2,18},{3,19},{4,20},{5,21},{6,22},{7,23},{8,24},{9,... | collective-permute-start | bytes 3145736 | tf_op jit(solution)/shard_map/ppermute | solution.py:27
  184.6 103.5 %collective-permute-start.35 = (bf16[4,512,512]{2,1,0:T(8,128)(2,1)}, bf16[4,512,512]{2,1,0:T(8,128)(2,1)}, u32[]{:S(2)}, u32[]{:S(2)}) collective-permute-start(bf16[4,512,512]{2,1,0:T(8,128)(2,1)} %bitcast_dynamic-update-slice_fusion.4), channel_id=1, source_target_pairs={{0,8},{1,9},{2,10},{3,11},{4,12},{5,13},{6,14},{7,15},{8,0},{9,1},... | collective-permute-start | bytes 6291464 | tf_op jit(solution)/shard_map/ppermute | solution.py:27
  188.7 105.3 %collective-permute-start.34 = (bf16[4,512,512]{2,1,0:T(8,128)(2,1)}, bf16[4,512,512]{2,1,0:T(8,128)(2,1)}, u32[]{:S(2)}, u32[]{:S(2)}) collective-permute-start(bf16[4,512,512]{2,1,0:T(8,128)(2,1)} %bitcast_dynamic-update-slice_fusion.4), channel_id=1, source_target_pairs={{0,16},{1,17},{2,18},{3,19},{4,20},{5,21},{6,22},{7,23},{8,24},{9,... | collective-permute-start | bytes 6291464 | tf_op jit(solution)/shard_map/ppermute | solution.py:27
  189.9 51.4 %collective-permute-start.40 = (bf16[256,512]{1,0:T(8,128)(2,1)S(1)}, bf16[256,512]{1,0:T(8,128)(2,1)S(1)}, u32[]{:S(2)}, u32[]{:S(2)}) collective-permute-start(bf16[256,512]{1,0:T(8,128)(2,1)S(1)} %collective-permute-done.39), channel_id=1, source_target_pairs={{1,0},{2,1},{3,2},{5,4},{6,5},{7,6},{9,8},{10,9},{11,10},{13,12},{... | collective-permute-start | bytes 786440 | tf_op jit(solution)/shard_map/ppermute | solution.py:27
  245.2 55.0 %collective-permute-start.33 = (bf16[1024,1024]{0,1:T(8,128)(2,1)}, bf16[1024,1024]{0,1:T(8,128)(2,1)}, u32[]{:S(2)}, u32[]{:S(2)}) collective-permute-start(bf16[1024,1024]{0,1:T(8,128)(2,1)} %convolution_convert_fusion.18), channel_id=1, source_target_pairs={{0,4},{1,5},{2,6},{3,7},{4,0},{5,1},{6,2},{7,3},{8,12},{9,13},{10,... | collective-permute-start | bytes 6291464 | tf_op jit(solution)/shard_map/ppermute | solution.py:27
  284.3 63.2 %collective-permute-start.51 = (bf16[4,256,512]{2,1,0:T(8,128)(2,1)}, bf16[4,256,512]{2,1,0:T(8,128)(2,1)S(1)}, u32[]{:S(2)}, u32[]{:S(2)}) collective-permute-start(bf16[4,256,512]{2,1,0:T(8,128)(2,1)} %bitcast_dynamic-update-slice_fusion.11), channel_id=1, source_target_pairs={{0,8},{1,9},{2,10},{3,11},{4,12},{5,13},{6,14},{7,15},{8,0},{9,1},... | collective-permute-start | bytes 3145736 | tf_op jit(solution)/shard_map/ppermute | solution.py:27
  506.2 57.8 %all-to-all-start.2 = ((bf16[4,256,1024]{2,1,0:T(8,128)(2,1)}), bf16[4,256,1024]{2,1,0:T(8,128)(2,1)}, u32[]{:S(2)}, u32[]{:S(2)}) async-start(bf16[4,256,1024]{2,1,0:T(8,128)(2,1)} %bitcast.91), calls=%async_computation.2 | async-start | bytes 4194304 | tf_op jit(solution)/shard_map/all_to_all | solution.py:393
  516.0 48.0 %collective-permute-start.60 = (bf16[4,512,512]{2,1,0:T(8,128)(2,1)S(1)}, bf16[4,512,512]{2,1,0:T(8,128)(2,1)}, u32[]{:S(2)}, u32[]{:S(2)}) collective-permute-start(bf16[4,512,512]{2,1,0:T(8,128)(2,1)S(1)} %bitcast.383), channel_id=1, source_target_pairs={{0,8},{1,9},{2,10},{3,11},{4,12},{5,13},{6,14},{7,15},{8,0},{9,1},... | collective-permute-start | bytes 6291464 | tf_op jit(solution)/shard_map/ppermute | solution.py:27
  574.4 88.4 %collective-permute-start.65 = (bf16[4,512,512]{2,1,0:T(8,128)(2,1)}, bf16[4,512,512]{2,1,0:T(8,128)(2,1)}, u32[]{:S(2)}, u32[]{:S(2)}) collective-permute-start(bf16[4,512,512]{2,1,0:T(8,128)(2,1)} %bitcast.94), channel_id=1, source_target_pairs={{0,8},{1,9},{2,10},{3,11},{4,12},{5,13},{6,14},{7,15},{8,0},{9,1},... | collective-permute-start | bytes 6291464 | tf_op jit(solution)/shard_map/ppermute | solution.py:27
  587.7 75.2 %collective-permute-start.63 = (bf16[4,512,512]{2,1,0:T(8,128)(2,1)}, bf16[4,512,512]{2,1,0:T(8,128)(2,1)}, u32[]{:S(2)}, u32[]{:S(2)}) collective-permute-start(bf16[4,512,512]{2,1,0:T(8,128)(2,1)} %fusion.27), channel_id=1, source_target_pairs={{0,16},{1,17},{2,18},{3,19},{4,20},{5,21},{6,22},{7,23},{8,24},{9,... | collective-permute-start | bytes 6291464 | tf_op jit(solution)/shard_map/ppermute | solution.py:27
  591.0 71.9 %collective-permute-start.64 = (bf16[4,256,1024]{2,1,0:T(8,128)(2,1)}, bf16[4,256,1024]{2,1,0:T(8,128)(2,1)}, u32[]{:S(2)}, u32[]{:S(2)}) collective-permute-start(bf16[4,256,1024]{2,1,0:T(8,128)(2,1)} %all-to-all-done.2), channel_id=1, source_target_pairs={{0,0},{1,1},{2,2},{3,3},{4,16},{5,17},{6,18},{7,19},{8,8},{9,9},{1... | collective-permute-start | bytes 6291464 | tf_op jit(solution)/shard_map/ppermute | solution.py:27
  655.9 67.4 %collective-permute-start.67 = (bf16[4,512,512]{2,1,0:T(8,128)(2,1)}, bf16[4,512,512]{2,1,0:T(8,128)(2,1)}, u32[]{:S(2)}, u32[]{:S(2)}) collective-permute-start(bf16[4,512,512]{2,1,0:T(8,128)(2,1)} %bitcast.97), channel_id=1, source_target_pairs={{0,8},{1,9},{2,10},{3,11},{4,12},{5,13},{6,14},{7,15},{8,0},{9,1},... | collective-permute-start | bytes 6291464 | tf_op jit(solution)/shard_map/ppermute | solution.py:27
  674.0 112.9 %all-to-all-start.4 = ((bf16[4,512,1024]{2,1,0:T(8,128)(2,1)}), bf16[4,512,1024]{2,1,0:T(8,128)(2,1)}, u32[]{:S(2)}, u32[]{:S(2)}) async-start(bf16[4,512,1024]{2,1,0:T(8,128)(2,1)} %pad_maximum_fusion.4), calls=%async_computation.4 | async-start | bytes 8388608 | tf_op jit(solution)/shard_map/all_to_all | solution.py:475
  738.3 48.6 %collective-permute-start.69 = (bf16[4,512,512]{2,1,0:T(8,128)(2,1)S(1)}, bf16[4,512,512]{2,1,0:T(8,128)(2,1)}, u32[]{:S(2)}, u32[]{:S(2)}) collective-permute-start(bf16[4,512,512]{2,1,0:T(8,128)(2,1)S(1)} %bitcast.384), channel_id=1, source_target_pairs={{0,8},{1,9},{2,10},{3,11},{4,12},{5,13},{6,14},{7,15},{8,0},{9,1},... | collective-permute-start | bytes 6291464 | tf_op jit(solution)/shard_map/ppermute | solution.py:27
  746.0 85.4 %collective-permute-start.75 = (bf16[4,512,512]{2,1,0:T(8,128)(2,1)}, bf16[4,512,512]{2,1,0:T(8,128)(2,1)}, u32[]{:S(2)}, u32[]{:S(2)}) collective-permute-start(bf16[4,512,512]{2,1,0:T(8,128)(2,1)} %pad_maximum_fusion.9), channel_id=1, source_target_pairs={{0,8},{1,9},{2,10},{3,11},{4,12},{5,13},{6,14},{7,15},{8,0},{9,1},... | collective-permute-start | bytes 6291464 | tf_op jit(solution)/shard_map/ppermute | solution.py:27
  750.6 80.8 %collective-permute-start.74 = (bf16[4,512,512]{2,1,0:T(8,128)(2,1)}, bf16[4,512,512]{2,1,0:T(8,128)(2,1)}, u32[]{:S(2)}, u32[]{:S(2)}) collective-permute-start(bf16[4,512,512]{2,1,0:T(8,128)(2,1)} %fusion.25), channel_id=1, source_target_pairs={{16,0},{17,1},{18,2},{19,3},{20,4},{21,5},{22,6},{23,7},{24,8},{25... | collective-permute-start | bytes 6291464 | tf_op jit(solution)/shard_map/ppermute | solution.py:27
  837.4 65.5 %all-to-all-start.6 = ((bf16[4,512,512]{2,1,0:T(8,128)(2,1)}), bf16[4,512,512]{2,1,0:T(8,128)(2,1)}, u32[]{:S(2)}, u32[]{:S(2)}) async-start(bf16[4,512,512]{2,1,0:T(8,128)(2,1)} %fusion.31), calls=%async_computation.6 | async-start | bytes 4194304 | tf_op jit(solution)/shard_map/all_to_all | solution.py:475
  849.2 49.0 %collective-permute-start.80 = (bf16[4,512,512]{2,1,0:T(8,128)(2,1)S(1)}, bf16[4,512,512]{2,1,0:T(8,128)(2,1)S(1)}, u32[]{:S(2)}, u32[]{:S(2)}) collective-permute-start(bf16[4,512,512]{2,1,0:T(8,128)(2,1)S(1)} %fusion.24), channel_id=1, source_target_pairs={{16,0},{17,1},{18,2},{19,3},{20,4},{21,5},{22,6},{23,7},{24,8},{25... | collective-permute-start | bytes 6291464 | tf_op jit(solution)/shard_map/ppermute | solution.py:27
  902.9 61.9 %all-to-all-start.8 = ((bf16[4,512,512]{2,1,0:T(8,128)(2,1)}), bf16[4,512,512]{2,1,0:T(8,128)(2,1)}, u32[]{:S(2)}, u32[]{:S(2)}) async-start(bf16[4,512,512]{2,1,0:T(8,128)(2,1)} %fusion.32), calls=%async_computation.8 | async-start | bytes 4194304 | tf_op jit(solution)/shard_map/all_to_all | solution.py:475
  964.8 148.0 %all-to-all-start.7 = ((bf16[4,512,512]{2,1,0:T(8,128)(2,1)}), bf16[4,512,512]{2,1,0:T(8,128)(2,1)S(1)}, u32[]{:S(2)}, u32[]{:S(2)}) async-start(bf16[4,512,512]{2,1,0:T(8,128)(2,1)} %add_convert_fusion.4), calls=%async_computation.7 | async-start | bytes 4194304 | tf_op jit(solution)/shard_map/all_to_all | solution.py:475
  969.6 143.2 %all-reduce.2.cloned.1.call-start = ((), (), s32[]{:S(2)}) async-start(), calls=%async_computation.9 | async-start | bytes 196608 | tf_op jit(solution)/shard_map/psum | solution.py:685
  (192 other events, 2764.7 us)
Sparse Core Ops, SparseCore 0:
  985.6 127.1 all-reduce.1

commit v6 on v5

--- a/solution.py
+++ b/solution.py
@@ -444,11 +444,12 @@
 
     def chips_twice(item, across, along):
         part = item.shape[0] // 2
-        far = []
-        for k in range(1, chips):
-            upper = move(across[:part], lambda s, d, t: (s, d ^ (2 * k), t))
-            lower = move(along[k - 1][part:], lambda s, d, t: (1 - s, d, t))
-            far.append(jnp.concatenate([upper, lower], axis=0))
+        uppers = [move(across[:part], lambda s, d, t: (s, d ^ (2 * k), t)) for k in range(1, chips)]
+        lowers = [move(along[k - 1][part:], lambda s, d, t: (1 - s, d, t)) for k in range(1, chips)]
+        return uppers, lowers
+
+    def both_layers(item, across, along, uppers, lowers):
+        far = [jnp.concatenate(pair, axis=0) for pair in zip(uppers, lowers)]
         mine, other = [item] + along, [across] + far
         result = []
         for layer in range(2):
@@ -457,7 +458,8 @@
         return result
 
     def over_chips(item):
-        return chips_twice(item, *chips_once(item))
+        across, along = chips_once(item)
+        return both_layers(item, across, along, *chips_twice(item, across, along))
 
     def from_x(slabs):
         return [move(slabs[k], lambda s, d, t: (s, d ^ (2 * k), t)) for k in range(1, chips)]
@@ -497,7 +499,12 @@
     out_first = w_out[0].reshape(2, head_half, local)
     back_first = w_back[0].reshape(2, hidden_half, local)
     later = hidden_half // 2
-    attention_own = own_half(jnp.concatenate([qkv_first, out_first], axis=1))
+    gain_count, bias_count = gains.shape[1], biases.shape[1]
+    table = jnp.concatenate([gains[0], biases[0], ffn_bias.reshape(-1, local)], axis=0)
+    table_rows = table.shape[0]
+    table = jnp.pad(table, ((0, -table_rows % 16), (0, 0)))
+    table = jnp.broadcast_to(table, (2,) + table.shape)
+    attention_own = own_half(jnp.concatenate([qkv_first, out_first, table], axis=1))
     back_own = own_half(back_first)
     in_own = own_half(in_first)
     back_two = jnp.stack(over_chips(back_own[later:]))
@@ -509,23 +516,28 @@
     upward, downward = [in_own], [in_own]
     for at in range(1, ranks):
         relay(upward, downward)
+        if at == 1:
+            upward[-1], downward[-1], seq_lengths = tie(upward[-1], downward[-1], seq_lengths)
         if at == ranks // 2:
             upward[-1], downward[-1], across, *along = tie(upward[-1], downward[-1], across, *along)
-            attention_all = chips_twice(attention_item, across, along)
-    upward[-1], downward[-1], gains, seq_lengths = tie(upward[-1], downward[-1], gains, seq_lengths)
+            uppers, lowers = chips_twice(attention_item, across, along)
+    upward[-1], downward[-1], *far = tie(upward[-1], downward[-1], *uppers, *lowers)
+    attention_all = both_layers(attention_item, across, along, far[: chips - 1], far[chips - 1 :])
     in_item = assemble(upward, downward)
-    in_all = over_chips(in_item)
+    in_across, in_along = chips_once(in_item)
     back_item = over_ranks(after(back_own[:later], in_item))
+    back_item, back_two, in_across, *in_along = tie(back_item, back_two, in_across, *in_along)
+    in_all = both_layers(in_item, in_across, in_along, *chips_twice(in_item, in_across, in_along))
     across, along = chips_once(back_item)
-    back_two = after(back_two, back_item)
     upward, downward = [back_two], [back_two]
     for _ in range(1, ranks):
         relay(upward, downward)
 
     def late_weights(active):
         tied = tie(active, across, upward[-1], downward[-1], *along)
+        here = (back_item, tied[1], list(tied[4:]))
         halves = zip(
-            chips_twice(back_item, tied[1], list(tied[4:])),
+            both_layers(*here, *chips_twice(*here)),
             jnp.moveaxis(assemble(upward[:-1] + [tied[2]], downward[:-1] + [tied[3]]), 1, 0),
         )
         return tied[0], [jnp.concatenate(pair, axis=1).reshape(-1, width) for pair in halves]
@@ -533,45 +545,27 @@
     weights = [
         (
             attention_all[layer][:, : 3 * head_half].reshape(-1, width),
-            attention_all[layer][:, 3 * head_half :].reshape(-1, width),
+            attention_all[layer][:, 3 * head_half : 4 * head_half].reshape(-1, width),
             in_all[layer].reshape(-1, width),
         )
         for layer in range(2)
     ]
 
-    gain_count, bias_count = gains.shape[1], biases.shape[1]
-    packed_small = jnp.concatenate([gains, biases, ffn_bias.reshape(1, -1, local)], axis=1)
-    table_parts = [
-        [
-            packed_small
-            if a == 0 and b == 0
-            else move(packed_small, lambda s, d, t: (s ^ a, d ^ b, t))
-            for b in range(copies)
-        ]
-        for a in range(2)
-    ]
-    table_all = jnp.stack([jnp.stack(row) for row in table_parts])[:, :, 0].astype(WIDE)
-    small_all = jnp.stack([choose(section, (table_all[at], table_all[1 - at])) for at in range(2)])
-    order = [[at ^ b for b in range(copies)] for at in range(copies)]
-    small_all = jnp.stack(
-        [choose(copy_at, [small_all[:, order[at][b]] for b in range(copies)]) for at in range(copies)],
-        axis=1,
-    )
-
     def head_columns(row):
         halves = row.reshape(ranks, 2, -1)
         return choose(core, (halves[:, 0], halves[:, 1])).reshape(-1)
 
     small = []
     for layer in range(2):
-        table = jnp.moveaxis(small_all[layer, :, : gain_count + bias_count], 0, 1).reshape(-1, width)
-        query_bias = head_columns(table[gain_count])
-        value_bias = head_columns(table[gain_count + 1])
+        table = attention_all[layer][0, 4 * head_half : 4 * head_half + table_rows].astype(WIDE)
+        whole = relative(table)
+        query_bias = head_columns(whole[gain_count])
+        value_bias = head_columns(whole[gain_count + 1])
         query_bias, value_bias = query_bias.reshape(ranks, 1, -1), value_bias.reshape(ranks, 1, -1)
         offset = jnp.concatenate([query_bias, jnp.zeros_like(query_bias), value_bias], axis=1).reshape(-1)
-        inner_bias = head_columns(small_all[layer, :, gain_count + bias_count :].reshape(-1))
-        table = relative(table)
-        small.append((table[:gain_count], table[gain_count:], offset, inner_bias, head_half))
+        inner_bias = whole[gain_count + bias_count :].reshape(-1, copies, local)
+        inner_bias = head_columns(jnp.swapaxes(inner_bias, 0, 1).reshape(-1))
+        small.append((table[:gain_count], table[gain_count : gain_count + bias_count], offset, inner_bias, head_half))
 
     lengths = jnp.where(core == section, seq_lengths, to_other_core(seq_lengths))[:, 0]
     lengths = lax.dynamic_index_in_dim(lengths, rank // repeats, 0, keepdims=False)
@@ -642,28 +636,24 @@
     first_in = first_grad + core_sum(matmul(packed_low, weights[0][0]))
     attention_slabs = attention_grads(first_saved, attended_grad, packed_low)
     attention_one_here = from_x(attention_slabs)
-    first_in, attention_here, *in_here = tie(first_in, attention_here, *in_here)
-    first_in_spread = spread_rows(first_in.astype(LOW))
+    first_in, attention_here, back_sent, *in_here = tie(first_in, attention_here, back_sent, *in_here)
     in_one = add(in_slabs[0], in_here)
     in_sent = from_section(in_one, 0)
+    first_in_spread = spread_rows(first_in.astype(LOW))
+    back_here = from_z(by_section(add(back_one, [back_sent]), back_two))
     attention_two_slabs = jnp.split(add_ranks(attention_here), chips, axis=-1)
     attention_two_here = from_x(attention_two_slabs)
 
-    back_sent, *attention_one_here = tie(back_sent, *attention_one_here)
-    back_here = from_z(by_section(add(back_one, [back_sent]), back_two))
+    in_sent, back_here, first_in_spread, *attention_one_here = tie(
+        in_sent, back_here, first_in_spread, *attention_one_here
+    )
     attention_one = add(attention_slabs[0], attention_one_here)
     attention_one_sent = from_section(attention_one, 0)
+    in_here = from_z(by_section(add(in_one, [in_sent]), in_two))
     attention_two = add(attention_two_slabs[0], attention_two_here)
     attention_two_sent = from_section(attention_two, 1)
-    in_here = from_z(by_section(add(in_one, [in_sent]), in_two))
     first_placed = place_rows(first_in_spread, 0)
-    attention_one_sent, attention_two_sent, back_here = tie(attention_one_sent, attention_two_sent, back_here)
-    attention_one = add(attention_one, [attention_one_sent])
-    attention_two = add(attention_two, [attention_two_sent])
     back_shard = finish(add_ranks(back_here))
-    input_grads = by_section(first_placed, second_placed).astype(WIDE)[None]
-    attention_here = from_z(attention_one)
-    in_shard = finish(add_ranks(in_here))
 
     def spread_columns(row):
         blocks = row.reshape(ranks, 1, -1)
@@ -682,15 +672,25 @@
         )
     table = jnp.stack(tables)
     table = jnp.where(counted, table, 0.0) if repeats > 1 else table
-    table = lax.psum(table, AXES)
-    attention_here, table = tie(attention_here, table)
+    table = table + to_other_core(table)
+    table = choose(section, (table[0], table[1])) + move(
+        choose(section, (table[1], table[0])), lambda s, d, t: (1 - s, d, t)
+    )
+    attention_one_sent, attention_two_sent, in_here, table = tie(
+        attention_one_sent, attention_two_sent, in_here, table
+    )
+    attention_here = from_z(add(attention_one, [attention_one_sent]))
+    table = sum([move(table, lambda s, d, t: (s, d ^ (2 * k), t)) for k in range(1, chips)], table)
+    table = sum([move(table, lambda s, d, t: (s, d, (t + j) % ranks)) for j in range(1, ranks)], table)
+    attention_two = add(attention_two, [attention_two_sent])
+    in_shard = finish(add_ranks(in_here))
+    input_grads = by_section(first_placed, second_placed).astype(WIDE)[None]
     attention_shard = finish(by_section(add_ranks(attention_here), attention_two))
     qkv_shard, out_shard = attention_shard[:, : 3 * head_half], attention_shard[:, 3 * head_half :]
     qkv_grad = jnp.transpose(qkv_shard.reshape(2, 3, head_half, local), (3, 1, 0, 2)).reshape(local, 3, -1)
     out_grad_w = out_shard.reshape(-1, local)
     in_grad = jnp.transpose(in_shard.reshape(-1, local))
     back_grad = back_shard.reshape(-1, local)
-    table = choose(section, (table[0], table[1]))
     sliced = lax.dynamic_slice_in_dim(table[: gain_count + bias_count], copy_at * local, local, 1)
     inner = lax.dynamic_index_in_dim(
         table[gain_count + bias_count :].reshape(copies, -1), copy_at, 0, keepdims=False

time: 1140 us -> 998 us (0.88)
  waiting for transfers between devices: 404 us -> 266 us
  between operations: 17.1 us -> 3.44 us
    psum x1 -> x0, waiting for transfers between devices: 101 us -> none  [on_device(): table = lax.psum(table, AXES)]
    ppermute x83 -> x82, waiting for transfers between devices: 291 us -> 245 us  [move(): return lax.ppermute(value, AXES, pairs)]
    ppermute x83 -> x82, starting transfers between devices: 180 us -> 177 us  [move(): return lax.ppermute(value, AXES, pairs)]
    unnamed x258 -> x218, local copies, waits for them, and re-layouts: 36.3 us -> 35.2 us
  transfers between devices with their start and end apart: 93 -> 91, of which waited for: 38 -> 38; matrix products, arithmetic and copies ran while one was open for 26% -> 28% of each run, Pallas kernels for 7% -> 8%
where the time goes in v6:
time: 998 us; the launch traced here: 986 us
  waiting for transfers between devices  266 us (27%)
  starting transfers between devices  223 us (22%)
  other arithmetic  174 us (17%)
  matrix products  143 us (14%)
  Pallas kernels  102 us (10%)
  local copies, waits for them, and re-layouts  74.1 us (7%)
    ppermute x82, waiting for transfers between devices, move(): return lax.ppermute(value, AXES, pairs)  245 us
    ppermute x82, starting transfers between devices, move(): return lax.ppermute(value, AXES, pairs)  177 us
    pallas_call x2, Pallas kernels, attend_backward(): pl.pallas_call(functools.partial(backward_kernel, widths), grid_spec=pltp...  58.9 us
    dot_general x14, matrix products, lhs_inner(): lax.dot_general(lhs_mat, rhs_mat, (((0,), (0,)), ((), ())), preferred_ele...  52.3 us
    dot_general x8, matrix products, rhs_inner(): lax.dot_general(lhs_mat, rhs_mat, (((1,), (1,)), ((), ())), preferred_ele...  46.5 us
    dot_general x10, matrix products, matmul(): return jnp.dot(lhs_mat, rhs_mat, preferred_element_type=WIDE)  44.4 us
    pallas_call x2, Pallas kernels, attend_forward(): pl.pallas_call(functools.partial(forward_kernel, widths), grid_spec=pltpu...  43.5 us
    unnamed x218, local copies, waits for them, and re-layouts  35.2 us
  transfers between devices with their start and end apart: 91, of which 38 were waited for; matrix products, arithmetic and copies ran while one was open for 28% of the time, Pallas kernels for 8%

profile of v6, /device:TPU:0, one launch (start us, length us, event | category | flops | bytes accessed | tf_op | source)
XLA Modules:
  0.0 986.0 jit_solution(14804810509649937133)
XLA Ops:
  86.9 11.6 %collective-permute-done.16 = bf16[512,512]{1,0:T(8,128)(2,1)S(1)} collective-permute-done((bf16[512,512]{1,0:T(8,128)(2,1)S(1)}, bf16[512,512]{1,0:T(8,128)(2,1)S(1)}, u32[]{:S(2)}, u32[]{:S(2)}) %collective-permute-start.16) | collective-permute-done | bytes 524320 | tf_op jit(solution)/shard_map/ppermute | solution.py:27
  107.2 9.0 collective-permute-done.18
  132.3 7.4 collective-permute-start.25
  155.9 7.3 collective-permute-done.25
  187.6 21.7 %shard_map.169 = (bf16[1024,512]{1,0:T(8,128)(2,1)S(1)}, f32[4,2,1024]{2,1,0:T(2,128)S(1)}) custom-call(s32[4]{0:T(128)S(1)} %compare_select_fusion.8.start_ref, s32[4]{0:T(128)S(1)} %get-tuple-element.158.kind_ref, bf16[1024,1536]{1,0:T(8,128)(2,1)S(1)} %add_convert_fusion.1.query_ref.key_ref.value_ref, ...), custom_call_target="tpu_custom_call" | custom-call | tf_op jit(solution)/shard_map/pallas_call | solution.py:245
  290.6 8.7 collective-permute-done.42
  305.3 7.7 multiply_convert_fusion.3
  313.0 9.5 collective-permute-done.43
  359.1 21.8 %shard_map.170 = (bf16[1024,512]{1,0:T(8,128)(2,1)S(1)}, f32[4,2,1024]{2,1,0:T(2,128)S(1)}) custom-call(s32[4]{0:T(128)S(1)} %compare_select_fusion.8.start_ref, s32[4]{0:T(128)S(1)} %get-tuple-element.158.kind_ref, bf16[1024,1536]{1,0:T(8,128)(2,1)S(1)} %add_convert_fusion.query_ref.key_ref.value_ref, ...), custom_call_target="tpu_custom_call" | custom-call | tf_op jit(solution)/shard_map/pallas_call | solution.py:245
  409.0 7.5 multiply_convert_fusion.2
  451.7 9.5 multiply_convert_fusion.1
  491.0 29.4 %shard_map.171 = (bf16[1024,1536]{1,0:T(8,128)(2,1)S(1)}, f32[4,2,128]{2,1,0:T(2,128)S(1)}) custom-call(s32[4]{0:T(128)S(1)} %compare_select_fusion.8.start_ref, s32[4]{0:T(128)S(1)} %get-tuple-element.158.kind_ref, bf16[1024,1536]{1,0:T(8,128)(2,1)} %copy-done.1, bf16[1024,1536]{1,0:T(8,128)(2,1)} %copy-done.1, bf16[1024,1536]{1,0:T(8,128)(2,1)} %copy-done.1, ...), custom_call_target="tpu_custom_call" | custom-call | tf_op jit(solution)/shard_map/pallas_call | solution.py:270
  522.1 7.3 collective-permute-done.53
  557.1 17.1 %collective-permute-start.57 = (bf16[4,256,1024]{2,1,0:T(8,128)(2,1)}, bf16[4,256,1024]{2,1,0:T(8,128)(2,1)}, u32[]{:S(2)}, u32[]{:S(2)}) collective-permute-start(bf16[4,256,1024]{2,1,0:T(8,128)(2,1)} %all-to-all-done.2), channel_id=1, source_target_pairs={{0,0},{1,1},{2,2},{3,3},{4,16},{5,17},{6,18},{7,19},{8,8},{9,9},{1... | collective-permute-start | bytes 6291464 | tf_op jit(solution)/shard_map/ppermute | solution.py:27
  580.3 9.4 multiply_convert_fusion
  634.1 7.3 all-to-all-done.3
  658.8 29.5 %shard_map.172 = (bf16[1024,1536]{1,0:T(8,128)(2,1)S(1)}, f32[4,2,128]{2,1,0:T(2,128)S(1)}) custom-call(s32[4]{0:T(128)S(1)} %compare_select_fusion.8.start_ref, s32[4]{0:T(128)S(1)} %get-tuple-element.158.kind_ref, bf16[1024,1536]{1,0:T(8,128)(2,1)} %copy-done, bf16[1024,1536]{1,0:T(8,128)(2,1)} %copy-done, bf16[1024,1536]{1,0:T(8,128)(2,1)} %copy-done, ...), custom_call_target="tpu_custom_call" | custom-call | tf_op jit(solution)/shard_map/pallas_call | solution.py:270
  701.3 41.6 %collective-permute-done.63 = bf16[4,512,512]{2,1,0:T(8,128)(2,1)} collective-permute-done((bf16[4,512,512]{2,1,0:T(8,128)(2,1)S(1)}, bf16[4,512,512]{2,1,0:T(8,128)(2,1)}, u32[]{:S(2)}, u32[]{:S(2)}) %collective-permute-start.63) | collective-permute-done | bytes 2097184 | tf_op jit(solution)/shard_map/ppermute | solution.py:27
  772.3 13.6 %all-to-all-done.6 = bf16[4,128,1024]{2,1,0:T(8,128)(2,1)} async-done(((bf16[4,128,1024]{2,1,0:T(8,128)(2,1)}), bf16[4,128,1024]{2,1,0:T(8,128)(2,1)}, u32[]{:S(2)}, u32[]{:S(2)}) %all-to-all-start.6) | async-done | bytes 1048608 | tf_op jit(solution)/shard_map/all_to_all | solution.py:403
  809.8 34.4 %collective-permute-done.65 = bf16[4,512,512]{2,1,0:T(8,128)(2,1)} collective-permute-done((bf16[4,512,512]{2,1,0:T(8,128)(2,1)}, bf16[4,512,512]{2,1,0:T(8,128)(2,1)}, u32[]{:S(2)}, u32[]{:S(2)}) %collective-permute-start.65) | collective-permute-done | bytes 2097184 | tf_op jit(solution)/shard_map/ppermute | solution.py:27
  876.2 10.2 %collective-permute-done.71 = bf16[512,512]{1,0:T(8,128)(2,1)} collective-permute-done((bf16[512,512]{1,0:T(8,128)(2,1)}, bf16[512,512]{1,0:T(8,128)(2,1)}, u32[]{:S(2)}, u32[]{:S(2)}) %collective-permute-start.71) | collective-permute-done | bytes 524320 | tf_op jit(solution)/shard_map/ppermute | solution.py:27
  894.2 23.3 %collective-permute-done.74 = f32[12,1024]{1,0:T(8,128)S(1)} collective-permute-done((f32[12,1024]{1,0:T(8,128)S(1)}, f32[12,1024]{1,0:T(8,128)S(1)}, u32[]{:S(2)}, u32[]{:S(2)}) %collective-permute-start.74) | collective-permute-done | bytes 49184 | tf_op jit(solution)/shard_map/ppermute | solution.py:27
  931.3 9.6 collective-permute-start.66
  969.3 7.3 collective-permute-done.80
  (631 shorter events, 620.5 us)
Async XLA Ops:
  62.5 43.9 %all-to-all-start = ((bf16[4,128,1024]{2,1,0:T(8,128)(2,1)}), bf16[4,128,1024]{2,1,0:T(8,128)(2,1)}, u32[]{:S(2)}, u32[]{:S(2)}) async-start(bf16[4,128,1024]{2,1,0:T(8,128)(2,1)} %select_select_fusion.1), calls=%async_computation | async-start | bytes 2097152 | tf_op jit(solution)/shard_map/all_to_all | solution.py:387
  67.5 53.5 %collective-permute-start.21 = (bf16[4,528,512]{2,1,0:T(8,128)(2,1)S(1)}, bf16[4,528,512]{2,1,0:T(8,128)(2,1)}, u32[]{:S(2)}, u32[]{:S(2)}) collective-permute-start(bf16[4,528,512]{2,1,0:T(8,128)(2,1)S(1)} %bitcast_dynamic-update-slice_fusion.4), channel_id=1, source_target_pairs={{0,8},{1,9},{2,10},{3,11},{4,12},{5,13},{6,14},{7,15},{8,0},{9,1},... | collective-permute-start | bytes 6488072 | tf_op jit(solution)/shard_map/ppermute | solution.py:27
  68.8 52.9 %collective-permute-start.20 = (bf16[4,528,512]{2,1,0:T(8,128)(2,1)S(1)}, bf16[4,528,512]{2,1,0:T(8,128)(2,1)}, u32[]{:S(2)}, u32[]{:S(2)}) collective-permute-start(bf16[4,528,512]{2,1,0:T(8,128)(2,1)S(1)} %bitcast_dynamic-update-slice_fusion.4), channel_id=1, source_target_pairs={{0,16},{1,17},{2,18},{3,19},{4,20},{5,21},{6,22},{7,23},{8,24},{9,... | collective-permute-start | bytes 6488072 | tf_op jit(solution)/shard_map/ppermute | solution.py:27
  180.1 69.4 %collective-permute-start.34 = (bf16[4,512,512]{2,1,0:T(8,128)(2,1)}, bf16[4,512,512]{2,1,0:T(8,128)(2,1)}, u32[]{:S(2)}, u32[]{:S(2)}) collective-permute-start(bf16[4,512,512]{2,1,0:T(8,128)(2,1)} %bitcast_dynamic-update-slice_fusion.7), channel_id=1, source_target_pairs={{0,8},{1,9},{2,10},{3,11},{4,12},{5,13},{6,14},{7,15},{8,0},{9,1},... | collective-permute-start | bytes 6291464 | tf_op jit(solution)/shard_map/ppermute | solution.py:27
  180.5 69.0 %collective-permute-start.33 = (bf16[4,512,512]{2,1,0:T(8,128)(2,1)}, bf16[4,512,512]{2,1,0:T(8,128)(2,1)}, u32[]{:S(2)}, u32[]{:S(2)}) collective-permute-start(bf16[4,512,512]{2,1,0:T(8,128)(2,1)} %bitcast_dynamic-update-slice_fusion.7), channel_id=1, source_target_pairs={{0,16},{1,17},{2,18},{3,19},{4,20},{5,21},{6,22},{7,23},{8,24},{9,... | collective-permute-start | bytes 6291464 | tf_op jit(solution)/shard_map/ppermute | solution.py:27
  212.0 48.8 %collective-permute-start.26 = (bf16[1024,1024]{0,1:T(8,128)(2,1)}, bf16[1024,1024]{0,1:T(8,128)(2,1)}, u32[]{:S(2)}, u32[]{:S(2)}) collective-permute-start(bf16[1024,1024]{0,1:T(8,128)(2,1)} %convolution_convert_fusion.18), channel_id=1, source_target_pairs={{0,4},{1,5},{2,6},{3,7},{4,0},{5,1},{6,2},{7,3},{8,12},{9,13},{10,... | collective-permute-start | bytes 6291464 | tf_op jit(solution)/shard_map/ppermute | solution.py:27
  260.8 52.3 %collective-permute-start.44 = (bf16[4,256,512]{2,1,0:T(8,128)(2,1)S(1)}, bf16[4,256,512]{2,1,0:T(8,128)(2,1)S(1)}, u32[]{:S(2)}, u32[]{:S(2)}) collective-permute-start(bf16[4,256,512]{2,1,0:T(8,128)(2,1)S(1)} %bitcast_dynamic-update-slice_fusion.11), channel_id=1, source_target_pairs={{0,8},{1,9},{2,10},{3,11},{4,12},{5,13},{6,14},{7,15},{8,0},{9,1},... | collective-permute-start | bytes 3145736 | tf_op jit(solution)/shard_map/ppermute | solution.py:27
  471.7 57.7 %all-to-all-start.2 = ((bf16[4,256,1024]{2,1,0:T(8,128)(2,1)}), bf16[4,256,1024]{2,1,0:T(8,128)(2,1)}, u32[]{:S(2)}, u32[]{:S(2)}) async-start(bf16[4,256,1024]{2,1,0:T(8,128)(2,1)} %bitcast.78), calls=%async_computation.2 | async-start | bytes 4194304 | tf_op jit(solution)/shard_map/all_to_all | solution.py:393
  481.7 47.6 %collective-permute-start.53 = (bf16[4,512,512]{2,1,0:T(8,128)(2,1)S(1)}, bf16[4,512,512]{2,1,0:T(8,128)(2,1)}, u32[]{:S(2)}, u32[]{:S(2)}) collective-permute-start(bf16[4,512,512]{2,1,0:T(8,128)(2,1)S(1)} %bitcast.368), channel_id=1, source_target_pairs={{0,8},{1,9},{2,10},{3,11},{4,12},{5,13},{6,14},{7,15},{8,0},{9,1},... | collective-permute-start | bytes 6291464 | tf_op jit(solution)/shard_map/ppermute | solution.py:27
  535.8 38.4 %collective-permute-start.54 = (bf16[1024,1024]{0,1:T(8,128)(2,1)S(1)}, bf16[1024,1024]{0,1:T(8,128)(2,1)S(1)}, u32[]{:S(2)}, u32[]{:S(2)}) collective-permute-start(bf16[1024,1024]{0,1:T(8,128)(2,1)S(1)} %convolution_convert_fusion.13), channel_id=1, source_target_pairs={{0,4},{1,5},{2,6},{3,7},{4,0},{5,1},{6,2},{7,3},{8,12},{9,13},{10,... | collective-permute-start | bytes 6291464 | tf_op jit(solution)/shard_map/ppermute | solution.py:27
  539.7 88.2 %collective-permute-start.58 = (bf16[4,512,512]{2,1,0:T(8,128)(2,1)}, bf16[4,512,512]{2,1,0:T(8,128)(2,1)}, u32[]{:S(2)}, u32[]{:S(2)}) collective-permute-start(bf16[4,512,512]{2,1,0:T(8,128)(2,1)} %bitcast.81), channel_id=1, source_target_pairs={{0,8},{1,9},{2,10},{3,11},{4,12},{5,13},{6,14},{7,15},{8,0},{9,1},... | collective-permute-start | bytes 6291464 | tf_op jit(solution)/shard_map/ppermute | solution.py:27
  552.8 75.1 %collective-permute-start.56 = (bf16[4,512,512]{2,1,0:T(8,128)(2,1)}, bf16[4,512,512]{2,1,0:T(8,128)(2,1)}, u32[]{:S(2)}, u32[]{:S(2)}) collective-permute-start(bf16[4,512,512]{2,1,0:T(8,128)(2,1)} %fusion.27), channel_id=1, source_target_pairs={{0,16},{1,17},{2,18},{3,19},{4,20},{5,21},{6,22},{7,23},{8,24},{9,... | collective-permute-start | bytes 6291464 | tf_op jit(solution)/shard_map/ppermute | solution.py:27
  557.1 70.8 %collective-permute-start.57 = (bf16[4,256,1024]{2,1,0:T(8,128)(2,1)}, bf16[4,256,1024]{2,1,0:T(8,128)(2,1)}, u32[]{:S(2)}, u32[]{:S(2)}) collective-permute-start(bf16[4,256,1024]{2,1,0:T(8,128)(2,1)} %all-to-all-done.2), channel_id=1, source_target_pairs={{0,0},{1,1},{2,2},{3,3},{4,16},{5,17},{6,18},{7,19},{8,8},{9,9},{1... | collective-permute-start | bytes 6291464 | tf_op jit(solution)/shard_map/ppermute | solution.py:27
  621.4 67.0 %collective-permute-start.60 = (bf16[4,512,512]{2,1,0:T(8,128)(2,1)}, bf16[4,512,512]{2,1,0:T(8,128)(2,1)}, u32[]{:S(2)}, u32[]{:S(2)}) collective-permute-start(bf16[4,512,512]{2,1,0:T(8,128)(2,1)} %bitcast.85), channel_id=1, source_target_pairs={{0,8},{1,9},{2,10},{3,11},{4,12},{5,13},{6,14},{7,15},{8,0},{9,1},... | collective-permute-start | bytes 6291464 | tf_op jit(solution)/shard_map/ppermute | solution.py:27
  631.5 56.9 %collective-permute-start.59 = (bf16[4,512,512]{2,1,0:T(8,128)(2,1)}, bf16[4,512,512]{2,1,0:T(8,128)(2,1)}, u32[]{:S(2)}, u32[]{:S(2)}) collective-permute-start(bf16[4,512,512]{2,1,0:T(8,128)(2,1)} %fusion.25), channel_id=1, source_target_pairs={{0,16},{1,17},{2,18},{3,19},{4,20},{5,21},{6,22},{7,23},{8,24},{9,... | collective-permute-start | bytes 6291464 | tf_op jit(solution)/shard_map/ppermute | solution.py:27
  641.4 101.5 %all-to-all-start.4 = ((bf16[4,512,1024]{2,1,0:T(8,128)(2,1)}), bf16[4,512,1024]{2,1,0:T(8,128)(2,1)}, u32[]{:S(2)}, u32[]{:S(2)}) async-start(bf16[4,512,1024]{2,1,0:T(8,128)(2,1)} %pad_maximum_fusion.4), calls=%async_computation.4 | async-start | bytes 8388608 | tf_op jit(solution)/shard_map/all_to_all | solution.py:477
  694.8 48.1 %collective-permute-start.63 = (bf16[4,512,512]{2,1,0:T(8,128)(2,1)S(1)}, bf16[4,512,512]{2,1,0:T(8,128)(2,1)}, u32[]{:S(2)}, u32[]{:S(2)}) collective-permute-start(bf16[4,512,512]{2,1,0:T(8,128)(2,1)S(1)} %bitcast.367), channel_id=1, source_target_pairs={{0,8},{1,9},{2,10},{3,11},{4,12},{5,13},{6,14},{7,15},{8,0},{9,1},... | collective-permute-start | bytes 6291464 | tf_op jit(solution)/shard_map/ppermute | solution.py:27
  698.5 50.2 %collective-permute-start.62 = (bf16[4,512,512]{2,1,0:T(8,128)(2,1)}, bf16[4,512,512]{2,1,0:T(8,128)(2,1)}, u32[]{:S(2)}, u32[]{:S(2)}) collective-permute-start(bf16[4,512,512]{2,1,0:T(8,128)(2,1)} %fusion.24), channel_id=1, source_target_pairs={{16,0},{17,1},{18,2},{19,3},{20,4},{21,5},{22,6},{23,7},{24,8},{25... | collective-permute-start | bytes 6291464 | tf_op jit(solution)/shard_map/ppermute | solution.py:27
  786.0 64.8 %all-to-all-start.5 = ((bf16[4,512,512]{2,1,0:T(8,128)(2,1)}), bf16[4,512,512]{2,1,0:T(8,128)(2,1)}, u32[]{:S(2)}, u32[]{:S(2)}) async-start(bf16[4,512,512]{2,1,0:T(8,128)(2,1)} %fusion.31), calls=%async_computation.5 | async-start | bytes 4194304 | tf_op jit(solution)/shard_map/all_to_all | solution.py:477
  797.3 46.9 %collective-permute-start.65 = (bf16[4,512,512]{2,1,0:T(8,128)(2,1)}, bf16[4,512,512]{2,1,0:T(8,128)(2,1)}, u32[]{:S(2)}, u32[]{:S(2)}) collective-permute-start(bf16[4,512,512]{2,1,0:T(8,128)(2,1)} %pad_maximum_fusion.9), channel_id=1, source_target_pairs={{0,8},{1,9},{2,10},{3,11},{4,12},{5,13},{6,14},{7,15},{8,0},{9,1},... | collective-permute-start | bytes 6291464 | tf_op jit(solution)/shard_map/ppermute | solution.py:27
  802.3 48.5 %collective-permute-start.64 = (bf16[4,512,512]{2,1,0:T(8,128)(2,1)}, bf16[4,512,512]{2,1,0:T(8,128)(2,1)}, u32[]{:S(2)}, u32[]{:S(2)}) collective-permute-start(bf16[4,512,512]{2,1,0:T(8,128)(2,1)} %fusion.26), channel_id=1, source_target_pairs={{16,0},{17,1},{18,2},{19,3},{20,4},{21,5},{22,6},{23,7},{24,8},{25... | collective-permute-start | bytes 6291464 | tf_op jit(solution)/shard_map/ppermute | solution.py:27
  856.7 60.8 %all-to-all-start.7 = ((bf16[4,512,512]{2,1,0:T(8,128)(2,1)}), bf16[4,512,512]{2,1,0:T(8,128)(2,1)}, u32[]{:S(2)}, u32[]{:S(2)}) async-start(bf16[4,512,512]{2,1,0:T(8,128)(2,1)} %fusion.32), calls=%async_computation.7 | async-start | bytes 4194304 | tf_op jit(solution)/shard_map/all_to_all | solution.py:477
  869.1 48.4 %collective-permute-start.70 = (bf16[4,512,512]{2,1,0:T(8,128)(2,1)S(1)}, bf16[4,512,512]{2,1,0:T(8,128)(2,1)}, u32[]{:S(2)}, u32[]{:S(2)}) collective-permute-start(bf16[4,512,512]{2,1,0:T(8,128)(2,1)S(1)} %add_convert_fusion.5), channel_id=1, source_target_pairs={{16,0},{17,1},{18,2},{19,3},{20,4},{21,5},{22,6},{23,7},{24,8},{25... | collective-permute-start | bytes 6291464 | tf_op jit(solution)/shard_map/ppermute | solution.py:27
  921.3 57.2 %all-to-all-start.8 = ((bf16[4,512,512]{2,1,0:T(8,128)(2,1)}), bf16[4,512,512]{2,1,0:T(8,128)(2,1)S(1)}, u32[]{:S(2)}, u32[]{:S(2)}) async-start(bf16[4,512,512]{2,1,0:T(8,128)(2,1)} %add_convert_fusion.2), calls=%async_computation.8 | async-start | bytes 4194304 | tf_op jit(solution)/shard_map/all_to_all | solution.py:477
  (170 other events, 2575.1 us)

commit v7 on v6

--- a/solution.py
+++ b/solution.py
@@ -394,7 +394,8 @@
         return spread.reshape(micro_count, repeats, own_rows, width)[:, 0]
 
     def place_both(spread):
-        return move(spread, lambda s, d, t: (d % 2, (d // 2) * 2 + s, t))
+        moved = move(spread, lambda s, d, t: (d % 2, (d // 2) * 2 + s, t) if d % 2 != s else None)
+        return jnp.where(core == section, spread, moved)
 
     def spread_rows(value):
         parts = relative(value).reshape(ranks, own_rows, width)
@@ -404,10 +405,16 @@
         return spread.reshape((micro_count, repeats) + spread.shape[1:])[:, 0]
 
     def place_rows(spread, layer):
-        halves = [
-            move(spread, lambda s, d, t: (layer, (d // 2) * 2 + s, t) if d % 2 == half else None)
-            for half in range(2)
-        ]
+        halves = []
+        for half in range(2):
+            own = lambda s, d: half == layer and s == layer and d % 2 == layer
+            moved = move(
+                spread,
+                lambda s, d, t: (layer, (d // 2) * 2 + s, t) if d % 2 == half and not own(s, d) else None,
+            )
+            if half == layer:
+                moved = jnp.where((section == layer) & (core == layer), spread, moved)
+            halves.append(moved)
         return jnp.concatenate(halves, axis=1)
 
     def by_section(first, second):
@@ -478,6 +485,17 @@
 
     def add_ranks(parts):
         return jnp.sum(parts.astype(WIDE), axis=0).astype(LOW)
+
+    def hops_z(parts):
+        own = lax.dynamic_index_in_dim(parts, rank, 0, keepdims=False)
+        received = [
+            move(
+                lax.dynamic_index_in_dim(parts, (rank + j) % ranks, 0, keepdims=False),
+                lambda s, d, t: (s, d, (t + j) % ranks),
+            )
+            for j in range(1, ranks)
+        ]
+        return own, received
 
     def ranked(slab):
         return slab.reshape((ranks, -1) + slab.shape[1:])
@@ -525,7 +543,13 @@
     attention_all = both_layers(attention_item, across, along, far[: chips - 1], far[chips - 1 :])
     in_item = assemble(upward, downward)
     in_across, in_along = chips_once(in_item)
-    back_item = over_ranks(after(back_own[:later], in_item))
+    back_one = after(back_own[:later], in_item)
+    back_up, back_down = [back_one], [back_one]
+    for at in range(1, ranks):
+        relay(back_up, back_down)
+        if at == 1:
+            rows, back_up[-1], back_down[-1] = tie(rows, back_up[-1], back_down[-1])
+    back_item = assemble(back_up, back_down)
     back_item, back_two, in_across, *in_along = tie(back_item, back_two, in_across, *in_along)
     in_all = both_layers(in_item, in_across, in_along, *chips_twice(in_item, in_across, in_along))
     across, along = chips_once(back_item)
@@ -636,24 +660,16 @@
     first_in = first_grad + core_sum(matmul(packed_low, weights[0][0]))
     attention_slabs = attention_grads(first_saved, attended_grad, packed_low)
     attention_one_here = from_x(attention_slabs)
-    first_in, attention_here, back_sent, *in_here = tie(first_in, attention_here, back_sent, *in_here)
-    in_one = add(in_slabs[0], in_here)
+    first_in, attention_here, back_sent, *held = tie(
+        first_in, attention_here, back_sent, *in_here, *attention_slabs
+    )
+    in_one = add(in_slabs[0], held[: chips - 1])
+    attention_slabs = held[chips - 1 :]
     in_sent = from_section(in_one, 0)
+    back_own, back_here = hops_z(by_section(add(back_one, [back_sent]), back_two))
     first_in_spread = spread_rows(first_in.astype(LOW))
-    back_here = from_z(by_section(add(back_one, [back_sent]), back_two))
     attention_two_slabs = jnp.split(add_ranks(attention_here), chips, axis=-1)
     attention_two_here = from_x(attention_two_slabs)
-
-    in_sent, back_here, first_in_spread, *attention_one_here = tie(
-        in_sent, back_here, first_in_spread, *attention_one_here
-    )
-    attention_one = add(attention_slabs[0], attention_one_here)
-    attention_one_sent = from_section(attention_one, 0)
-    in_here = from_z(by_section(add(in_one, [in_sent]), in_two))
-    attention_two = add(attention_two_slabs[0], attention_two_here)
-    attention_two_sent = from_section(attention_two, 1)
-    first_placed = place_rows(first_in_spread, 0)
-    back_shard = finish(add_ranks(back_here))
 
     def spread_columns(row):
         blocks = row.reshape(ranks, 1, -1)
@@ -676,16 +692,28 @@
     table = choose(section, (table[0], table[1])) + move(
         choose(section, (table[1], table[0])), lambda s, d, t: (1 - s, d, t)
     )
-    attention_one_sent, attention_two_sent, in_here, table = tie(
-        attention_one_sent, attention_two_sent, in_here, table
-    )
-    attention_here = from_z(add(attention_one, [attention_one_sent]))
-    table = sum([move(table, lambda s, d, t: (s, d ^ (2 * k), t)) for k in range(1, chips)], table)
-    table = sum([move(table, lambda s, d, t: (s, d, (t + j) % ranks)) for j in range(1, ranks)], table)
+    beside = [move(table, lambda s, d, t: (s, d ^ (2 * k), t)) for k in range(1, chips)]
+    in_sent, table, *held = tie(in_sent, table, *beside, *attention_one_here, *attention_two_here)
+    table, held = sum(held[: chips - 1], table), held[chips - 1 :]
+    attention_one = add(attention_slabs[0], held[: chips - 1])
+    attention_one_sent = from_section(attention_one, 0)
+    attention_two = add(attention_two_slabs[0], held[chips - 1 :])
+    attention_two_sent = from_section(attention_two, 1)
+    in_own, in_here = hops_z(by_section(add(in_one, [in_sent]), in_two))
+
+    beside = [move(table, lambda s, d, t: (s, d, (t + j) % ranks)) for j in range(1, ranks)]
+    attention_one_sent, attention_two_sent, first_in_spread, table, *held = tie(
+        attention_one_sent, attention_two_sent, first_in_spread, table, *beside, *back_here
+    )
+    table, back_here = sum(held[: ranks - 1], table), held[ranks - 1 :]
+    attention_own, attention_here = hops_z(add(attention_one, [attention_one_sent]))
+    first_placed = place_rows(first_in_spread, 0)
+    back_shard = finish(add(back_own, back_here))
+    table, *in_here = tie(table, *in_here)
     attention_two = add(attention_two, [attention_two_sent])
-    in_shard = finish(add_ranks(in_here))
+    in_shard = finish(add(in_own, in_here))
     input_grads = by_section(first_placed, second_placed).astype(WIDE)[None]
-    attention_shard = finish(by_section(add_ranks(attention_here), attention_two))
+    attention_shard = finish(by_section(add(attention_own, attention_here), attention_two))
     qkv_shard, out_shard = attention_shard[:, : 3 * head_half], attention_shard[:, 3 * head_half :]
     qkv_grad = jnp.transpose(qkv_shard.reshape(2, 3, head_half, local), (3, 1, 0, 2)).reshape(local, 3, -1)
     out_grad_w = out_shard.reshape(-1, local)

time: 998 us -> 1030 us (1.032)
  waiting for transfers between devices: 266 us -> 333 us
  starting transfers between devices: 223 us -> 208 us
  Pallas kernels: 102 us -> 88.8 us
    ppermute x82 -> x91, waiting for transfers between devices: 245 us -> 307 us  [move(): return lax.ppermute(value, AXES, pairs)]
    all_to_all x4 -> x1, starting transfers between devices: 18.8 us -> 5.09 us  [from_z(): lax.all_to_all(parts, 'tensor', split_axis=0, concat_axis=0, tiled=True)]
    all_to_all x4 -> x1, waiting for transfers between devices: 0.01 us -> 11.5 us  [from_z(): lax.all_to_all(parts, 'tensor', split_axis=0, concat_axis=0, tiled=True)]
    unnamed x218 -> x250, local copies, waits for them, and re-layouts: 35.2 us -> 41 us
    ppermute x82 -> x91, starting transfers between devices: 177 us -> 175 us  [move(): return lax.ppermute(value, AXES, pairs)]
    convert_element_type x7 -> x9, other arithmetic: 21.5 us -> 23.4 us  [add(): return total.astype(LOW)]
  transfers between devices with their start and end apart: 91 -> 97, of which waited for: 38 -> 41; matrix products, arithmetic and copies ran while one was open for 28% -> 28% of each run, Pallas kernels for 8% -> 7%
where the time goes in v7:
time: 1030 us; the launch traced here: 1010 us
  waiting for transfers between devices  333 us (32%)
  starting transfers between devices  208 us (20%)
  other arithmetic  168 us (16%)
  matrix products  134 us (13%)
  Pallas kernels  88.8 us (9%)
  local copies, waits for them, and re-layouts  79.2 us (8%)
    ppermute x91, waiting for transfers between devices, move(): return lax.ppermute(value, AXES, pairs)  307 us
    ppermute x91, starting transfers between devices, move(): return lax.ppermute(value, AXES, pairs)  175 us
    pallas_call x2, Pallas kernels, attend_backward(): pl.pallas_call(functools.partial(backward_kernel, widths), grid_spec=pltp...  50.5 us
    dot_general x14, matrix products, lhs_inner(): lax.dot_general(lhs_mat, rhs_mat, (((0,), (0,)), ((), ())), preferred_ele...  45.6 us
    dot_general x8, matrix products, rhs_inner(): lax.dot_general(lhs_mat, rhs_mat, (((1,), (1,)), ((), ())), preferred_ele...  44.2 us
    dot_general x10, matrix products, matmul(): return jnp.dot(lhs_mat, rhs_mat, preferred_element_type=WIDE)  43.9 us
    unnamed x250, local copies, waits for them, and re-layouts  41 us
    pallas_call x2, Pallas kernels, attend_forward(): pl.pallas_call(functools.partial(forward_kernel, widths), grid_spec=pltpu...  38.3 us
  transfers between devices with their start and end apart: 97, of which 41 were waited for; matrix products, arithmetic and copies ran while one was open for 28% of the time, Pallas kernels for 7%

profile of v7, /device:TPU:0, one launch (start us, length us, event | category | flops | bytes accessed | tf_op | source)
XLA Modules:
  0.0 1014.3 jit_solution(5084892650160377629)
XLA Ops:
  86.9 11.7 %collective-permute-done.16 = bf16[512,512]{1,0:T(8,128)(2,1)S(1)} collective-permute-done((bf16[512,512]{1,0:T(8,128)(2,1)S(1)}, bf16[512,512]{1,0:T(8,128)(2,1)S(1)}, u32[]{:S(2)}, u32[]{:S(2)}) %collective-permute-start.16) | collective-permute-done | bytes 524320 | tf_op jit(solution)/shard_map/ppermute | solution.py:27
  107.2 9.0 collective-permute-done.17
  126.3 9.6 collective-permute-start.24
  189.5 19.1 %shard_map.169 = (bf16[1024,512]{1,0:T(8,128)(2,1)S(1)}, f32[4,2,1024]{2,1,0:T(2,128)S(1)}) custom-call(s32[4]{0:T(128)S(1)} %compare_select_fusion.8.start_ref, s32[4]{0:T(128)S(1)} %get-tuple-element.188.kind_ref, bf16[1024,1536]{1,0:T(8,128)(2,1)S(1)} %add_convert_fusion.1.query_ref.key_ref.value_ref, ...), custom_call_target="tpu_custom_call" | custom-call | tf_op jit(solution)/shard_map/pallas_call | solution.py:245
  210.0 8.0 collective-permute-start.31
  252.9 8.0 collective-permute-done.41
  275.5 10.5 %collective-permute-done.42 = bf16[2,256,1024]{2,1,0:T(8,128)(2,1)S(1)} collective-permute-done((bf16[2,256,1024]{2,1,0:T(8,128)(2,1)S(1)}, bf16[2,256,1024]{2,1,0:T(8,128)(2,1)S(1)}, u32[]{:S(2)}, u32[]{:S(2)}) %collective-permute-start.42) | collective-permute-done | bytes 1048608 | tf_op jit(solution)/shard_map/ppermute | solution.py:27
  291.9 7.7 multiply_convert_fusion.3
  299.6 10.5 %collective-permute-done.43 = bf16[2,256,1024]{2,1,0:T(8,128)(2,1)S(1)} collective-permute-done((bf16[2,256,1024]{2,1,0:T(8,128)(2,1)S(1)}, bf16[2,256,1024]{2,1,0:T(8,128)(2,1)S(1)}, u32[]{:S(2)}, u32[]{:S(2)}) %collective-permute-start.43) | collective-permute-done | bytes 1048608 | tf_op jit(solution)/shard_map/ppermute | solution.py:27
  348.3 19.2 %shard_map.170 = (bf16[1024,512]{1,0:T(8,128)(2,1)S(1)}, f32[4,2,1024]{2,1,0:T(2,128)S(1)}) custom-call(s32[4]{0:T(128)S(1)} %compare_select_fusion.8.start_ref, s32[4]{0:T(128)S(1)} %get-tuple-element.188.kind_ref, bf16[1024,1536]{1,0:T(8,128)(2,1)S(1)} %add_convert_fusion.query_ref.key_ref.value_ref, ...), custom_call_target="tpu_custom_call" | custom-call | tf_op jit(solution)/shard_map/pallas_call | solution.py:245
  376.9 8.4 all-to-all-start.1
  439.4 9.5 multiply_convert_fusion.1
  493.8 25.2 %shard_map.171 = (bf16[1024,1536]{1,0:T(8,128)(2,1)S(1)}, f32[4,2,128]{2,1,0:T(2,128)S(1)}) custom-call(s32[4]{0:T(128)S(1)} %compare_select_fusion.8.start_ref, s32[4]{0:T(128)S(1)} %get-tuple-element.188.kind_ref, bf16[1024,1536]{1,0:T(8,128)(2,1)} %copy-done.1, bf16[1024,1536]{1,0:T(8,128)(2,1)} %copy-done.1, bf16[1024,1536]{1,0:T(8,128)(2,1)} %copy-done.1, ...), custom_call_target="tpu_custom_call" | custom-call | tf_op jit(solution)/shard_map/pallas_call | solution.py:270
  520.7 8.3 collective-permute-done.53
  560.4 9.5 multiply_convert_fusion
  613.1 13.4 %all-to-all-done.3 = bf16[4,128,1024]{2,1,0:T(8,128)(2,1)} async-done(((bf16[4,128,1024]{2,1,0:T(8,128)(2,1)}), bf16[4,128,1024]{2,1,0:T(8,128)(2,1)}, u32[]{:S(2)}, u32[]{:S(2)}) %all-to-all-start.3) | async-done | bytes 1048608 | tf_op jit(solution)/shard_map/all_to_all | solution.py:404
  652.9 25.4 %shard_map.172 = (bf16[1024,1536]{1,0:T(8,128)(2,1)S(1)}, f32[4,2,128]{2,1,0:T(2,128)S(1)}) custom-call(s32[4]{0:T(128)S(1)} %compare_select_fusion.8.start_ref, s32[4]{0:T(128)S(1)} %get-tuple-element.188.kind_ref, bf16[1024,1536]{1,0:T(8,128)(2,1)} %copy-done, bf16[1024,1536]{1,0:T(8,128)(2,1)} %copy-done, bf16[1024,1536]{1,0:T(8,128)(2,1)} %copy-done, ...), custom_call_target="tpu_custom_call" | custom-call | tf_op jit(solution)/shard_map/pallas_call | solution.py:270
  712.9 11.5 %all-to-all-done.4 = bf16[4,512,1024]{2,1,0:T(8,128)(2,1)} async-done(((bf16[4,512,1024]{2,1,0:T(8,128)(2,1)}), bf16[4,512,1024]{2,1,0:T(8,128)(2,1)}, u32[]{:S(2)}, u32[]{:S(2)}) %all-to-all-start.4) | async-done | bytes 4194336 | tf_op jit(solution)/shard_map/all_to_all | solution.py:484
  724.4 25.1 %collective-permute-done.62 = bf16[4,512,512]{2,1,0:T(8,128)(2,1)} collective-permute-done((bf16[4,512,512]{2,1,0:T(8,128)(2,1)}, bf16[4,512,512]{2,1,0:T(8,128)(2,1)}, u32[]{:S(2)}, u32[]{:S(2)}) %collective-permute-start.62) | collective-permute-done | bytes 2097184 | tf_op jit(solution)/shard_map/ppermute | solution.py:27
  767.7 36.9 %collective-permute-done.66 = f32[12,1024]{1,0:T(8,128)S(1)} collective-permute-done((f32[12,1024]{1,0:T(8,128)S(1)}, f32[12,1024]{1,0:T(8,128)S(1)}, u32[]{:S(2)}, u32[]{:S(2)}) %collective-permute-start.66) | collective-permute-done | bytes 49184 | tf_op jit(solution)/shard_map/ppermute | solution.py:27
  846.9 8.7 collective-permute-done.77
  860.0 37.2 %collective-permute-done.76 = bf16[512,512]{1,0:T(8,128)(2,1)S(1)} collective-permute-done((bf16[512,512]{1,0:T(8,128)(2,1)S(1)}, bf16[512,512]{1,0:T(8,128)(2,1)S(1)}, u32[]{:S(2)}, u32[]{:S(2)}) %collective-permute-start.76) | collective-permute-done | bytes 524320 | tf_op jit(solution)/shard_map/ppermute | solution.py:27
  921.6 27.0 %collective-permute-done.87 = bf16[512,512]{1,0:T(8,128)(2,1)} collective-permute-done((bf16[512,512]{1,0:T(8,128)(2,1)}, bf16[512,512]{1,0:T(8,128)(2,1)}, u32[]{:S(2)}, u32[]{:S(2)}) %collective-permute-start.87) | collective-permute-done | bytes 524320 | tf_op jit(solution)/shard_map/ppermute | solution.py:27
  977.8 23.6 %collective-permute-done.83 = bf16[512,512]{1,0:T(8,128)(2,1)} collective-permute-done((bf16[512,512]{1,0:T(8,128)(2,1)}, bf16[512,512]{1,0:T(8,128)(2,1)}, u32[]{:S(2)}, u32[]{:S(2)}) %collective-permute-start.83) | collective-permute-done | bytes 524320 | tf_op jit(solution)/shard_map/ppermute | solution.py:27
  (682 shorter events, 627.6 us)
Async XLA Ops:
  67.4 53.5 %collective-permute-start.20 = (bf16[4,528,512]{2,1,0:T(8,128)(2,1)S(1)}, bf16[4,528,512]{2,1,0:T(8,128)(2,1)}, u32[]{:S(2)}, u32[]{:S(2)}) collective-permute-start(bf16[4,528,512]{2,1,0:T(8,128)(2,1)S(1)} %bitcast_dynamic-update-slice_fusion.4), channel_id=1, source_target_pairs={{0,8},{1,9},{2,10},{3,11},{4,12},{5,13},{6,14},{7,15},{8,0},{9,1},... | collective-permute-start | bytes 6488072 | tf_op jit(solution)/shard_map/ppermute | solution.py:27
  68.7 53.0 %collective-permute-start.19 = (bf16[4,528,512]{2,1,0:T(8,128)(2,1)S(1)}, bf16[4,528,512]{2,1,0:T(8,128)(2,1)}, u32[]{:S(2)}, u32[]{:S(2)}) collective-permute-start(bf16[4,528,512]{2,1,0:T(8,128)(2,1)S(1)} %bitcast_dynamic-update-slice_fusion.4), channel_id=1, source_target_pairs={{0,16},{1,17},{2,18},{3,19},{4,20},{5,21},{6,22},{7,23},{8,24},{9,... | collective-permute-start | bytes 6488072 | tf_op jit(solution)/shard_map/ppermute | solution.py:27
  172.6 61.7 %collective-permute-start.34 = (bf16[4,512,512]{2,1,0:T(8,128)(2,1)}, bf16[4,512,512]{2,1,0:T(8,128)(2,1)}, u32[]{:S(2)}, u32[]{:S(2)}) collective-permute-start(bf16[4,512,512]{2,1,0:T(8,128)(2,1)} %bitcast_dynamic-update-slice_fusion.7), channel_id=1, source_target_pairs={{0,8},{1,9},{2,10},{3,11},{4,12},{5,13},{6,14},{7,15},{8,0},{9,1},... | collective-permute-start | bytes 6291464 | tf_op jit(solution)/shard_map/ppermute | solution.py:27
  173.1 61.2 %collective-permute-start.33 = (bf16[4,512,512]{2,1,0:T(8,128)(2,1)}, bf16[4,512,512]{2,1,0:T(8,128)(2,1)}, u32[]{:S(2)}, u32[]{:S(2)}) collective-permute-start(bf16[4,512,512]{2,1,0:T(8,128)(2,1)} %bitcast_dynamic-update-slice_fusion.7), channel_id=1, source_target_pairs={{0,16},{1,17},{2,18},{3,19},{4,20},{5,21},{6,22},{7,23},{8,24},{9,... | collective-permute-start | bytes 6291464 | tf_op jit(solution)/shard_map/ppermute | solution.py:27
  464.9 64.1 %all-to-all-start.2 = ((bf16[4,256,1024]{2,1,0:T(8,128)(2,1)}), bf16[4,256,1024]{2,1,0:T(8,128)(2,1)}, u32[]{:S(2)}, u32[]{:S(2)}) async-start(bf16[4,256,1024]{2,1,0:T(8,128)(2,1)} %bitcast.78), calls=%async_computation.2 | async-start | bytes 4194304 | tf_op jit(solution)/shard_map/all_to_all | solution.py:393
  480.1 48.9 %collective-permute-start.53 = (bf16[4,512,512]{2,1,0:T(8,128)(2,1)}, bf16[4,512,512]{2,1,0:T(8,128)(2,1)}, u32[]{:S(2)}, u32[]{:S(2)}) collective-permute-start(bf16[4,512,512]{2,1,0:T(8,128)(2,1)} %bitcast.79), channel_id=1, source_target_pairs={{0,8},{1,9},{2,10},{3,11},{4,12},{5,13},{6,14},{7,15},{8,0},{9,1},... | collective-permute-start | bytes 6291464 | tf_op jit(solution)/shard_map/ppermute | solution.py:27
  481.9 155.4 %collective-permute-start.58 = (bf16[4,512,512]{2,1,0:T(8,128)(2,1)}, bf16[4,512,512]{2,1,0:T(8,128)(2,1)}, u32[]{:S(2)}, u32[]{:S(2)}) collective-permute-start(bf16[4,512,512]{2,1,0:T(8,128)(2,1)} %bitcast.81), channel_id=1, source_target_pairs={{0,8},{1,9},{2,10},{3,11},{4,12},{5,13},{6,14},{7,15},{8,0},{9,1},... | collective-permute-start | bytes 6291464 | tf_op jit(solution)/shard_map/ppermute | solution.py:27
  540.8 96.6 %collective-permute-start.56 = (bf16[4,512,512]{2,1,0:T(8,128)(2,1)}, bf16[4,512,512]{2,1,0:T(8,128)(2,1)}, u32[]{:S(2)}, u32[]{:S(2)}) collective-permute-start(bf16[4,512,512]{2,1,0:T(8,128)(2,1)} %fusion.27), channel_id=1, source_target_pairs={{0,16},{1,17},{2,18},{3,19},{4,20},{5,21},{6,22},{7,23},{8,24},{9,... | collective-permute-start | bytes 6291464 | tf_op jit(solution)/shard_map/ppermute | solution.py:27
  545.1 56.0 %collective-permute-start.57 = (bf16[4,256,1024]{2,1,0:T(8,128)(2,1)}, bf16[4,256,1024]{2,1,0:T(8,128)(2,1)}, u32[]{:S(2)}, u32[]{:S(2)}) collective-permute-start(bf16[4,256,1024]{2,1,0:T(8,128)(2,1)} %all-to-all-done.2), channel_id=1, source_target_pairs={{4,16},{5,17},{6,18},{7,19},{12,24},{13,25},{14,26},{15,27},{16,4}... | collective-permute-start | bytes 6291464 | tf_op jit(solution)/shard_map/ppermute | solution.py:27
  581.6 50.1 %collective-permute-start.55 = (bf16[1024,1024]{0,1:T(8,128)(2,1)}, bf16[1024,1024]{0,1:T(8,128)(2,1)}, u32[]{:S(2)}, u32[]{:S(2)}) collective-permute-start(bf16[1024,1024]{0,1:T(8,128)(2,1)} %convolution_convert_fusion.12), channel_id=1, source_target_pairs={{0,4},{1,5},{2,6},{3,7},{4,0},{5,1},{6,2},{7,3},{8,12},{9,13},{10,... | collective-permute-start | bytes 6291464 | tf_op jit(solution)/shard_map/ppermute | solution.py:27
  600.3 81.7 %collective-permute-start.60 = (bf16[4,512,512]{2,1,0:T(8,128)(2,1)}, bf16[4,512,512]{2,1,0:T(8,128)(2,1)}, u32[]{:S(2)}, u32[]{:S(2)}) collective-permute-start(bf16[4,512,512]{2,1,0:T(8,128)(2,1)} %bitcast.395), channel_id=1, source_target_pairs={{0,8},{1,9},{2,10},{3,11},{4,12},{5,13},{6,14},{7,15},{8,0},{9,1},... | collective-permute-start | bytes 6291464 | tf_op jit(solution)/shard_map/ppermute | solution.py:27
  601.1 111.8 %collective-permute-start.63 = (bf16[4,512,512]{2,1,0:T(8,128)(2,1)}, bf16[4,512,512]{2,1,0:T(8,128)(2,1)}, u32[]{:S(2)}, u32[]{:S(2)}) collective-permute-start(bf16[4,512,512]{2,1,0:T(8,128)(2,1)} %bitcast.394), channel_id=1, source_target_pairs={{0,8},{1,9},{2,10},{3,11},{4,12},{5,13},{6,14},{7,15},{8,0},{9,1},... | collective-permute-start | bytes 6291464 | tf_op jit(solution)/shard_map/ppermute | solution.py:27
  626.5 97.9 %all-to-all-start.4 = ((bf16[4,512,1024]{2,1,0:T(8,128)(2,1)}), bf16[4,512,1024]{2,1,0:T(8,128)(2,1)}, u32[]{:S(2)}, u32[]{:S(2)}) async-start(bf16[4,512,1024]{2,1,0:T(8,128)(2,1)} %pad_maximum_fusion.4), calls=%async_computation.4 | async-start | bytes 8388608 | tf_op jit(solution)/shard_map/all_to_all | solution.py:484
  699.2 50.3 %collective-permute-start.62 = (bf16[4,512,512]{2,1,0:T(8,128)(2,1)}, bf16[4,512,512]{2,1,0:T(8,128)(2,1)}, u32[]{:S(2)}, u32[]{:S(2)}) collective-permute-start(bf16[4,512,512]{2,1,0:T(8,128)(2,1)} %fusion.25), channel_id=1, source_target_pairs={{16,0},{17,1},{18,2},{19,3},{20,4},{21,5},{22,6},{23,7},{24,8},{25... | collective-permute-start | bytes 6291464 | tf_op jit(solution)/shard_map/ppermute | solution.py:27
  704.7 104.2 %collective-permute-start.68 = (bf16[4,512,512]{2,1,0:T(8,128)(2,1)}, bf16[4,512,512]{2,1,0:T(8,128)(2,1)}, u32[]{:S(2)}, u32[]{:S(2)}) collective-permute-start(bf16[4,512,512]{2,1,0:T(8,128)(2,1)} %pad_maximum_fusion.9), channel_id=1, source_target_pairs={{0,8},{1,9},{2,10},{3,11},{4,12},{5,13},{6,14},{7,15},{8,0},{9,1},... | collective-permute-start | bytes 6291464 | tf_op jit(solution)/shard_map/ppermute | solution.py:27
  753.7 56.0 %collective-permute-start.64 = (bf16[4,512,512]{2,1,0:T(8,128)(2,1)}, bf16[4,512,512]{2,1,0:T(8,128)(2,1)}, u32[]{:S(2)}, u32[]{:S(2)}) collective-permute-start(bf16[4,512,512]{2,1,0:T(8,128)(2,1)} %fusion.24), channel_id=1, source_target_pairs={{16,0},{17,1},{18,2},{19,3},{20,4},{21,5},{22,6},{23,7},{24,8},{25... | collective-permute-start | bytes 6291464 | tf_op jit(solution)/shard_map/ppermute | solution.py:27
  755.5 50.0 %collective-permute-start.81 = (bf16[4,128,1024]{2,1,0:T(8,128)(2,1)}, bf16[4,128,1024]{2,1,0:T(8,128)(2,1)}, u32[]{:S(2)}, u32[]{:S(2)}) collective-permute-start(bf16[4,128,1024]{2,1,0:T(8,128)(2,1)} %all-to-all-done.3), channel_id=1, source_target_pairs={{4,16},{5,17},{6,18},{7,19},{12,24},{13,25},{14,26},{15,27}} | collective-permute-start | bytes 3145736 | tf_op jit(solution)/shard_map/ppermute | solution.py:27
  811.9 99.0 %collective-permute-start.70 = (bf16[4,512,512]{2,1,0:T(8,128)(2,1)S(1)}, bf16[4,512,512]{2,1,0:T(8,128)(2,1)}, u32[]{:S(2)}, u32[]{:S(2)}) collective-permute-start(bf16[4,512,512]{2,1,0:T(8,128)(2,1)S(1)} %add_convert_fusion.7), channel_id=1, source_target_pairs={{16,0},{17,1},{18,2},{19,3},{20,4},{21,5},{22,6},{23,7},{24,8},{25... | collective-permute-start | bytes 6291464 | tf_op jit(solution)/shard_map/ppermute | solution.py:27
  821.5 89.4 %all-to-all-start.5 = ((bf16[4,128,1024]{2,1,0:T(8,128)(2,1)}), bf16[4,128,1024]{2,1,0:T(8,128)(2,1)}, u32[]{:S(2)}, u32[]{:S(2)}) async-start(bf16[4,128,1024]{2,1,0:T(8,128)(2,1)} %slice_select_fusion), calls=%async_computation.5 | async-start | bytes 2097152 | tf_op jit(solution)/shard_map/all_to_all | solution.py:404
  835.0 62.2 %collective-permute-start.76 = (bf16[512,512]{1,0:T(8,128)(2,1)S(1)}, bf16[512,512]{1,0:T(8,128)(2,1)S(1)}, u32[]{:S(2)}, u32[]{:S(2)}) collective-permute-start(bf16[512,512]{1,0:T(8,128)(2,1)S(1)} %get-tuple-element.208), channel_id=1, source_target_pairs={{0,2},{1,3},{2,0},{3,1},{4,6},{5,7},{6,4},{7,5},{8,10},{9,11},{10,... | collective-permute-start | bytes 1572872 | tf_op jit(solution)/shard_map/ppermute | solution.py:27
  835.0 62.2 %collective-permute-start.75 = (bf16[512,512]{1,0:T(8,128)(2,1)S(1)}, bf16[512,512]{1,0:T(8,128)(2,1)S(1)}, u32[]{:S(2)}, u32[]{:S(2)}) collective-permute-start(bf16[512,512]{1,0:T(8,128)(2,1)S(1)} %get-tuple-element.209), channel_id=1, source_target_pairs={{0,1},{1,2},{2,3},{3,0},{4,5},{5,6},{6,7},{7,4},{8,9},{9,10},{10,1... | collective-permute-start | bytes 1572872 | tf_op jit(solution)/shard_map/ppermute | solution.py:27
  836.3 73.6 %collective-permute-start.71 = (bf16[512,512]{1,0:T(8,128)(2,1)S(1)}, bf16[512,512]{1,0:T(8,128)(2,1)S(1)}, u32[]{:S(2)}, u32[]{:S(2)}) collective-permute-start(bf16[512,512]{1,0:T(8,128)(2,1)S(1)} %add_convert_fusion.14), channel_id=1, source_target_pairs={{0,16},{1,17},{2,18},{3,19},{4,20},{5,21},{6,22},{7,23},{8,24},{9,... | collective-permute-start | bytes 1572872 | tf_op jit(solution)/shard_map/ppermute | solution.py:27
  898.6 110.8 %collective-permute-start.80 = (bf16[4,128,1024]{2,1,0:T(8,128)(2,1)}, bf16[4,128,1024]{2,1,0:T(8,128)(2,1)}, u32[]{:S(2)}, u32[]{:S(2)}) collective-permute-start(bf16[4,128,1024]{2,1,0:T(8,128)(2,1)} %all-to-all-done.3), channel_id=1, source_target_pairs={{0,16},{1,17},{2,18},{3,19},{8,24},{9,25},{10,26},{11,27},{16,20},... | collective-permute-start | bytes 3145736 | tf_op jit(solution)/shard_map/ppermute | solution.py:27
  959.3 48.8 %collective-permute-start.78 = (bf16[4,128,1024]{2,1,0:T(8,128)(2,1)}, bf16[4,128,1024]{2,1,0:T(8,128)(2,1)}, u32[]{:S(2)}, u32[]{:S(2)}) collective-permute-start(bf16[4,128,1024]{2,1,0:T(8,128)(2,1)} %all-to-all-done.5), channel_id=1, source_target_pairs={{16,4},{17,5},{18,6},{19,7},{24,12},{25,13},{26,14},{27,15}} | collective-permute-start | bytes 3145736 | tf_op jit(solution)/shard_map/ppermute | solution.py:27
  (192 other events, 3342.9 us)

commit v8 on v7

--- a/solution.py
+++ b/solution.py
@@ -661,11 +661,13 @@
     attention_slabs = attention_grads(first_saved, attended_grad, packed_low)
     attention_one_here = from_x(attention_slabs)
     first_in, attention_here, back_sent, *held = tie(
-        first_in, attention_here, back_sent, *in_here, *attention_slabs
+        first_in, attention_here, back_sent, *in_here, *attention_one_here, *attention_slabs
     )
     in_one = add(in_slabs[0], held[: chips - 1])
-    attention_slabs = held[chips - 1 :]
+    attention_one_here, attention_slabs = held[chips - 1 : 2 * chips - 2], held[2 * chips - 2 :]
+    attention_one = add(attention_slabs[0], attention_one_here)
     in_sent = from_section(in_one, 0)
+    attention_one_sent = from_section(attention_one, 0)
     back_own, back_here = hops_z(by_section(add(back_one, [back_sent]), back_two))
     first_in_spread = spread_rows(first_in.astype(LOW))
     attention_two_slabs = jnp.split(add_ranks(attention_here), chips, axis=-1)
@@ -689,27 +691,27 @@
     table = jnp.stack(tables)
     table = jnp.where(counted, table, 0.0) if repeats > 1 else table
     table = table + to_other_core(table)
-    table = choose(section, (table[0], table[1])) + move(
+    table, table_sent = choose(section, (table[0], table[1])), move(
         choose(section, (table[1], table[0])), lambda s, d, t: (1 - s, d, t)
     )
+
+    in_sent, first_in_spread, table_sent, *held = tie(
+        in_sent, first_in_spread, table_sent, *attention_two_here, *back_here
+    )
+    table = table + table_sent
     beside = [move(table, lambda s, d, t: (s, d ^ (2 * k), t)) for k in range(1, chips)]
-    in_sent, table, *held = tie(in_sent, table, *beside, *attention_one_here, *attention_two_here)
-    table, held = sum(held[: chips - 1], table), held[chips - 1 :]
-    attention_one = add(attention_slabs[0], held[: chips - 1])
-    attention_one_sent = from_section(attention_one, 0)
-    attention_two = add(attention_two_slabs[0], held[chips - 1 :])
+    attention_two = add(attention_two_slabs[0], held[: chips - 1])
     attention_two_sent = from_section(attention_two, 1)
+    back_here = held[chips - 1 :]
     in_own, in_here = hops_z(by_section(add(in_one, [in_sent]), in_two))
 
-    beside = [move(table, lambda s, d, t: (s, d, (t + j) % ranks)) for j in range(1, ranks)]
-    attention_one_sent, attention_two_sent, first_in_spread, table, *held = tie(
-        attention_one_sent, attention_two_sent, first_in_spread, table, *beside, *back_here
-    )
-    table, back_here = sum(held[: ranks - 1], table), held[ranks - 1 :]
+    attention_one_sent, attention_two_sent, *beside = tie(attention_one_sent, attention_two_sent, *beside)
+    table = sum(beside, table)
     attention_own, attention_here = hops_z(add(attention_one, [attention_one_sent]))
     first_placed = place_rows(first_in_spread, 0)
     back_shard = finish(add(back_own, back_here))
-    table, *in_here = tie(table, *in_here)
+    table = sum([move(table, lambda s, d, t: (s, d, (t + j) % ranks)) for j in range(1, ranks)], table)
+    attention_one_sent, *in_here = tie(attention_one_sent, *in_here)
     attention_two = add(attention_two, [attention_two_sent])
     in_shard = finish(add(in_own, in_here))
     input_grads = by_section(first_placed, second_placed).astype(WIDE)[None]

time: 1030 us -> 982 us (0.953)
  waiting for transfers between devices: 333 us -> 260 us
  Pallas kernels: 88.8 us -> 106 us
  starting transfers between devices: 208 us -> 219 us
    ppermute x91, waiting for transfers between devices: 307 us -> 251 us  [move(): return lax.ppermute(value, AXES, pairs)]
    ppermute x91, starting transfers between devices: 175 us -> 188 us  [move(): return lax.ppermute(value, AXES, pairs)]
    all_to_all x2, waiting for transfers between devices: 13.5 us -> 1.45 us  [spread_rows(): lax.all_to_all(mine, 'tensor', split_axis=0, concat_axis=0, tiled=True)]
    pallas_call x2, Pallas kernels: 50.5 us -> 61.2 us  [attend_backward(): pl.pallas_call(functools.partial(backward_kernel, widths), grid_spec=pltp...]
    unnamed x250 -> x254, local copies, waits for them, and re-layouts: 41 us -> 41.8 us
  transfers between devices with their start and end apart: 97 -> 97, of which waited for: 41 -> 38; matrix products, arithmetic and copies ran while one was open for 28% -> 30% of each run, Pallas kernels for 7% -> 9%
where the time goes in v8:
time: 982 us; the launch traced here: 972 us
  waiting for transfers between devices  260 us (26%)
  starting transfers between devices  219 us (22%)
  other arithmetic  173 us (18%)
  matrix products  132 us (13%)
  Pallas kernels  106 us (11%)
  local copies, waits for them, and re-layouts  79.1 us (8%)
    ppermute x91, waiting for transfers between devices, move(): return lax.ppermute(value, AXES, pairs)  251 us
    ppermute x91, starting transfers between devices, move(): return lax.ppermute(value, AXES, pairs)  188 us
    pallas_call x2, Pallas kernels, attend_backward(): pl.pallas_call(functools.partial(backward_kernel, widths), grid_spec=pltp...  61.2 us
    dot_general x14, matrix products, lhs_inner(): lax.dot_general(lhs_mat, rhs_mat, (((0,), (0,)), ((), ())), preferred_ele...  45.6 us
    pallas_call x2, Pallas kernels, attend_forward(): pl.pallas_call(functools.partial(forward_kernel, widths), grid_spec=pltpu...  45.1 us
    dot_general x8, matrix products, rhs_inner(): lax.dot_general(lhs_mat, rhs_mat, (((1,), (1,)), ((), ())), preferred_ele...  44.2 us
    unnamed x254, local copies, waits for them, and re-layouts  41.8 us
    dot_general x10, matrix products, matmul(): return jnp.dot(lhs_mat, rhs_mat, preferred_element_type=WIDE)  41.7 us
  transfers between devices with their start and end apart: 97, of which 38 were waited for; matrix products, arithmetic and copies ran while one was open for 30% of the time, Pallas kernels for 9%

profile of v8, /device:TPU:0, one launch (start us, length us, event | category | flops | bytes accessed | tf_op | source)
XLA Modules:
  0.0 972.0 jit_solution(14248500228797518312)
XLA Ops:
  55.7 6.7 collective-permute-done.5
  87.8 12.8 %collective-permute-done.16 = bf16[512,512]{1,0:T(8,128)(2,1)S(1)} collective-permute-done((bf16[512,512]{1,0:T(8,128)(2,1)S(1)}, bf16[512,512]{1,0:T(8,128)(2,1)S(1)}, u32[]{:S(2)}, u32[]{:S(2)}) %collective-permute-start.16) | collective-permute-done | bytes 524320 | tf_op jit(solution)/shard_map/ppermute | solution.py:27
  100.6 10.4 %collective-permute-start.17 = (bf16[512,512]{1,0:T(8,128)(2,1)}, bf16[512,512]{1,0:T(8,128)(2,1)}, u32[]{:S(2)}, u32[]{:S(2)}) collective-permute-start(bf16[512,512]{1,0:T(8,128)(2,1)} %collective-permute-done.15), channel_id=1, source_target_pairs={{0,1},{1,2},{2,3},{4,5},{5,6},{6,7},{8,9},{9,10},{10,11},{12,13},{... | collective-permute-start | bytes 1572872 | tf_op jit(solution)/shard_map/ppermute | solution.py:27
  113.3 9.0 collective-permute-done.17
  190.1 22.4 %shard_map.169 = (bf16[1024,512]{1,0:T(8,128)(2,1)S(1)}, f32[4,2,1024]{2,1,0:T(2,128)S(1)}) custom-call(s32[4]{0:T(128)S(1)} %compare_select_fusion.8.start_ref, s32[4]{0:T(128)S(1)} %get-tuple-element.178.kind_ref, bf16[1024,1536]{1,0:T(8,128)(2,1)S(1)} %add_convert_fusion.1.query_ref.key_ref.value_ref, ...), custom_call_target="tpu_custom_call" | custom-call | tf_op jit(solution)/shard_map/pallas_call | solution.py:245
  254.0 6.7 collective-permute-done.41
  276.2 9.6 collective-permute-done.42
  291.7 7.7 multiply_convert_fusion.3
  299.5 10.5 %collective-permute-done.43 = bf16[2,256,1024]{2,1,0:T(8,128)(2,1)S(1)} collective-permute-done((bf16[2,256,1024]{2,1,0:T(8,128)(2,1)S(1)}, bf16[2,256,1024]{2,1,0:T(8,128)(2,1)S(1)}, u32[]{:S(2)}, u32[]{:S(2)}) %collective-permute-start.43) | collective-permute-done | bytes 1048608 | tf_op jit(solution)/shard_map/ppermute | solution.py:27
  349.2 22.6 %shard_map.170 = (bf16[1024,512]{1,0:T(8,128)(2,1)S(1)}, f32[4,2,1024]{2,1,0:T(2,128)S(1)}) custom-call(s32[4]{0:T(128)S(1)} %compare_select_fusion.8.start_ref, s32[4]{0:T(128)S(1)} %get-tuple-element.178.kind_ref, bf16[1024,1536]{1,0:T(8,128)(2,1)S(1)} %add_convert_fusion.query_ref.key_ref.value_ref, ...), custom_call_target="tpu_custom_call" | custom-call | tf_op jit(solution)/shard_map/pallas_call | solution.py:245
  398.8 7.5 multiply_convert_fusion.2
  440.4 9.5 multiply_convert_fusion.1
  495.4 30.5 %shard_map.171 = (bf16[1024,1536]{1,0:T(8,128)(2,1)S(1)}, f32[4,2,128]{2,1,0:T(2,128)S(1)}) custom-call(s32[4]{0:T(128)S(1)} %compare_select_fusion.8.start_ref, s32[4]{0:T(128)S(1)} %get-tuple-element.178.kind_ref, bf16[1024,1536]{1,0:T(8,128)(2,1)} %copy-done.1, bf16[1024,1536]{1,0:T(8,128)(2,1)} %copy-done.1, bf16[1024,1536]{1,0:T(8,128)(2,1)} %copy-done.1, ...), custom_call_target="tpu_custom_call" | custom-call | tf_op jit(solution)/shard_map/pallas_call | solution.py:270
  561.7 9.5 multiply_convert_fusion
  634.1 13.6 %collective-permute-start.59 = (bf16[4,512,512]{2,1,0:T(8,128)(2,1)}, bf16[4,512,512]{2,1,0:T(8,128)(2,1)}, u32[]{:S(2)}, u32[]{:S(2)}) collective-permute-start(bf16[4,512,512]{2,1,0:T(8,128)(2,1)} %fusion.25), channel_id=1, source_target_pairs={{0,16},{1,17},{2,18},{3,19},{4,20},{5,21},{6,22},{7,23},{8,24},{9,... | collective-permute-start | bytes 6291464 | tf_op jit(solution)/shard_map/ppermute | solution.py:27
  647.7 6.8 fusion.79
  658.6 30.7 %shard_map.172 = (bf16[1024,1536]{1,0:T(8,128)(2,1)S(1)}, f32[4,2,128]{2,1,0:T(2,128)S(1)}) custom-call(s32[4]{0:T(128)S(1)} %compare_select_fusion.8.start_ref, s32[4]{0:T(128)S(1)} %get-tuple-element.178.kind_ref, bf16[1024,1536]{1,0:T(8,128)(2,1)} %copy-done, bf16[1024,1536]{1,0:T(8,128)(2,1)} %copy-done, bf16[1024,1536]{1,0:T(8,128)(2,1)} %copy-done, ...), custom_call_target="tpu_custom_call" | custom-call | tf_op jit(solution)/shard_map/pallas_call | solution.py:270
  727.6 23.9 %collective-permute-done.64 = bf16[4,512,512]{2,1,0:T(8,128)(2,1)} collective-permute-done((bf16[4,512,512]{2,1,0:T(8,128)(2,1)}, bf16[4,512,512]{2,1,0:T(8,128)(2,1)}, u32[]{:S(2)}, u32[]{:S(2)}) %collective-permute-start.64) | collective-permute-done | bytes 2097184 | tf_op jit(solution)/shard_map/ppermute | solution.py:27
  751.5 6.7 collective-permute-done.62
  791.7 21.1 %collective-permute-done.67 = f32[12,1024]{1,0:T(8,128)S(1)} collective-permute-done((f32[12,1024]{1,0:T(8,128)S(1)}, f32[12,1024]{1,0:T(8,128)S(1)}, u32[]{:S(2)}, u32[]{:S(2)}) %collective-permute-start.67) | collective-permute-done | bytes 49184 | tf_op jit(solution)/shard_map/ppermute | solution.py:27
  822.1 26.7 %collective-permute-done.70 = bf16[512,512]{1,0:T(8,128)(2,1)S(1)} collective-permute-done((bf16[512,512]{1,0:T(8,128)(2,1)S(1)}, bf16[512,512]{1,0:T(8,128)(2,1)S(1)}, u32[]{:S(2)}, u32[]{:S(2)}) %collective-permute-start.70) | collective-permute-done | bytes 524320 | tf_op jit(solution)/shard_map/ppermute | solution.py:27
  877.6 33.1 %collective-permute-done.84 = bf16[512,512]{1,0:T(8,128)(2,1)S(1)} collective-permute-done((bf16[512,512]{1,0:T(8,128)(2,1)S(1)}, bf16[512,512]{1,0:T(8,128)(2,1)S(1)}, u32[]{:S(2)}, u32[]{:S(2)}) %collective-permute-start.84) | collective-permute-done | bytes 524320 | tf_op jit(solution)/shard_map/ppermute | solution.py:27
  919.6 19.3 %collective-permute-start.74 = (bf16[4,128,1024]{2,1,0:T(8,128)(2,1)S(1)}, bf16[4,128,1024]{2,1,0:T(8,128)(2,1)}, u32[]{:S(2)}, u32[]{:S(2)}) collective-permute-start(bf16[4,128,1024]{2,1,0:T(8,128)(2,1)S(1)} %copy-done.62), channel_id=1, source_target_pairs={{0,16},{1,17},{2,18},{3,19},{8,24},{9,25},{10,26},{11,27},{16,20},... | collective-permute-start | bytes 3145736 | tf_op jit(solution)/shard_map/ppermute | solution.py:27
  942.5 18.1 %collective-permute-done.80 = bf16[512,512]{1,0:T(8,128)(2,1)} collective-permute-done((bf16[512,512]{1,0:T(8,128)(2,1)}, bf16[512,512]{1,0:T(8,128)(2,1)}, u32[]{:S(2)}, u32[]{:S(2)}) %collective-permute-start.80) | collective-permute-done | bytes 524320 | tf_op jit(solution)/shard_map/ppermute | solution.py:27
  (687 shorter events, 592.8 us)
Async XLA Ops:
  66.2 46.3 %all-to-all-start = ((bf16[4,128,1024]{2,1,0:T(8,128)(2,1)}), bf16[4,128,1024]{2,1,0:T(8,128)(2,1)}, u32[]{:S(2)}, u32[]{:S(2)}) async-start(bf16[4,128,1024]{2,1,0:T(8,128)(2,1)} %select_select_fusion.1), calls=%async_computation | async-start | bytes 2097152 | tf_op jit(solution)/shard_map/all_to_all | solution.py:387
  72.0 55.1 %collective-permute-start.20 = (bf16[4,528,512]{2,1,0:T(8,128)(2,1)S(1)}, bf16[4,528,512]{2,1,0:T(8,128)(2,1)}, u32[]{:S(2)}, u32[]{:S(2)}) collective-permute-start(bf16[4,528,512]{2,1,0:T(8,128)(2,1)S(1)} %bitcast_dynamic-update-slice_fusion.4), channel_id=1, source_target_pairs={{0,8},{1,9},{2,10},{3,11},{4,12},{5,13},{6,14},{7,15},{8,0},{9,1},... | collective-permute-start | bytes 6488072 | tf_op jit(solution)/shard_map/ppermute | solution.py:27
  73.6 53.4 %collective-permute-start.19 = (bf16[4,528,512]{2,1,0:T(8,128)(2,1)S(1)}, bf16[4,528,512]{2,1,0:T(8,128)(2,1)}, u32[]{:S(2)}, u32[]{:S(2)}) collective-permute-start(bf16[4,528,512]{2,1,0:T(8,128)(2,1)S(1)} %bitcast_dynamic-update-slice_fusion.4), channel_id=1, source_target_pairs={{0,16},{1,17},{2,18},{3,19},{4,20},{5,21},{6,22},{7,23},{8,24},{9,... | collective-permute-start | bytes 6488072 | tf_op jit(solution)/shard_map/ppermute | solution.py:27
  173.4 60.7 %collective-permute-start.34 = (bf16[4,512,512]{2,1,0:T(8,128)(2,1)}, bf16[4,512,512]{2,1,0:T(8,128)(2,1)}, u32[]{:S(2)}, u32[]{:S(2)}) collective-permute-start(bf16[4,512,512]{2,1,0:T(8,128)(2,1)} %bitcast_dynamic-update-slice_fusion.7), channel_id=1, source_target_pairs={{0,8},{1,9},{2,10},{3,11},{4,12},{5,13},{6,14},{7,15},{8,0},{9,1},... | collective-permute-start | bytes 6291464 | tf_op jit(solution)/shard_map/ppermute | solution.py:27
  173.7 60.4 %collective-permute-start.33 = (bf16[4,512,512]{2,1,0:T(8,128)(2,1)}, bf16[4,512,512]{2,1,0:T(8,128)(2,1)}, u32[]{:S(2)}, u32[]{:S(2)}) collective-permute-start(bf16[4,512,512]{2,1,0:T(8,128)(2,1)} %bitcast_dynamic-update-slice_fusion.7), channel_id=1, source_target_pairs={{0,16},{1,17},{2,18},{3,19},{4,20},{5,21},{6,22},{7,23},{8,24},{9,... | collective-permute-start | bytes 6291464 | tf_op jit(solution)/shard_map/ppermute | solution.py:27
  251.9 47.6 %collective-permute-start.44 = (bf16[4,256,512]{2,1,0:T(8,128)(2,1)S(1)}, bf16[4,256,512]{2,1,0:T(8,128)(2,1)S(1)}, u32[]{:S(2)}, u32[]{:S(2)}) collective-permute-start(bf16[4,256,512]{2,1,0:T(8,128)(2,1)S(1)} %bitcast_dynamic-update-slice_fusion.11), channel_id=1, source_target_pairs={{0,8},{1,9},{2,10},{3,11},{4,12},{5,13},{6,14},{7,15},{8,0},{9,1},... | collective-permute-start | bytes 3145736 | tf_op jit(solution)/shard_map/ppermute | solution.py:27
  466.1 64.4 %all-to-all-start.2 = ((bf16[4,256,1024]{2,1,0:T(8,128)(2,1)}), bf16[4,256,1024]{2,1,0:T(8,128)(2,1)}, u32[]{:S(2)}, u32[]{:S(2)}) async-start(bf16[4,256,1024]{2,1,0:T(8,128)(2,1)} %bitcast.78), calls=%async_computation.2 | async-start | bytes 4194304 | tf_op jit(solution)/shard_map/all_to_all | solution.py:393
  481.2 49.3 %collective-permute-start.53 = (bf16[4,512,512]{2,1,0:T(8,128)(2,1)}, bf16[4,512,512]{2,1,0:T(8,128)(2,1)}, u32[]{:S(2)}, u32[]{:S(2)}) collective-permute-start(bf16[4,512,512]{2,1,0:T(8,128)(2,1)} %bitcast.79), channel_id=1, source_target_pairs={{0,8},{1,9},{2,10},{3,11},{4,12},{5,13},{6,14},{7,15},{8,0},{9,1},... | collective-permute-start | bytes 6291464 | tf_op jit(solution)/shard_map/ppermute | solution.py:27
  483.7 136.9 %collective-permute-start.58 = (bf16[4,512,512]{2,1,0:T(8,128)(2,1)}, bf16[4,512,512]{2,1,0:T(8,128)(2,1)}, u32[]{:S(2)}, u32[]{:S(2)}) collective-permute-start(bf16[4,512,512]{2,1,0:T(8,128)(2,1)} %bitcast.81), channel_id=1, source_target_pairs={{0,8},{1,9},{2,10},{3,11},{4,12},{5,13},{6,14},{7,15},{8,0},{9,1},... | collective-permute-start | bytes 6291464 | tf_op jit(solution)/shard_map/ppermute | solution.py:27
  542.2 78.4 %collective-permute-start.56 = (bf16[4,512,512]{2,1,0:T(8,128)(2,1)}, bf16[4,512,512]{2,1,0:T(8,128)(2,1)}, u32[]{:S(2)}, u32[]{:S(2)}) collective-permute-start(bf16[4,512,512]{2,1,0:T(8,128)(2,1)} %fusion.27), channel_id=1, source_target_pairs={{0,16},{1,17},{2,18},{3,19},{4,20},{5,21},{6,22},{7,23},{8,24},{9,... | collective-permute-start | bytes 6291464 | tf_op jit(solution)/shard_map/ppermute | solution.py:27
  546.4 58.0 %collective-permute-start.57 = (bf16[4,256,1024]{2,1,0:T(8,128)(2,1)}, bf16[4,256,1024]{2,1,0:T(8,128)(2,1)}, u32[]{:S(2)}, u32[]{:S(2)}) collective-permute-start(bf16[4,256,1024]{2,1,0:T(8,128)(2,1)} %all-to-all-done.2), channel_id=1, source_target_pairs={{4,16},{5,17},{6,18},{7,19},{12,24},{13,25},{14,26},{15,27},{16,4}... | collective-permute-start | bytes 6291464 | tf_op jit(solution)/shard_map/ppermute | solution.py:27
  603.2 90.0 %collective-permute-start.60 = (bf16[4,512,512]{2,1,0:T(8,128)(2,1)}, bf16[4,512,512]{2,1,0:T(8,128)(2,1)}, u32[]{:S(2)}, u32[]{:S(2)}) collective-permute-start(bf16[4,512,512]{2,1,0:T(8,128)(2,1)} %bitcast.396), channel_id=1, source_target_pairs={{0,8},{1,9},{2,10},{3,11},{4,12},{5,13},{6,14},{7,15},{8,0},{9,1},... | collective-permute-start | bytes 6291464 | tf_op jit(solution)/shard_map/ppermute | solution.py:27
  604.3 116.6 %collective-permute-start.63 = (bf16[4,512,512]{2,1,0:T(8,128)(2,1)}, bf16[4,512,512]{2,1,0:T(8,128)(2,1)}, u32[]{:S(2)}, u32[]{:S(2)}) collective-permute-start(bf16[4,512,512]{2,1,0:T(8,128)(2,1)} %bitcast.395), channel_id=1, source_target_pairs={{0,8},{1,9},{2,10},{3,11},{4,12},{5,13},{6,14},{7,15},{8,0},{9,1},... | collective-permute-start | bytes 6291464 | tf_op jit(solution)/shard_map/ppermute | solution.py:27
  629.2 98.4 %all-to-all-start.4 = ((bf16[4,512,1024]{2,1,0:T(8,128)(2,1)}), bf16[4,512,1024]{2,1,0:T(8,128)(2,1)}, u32[]{:S(2)}, u32[]{:S(2)}) async-start(bf16[4,512,1024]{2,1,0:T(8,128)(2,1)} %pad_maximum_fusion.4), calls=%async_computation.4 | async-start | bytes 8388608 | tf_op jit(solution)/shard_map/all_to_all | solution.py:484
  634.1 59.1 %collective-permute-start.59 = (bf16[4,512,512]{2,1,0:T(8,128)(2,1)}, bf16[4,512,512]{2,1,0:T(8,128)(2,1)}, u32[]{:S(2)}, u32[]{:S(2)}) collective-permute-start(bf16[4,512,512]{2,1,0:T(8,128)(2,1)} %fusion.25), channel_id=1, source_target_pairs={{0,16},{1,17},{2,18},{3,19},{4,20},{5,21},{6,22},{7,23},{8,24},{9,... | collective-permute-start | bytes 6291464 | tf_op jit(solution)/shard_map/ppermute | solution.py:27
  703.1 48.3 %collective-permute-start.64 = (bf16[4,512,512]{2,1,0:T(8,128)(2,1)}, bf16[4,512,512]{2,1,0:T(8,128)(2,1)}, u32[]{:S(2)}, u32[]{:S(2)}) collective-permute-start(bf16[4,512,512]{2,1,0:T(8,128)(2,1)} %pad_maximum_fusion.8), channel_id=1, source_target_pairs={{0,8},{1,9},{2,10},{3,11},{4,12},{5,13},{6,14},{7,15},{8,0},{9,1},... | collective-permute-start | bytes 6291464 | tf_op jit(solution)/shard_map/ppermute | solution.py:27
  708.1 50.1 %collective-permute-start.62 = (bf16[4,512,512]{2,1,0:T(8,128)(2,1)}, bf16[4,512,512]{2,1,0:T(8,128)(2,1)}, u32[]{:S(2)}, u32[]{:S(2)}) collective-permute-start(bf16[4,512,512]{2,1,0:T(8,128)(2,1)} %fusion.24), channel_id=1, source_target_pairs={{16,0},{17,1},{18,2},{19,3},{20,4},{21,5},{22,6},{23,7},{24,8},{25... | collective-permute-start | bytes 6291464 | tf_op jit(solution)/shard_map/ppermute | solution.py:27
  713.1 102.6 %collective-permute-start.75 = (bf16[4,128,1024]{2,1,0:T(8,128)(2,1)S(1)}, bf16[4,128,1024]{2,1,0:T(8,128)(2,1)}, u32[]{:S(2)}, u32[]{:S(2)}) collective-permute-start(bf16[4,128,1024]{2,1,0:T(8,128)(2,1)S(1)} %all-to-all-done.3), channel_id=1, source_target_pairs={{4,16},{5,17},{6,18},{7,19},{12,24},{13,25},{14,26},{15,27}} | collective-permute-start | bytes 3145736 | tf_op jit(solution)/shard_map/ppermute | solution.py:27
  762.4 87.3 %collective-permute-start.65 = (bf16[4,512,512]{2,1,0:T(8,128)(2,1)}, bf16[4,512,512]{2,1,0:T(8,128)(2,1)}, u32[]{:S(2)}, u32[]{:S(2)}) collective-permute-start(bf16[4,512,512]{2,1,0:T(8,128)(2,1)} %fusion.26), channel_id=1, source_target_pairs={{16,0},{17,1},{18,2},{19,3},{20,4},{21,5},{22,6},{23,7},{24,8},{25... | collective-permute-start | bytes 6291464 | tf_op jit(solution)/shard_map/ppermute | solution.py:27
  769.2 80.5 %all-to-all-start.5 = ((bf16[4,128,1024]{2,1,0:T(8,128)(2,1)}), bf16[4,128,1024]{2,1,0:T(8,128)(2,1)}, u32[]{:S(2)}, u32[]{:S(2)}) async-start(bf16[4,128,1024]{2,1,0:T(8,128)(2,1)} %slice_select_fusion), calls=%async_computation.5 | async-start | bytes 2097152 | tf_op jit(solution)/shard_map/all_to_all | solution.py:404
  819.4 47.5 %collective-permute-start.76 = (bf16[4,512,512]{2,1,0:T(8,128)(2,1)S(1)}, bf16[4,512,512]{2,1,0:T(8,128)(2,1)}, u32[]{:S(2)}, u32[]{:S(2)}) collective-permute-start(bf16[4,512,512]{2,1,0:T(8,128)(2,1)S(1)} %add_convert_fusion.5), channel_id=1, source_target_pairs={{16,0},{17,1},{18,2},{19,3},{20,4},{21,5},{22,6},{23,7},{24,8},{25... | collective-permute-start | bytes 6291464 | tf_op jit(solution)/shard_map/ppermute | solution.py:27
  855.1 107.9 %collective-permute-start.72 = (bf16[4,128,1024]{2,1,0:T(8,128)(2,1)}, bf16[4,128,1024]{2,1,0:T(8,128)(2,1)}, u32[]{:S(2)}, u32[]{:S(2)}) collective-permute-start(bf16[4,128,1024]{2,1,0:T(8,128)(2,1)} %all-to-all-done.5), channel_id=1, source_target_pairs={{16,4},{17,5},{18,6},{19,7},{24,12},{25,13},{26,14},{27,15}} | collective-permute-start | bytes 3145736 | tf_op jit(solution)/shard_map/ppermute | solution.py:27
  914.9 45.7 %collective-permute-start.80 = (bf16[512,512]{1,0:T(8,128)(2,1)}, bf16[512,512]{1,0:T(8,128)(2,1)}, u32[]{:S(2)}, u32[]{:S(2)}) collective-permute-start(bf16[512,512]{1,0:T(8,128)(2,1)} %get-tuple-element.196), channel_id=1, source_target_pairs={{0,2},{1,3},{2,0},{3,1},{4,6},{5,7},{6,4},{7,5},{8,10},{9,11},{10,... | collective-permute-start | bytes 1572872 | tf_op jit(solution)/shard_map/ppermute | solution.py:27
  919.6 44.8 %collective-permute-start.74 = (bf16[4,128,1024]{2,1,0:T(8,128)(2,1)S(1)}, bf16[4,128,1024]{2,1,0:T(8,128)(2,1)}, u32[]{:S(2)}, u32[]{:S(2)}) collective-permute-start(bf16[4,128,1024]{2,1,0:T(8,128)(2,1)S(1)} %copy-done.62), channel_id=1, source_target_pairs={{0,16},{1,17},{2,18},{3,19},{8,24},{9,25},{10,26},{11,27},{16,20},... | collective-permute-start | bytes 3145736 | tf_op jit(solution)/shard_map/ppermute | solution.py:27
  (195 other events, 3063.3 us)

commit v9 on v8

--- a/solution.py
+++ b/solution.py
@@ -691,22 +691,21 @@
     table = jnp.stack(tables)
     table = jnp.where(counted, table, 0.0) if repeats > 1 else table
     table = table + to_other_core(table)
+
+    in_sent, first_in_spread, table, *held = tie(
+        in_sent, first_in_spread, table, *attention_two_here, *back_here
+    )
     table, table_sent = choose(section, (table[0], table[1])), move(
         choose(section, (table[1], table[0])), lambda s, d, t: (1 - s, d, t)
     )
-
-    in_sent, first_in_spread, table_sent, *held = tie(
-        in_sent, first_in_spread, table_sent, *attention_two_here, *back_here
-    )
-    table = table + table_sent
-    beside = [move(table, lambda s, d, t: (s, d ^ (2 * k), t)) for k in range(1, chips)]
     attention_two = add(attention_two_slabs[0], held[: chips - 1])
     attention_two_sent = from_section(attention_two, 1)
     back_here = held[chips - 1 :]
     in_own, in_here = hops_z(by_section(add(in_one, [in_sent]), in_two))
 
-    attention_one_sent, attention_two_sent, *beside = tie(attention_one_sent, attention_two_sent, *beside)
-    table = sum(beside, table)
+    attention_one_sent, attention_two_sent, table_sent = tie(attention_one_sent, attention_two_sent, table_sent)
+    table = table + table_sent
+    table = sum([move(table, lambda s, d, t: (s, d ^ (2 * k), t)) for k in range(1, chips)], table)
     attention_own, attention_here = hops_z(add(attention_one, [attention_one_sent]))
     first_placed = place_rows(first_in_spread, 0)
     back_shard = finish(add(back_own, back_here))

time: 982 us -> 975 us (level)
  waiting for transfers between devices: 260 us -> 288 us
  starting transfers between devices: 219 us -> 202 us
  Pallas kernels: 106 us -> 89.2 us
    ppermute x91, waiting for transfers between devices: 251 us -> 276 us  [move(): return lax.ppermute(value, AXES, pairs)]
    ppermute x91, starting transfers between devices: 188 us -> 169 us  [move(): return lax.ppermute(value, AXES, pairs)]
    pallas_call x2, Pallas kernels: 61.2 us -> 50.9 us  [attend_backward(): pl.pallas_call(functools.partial(backward_kernel, widths), grid_spec=pltp...]
  transfers between devices with their start and end apart: 97 -> 97, of which waited for: 38 -> 41; matrix products, arithmetic and copies ran while one was open for 30% -> 30% of each run, Pallas kernels for 9% -> 7%
where the time goes in v9:
time: 975 us; the launch traced here: 961 us
  waiting for transfers between devices  288 us (30%)
  starting transfers between devices  202 us (21%)
  other arithmetic  170 us (17%)
  matrix products  134 us (14%)
  Pallas kernels  89.2 us (9%)
  local copies, waits for them, and re-layouts  74.8 us (8%)
    ppermute x91, waiting for transfers between devices, move(): return lax.ppermute(value, AXES, pairs)  276 us
    ppermute x91, starting transfers between devices, move(): return lax.ppermute(value, AXES, pairs)  169 us
    pallas_call x2, Pallas kernels, attend_backward(): pl.pallas_call(functools.partial(backward_kernel, widths), grid_spec=pltp...  50.9 us
    dot_general x14, matrix products, lhs_inner(): lax.dot_general(lhs_mat, rhs_mat, (((0,), (0,)), ((), ())), preferred_ele...  49.5 us
    dot_general x8, matrix products, rhs_inner(): lax.dot_general(lhs_mat, rhs_mat, (((1,), (1,)), ((), ())), preferred_ele...  44.2 us
    dot_general x10, matrix products, matmul(): return jnp.dot(lhs_mat, rhs_mat, preferred_element_type=WIDE)  39.8 us
    unnamed x254, local copies, waits for them, and re-layouts  38.9 us
    pallas_call x2, Pallas kernels, attend_forward(): pl.pallas_call(functools.partial(forward_kernel, widths), grid_spec=pltpu...  38.3 us
  transfers between devices with their start and end apart: 97, of which 41 were waited for; matrix products, arithmetic and copies ran while one was open for 30% of the time, Pallas kernels for 7%

profile of v9, /device:TPU:0, one launch (start us, length us, event | category | flops | bytes accessed | tf_op | source)
XLA Modules:
  0.0 961.2 jit_solution(7502200388370515513)
XLA Ops:
  86.9 11.6 %collective-permute-done.16 = bf16[512,512]{1,0:T(8,128)(2,1)S(1)} collective-permute-done((bf16[512,512]{1,0:T(8,128)(2,1)S(1)}, bf16[512,512]{1,0:T(8,128)(2,1)S(1)}, u32[]{:S(2)}, u32[]{:S(2)}) %collective-permute-start.16) | collective-permute-done | bytes 524320 | tf_op jit(solution)/shard_map/ppermute | solution.py:27
  107.2 9.0 collective-permute-done.17
  126.3 9.6 collective-permute-start.24
  189.5 19.1 %shard_map.169 = (bf16[1024,512]{1,0:T(8,128)(2,1)S(1)}, f32[4,2,1024]{2,1,0:T(2,128)S(1)}) custom-call(s32[4]{0:T(128)S(1)} %compare_select_fusion.8.start_ref, s32[4]{0:T(128)S(1)} %get-tuple-element.178.kind_ref, bf16[1024,1536]{1,0:T(8,128)(2,1)S(1)} %add_convert_fusion.1.query_ref.key_ref.value_ref, ...), custom_call_target="tpu_custom_call" | custom-call | tf_op jit(solution)/shard_map/pallas_call | solution.py:245
  210.0 8.0 collective-permute-start.31
  253.1 7.8 collective-permute-done.41
  275.4 10.5 %collective-permute-done.42 = bf16[2,256,1024]{2,1,0:T(8,128)(2,1)S(1)} collective-permute-done((bf16[2,256,1024]{2,1,0:T(8,128)(2,1)S(1)}, bf16[2,256,1024]{2,1,0:T(8,128)(2,1)S(1)}, u32[]{:S(2)}, u32[]{:S(2)}) %collective-permute-start.42) | collective-permute-done | bytes 1048608 | tf_op jit(solution)/shard_map/ppermute | solution.py:27
  291.9 7.7 multiply_convert_fusion.3
  299.6 10.5 %collective-permute-done.43 = bf16[2,256,1024]{2,1,0:T(8,128)(2,1)S(1)} collective-permute-done((bf16[2,256,1024]{2,1,0:T(8,128)(2,1)S(1)}, bf16[2,256,1024]{2,1,0:T(8,128)(2,1)S(1)}, u32[]{:S(2)}, u32[]{:S(2)}) %collective-permute-start.43) | collective-permute-done | bytes 1048608 | tf_op jit(solution)/shard_map/ppermute | solution.py:27
  348.2 19.2 %shard_map.170 = (bf16[1024,512]{1,0:T(8,128)(2,1)S(1)}, f32[4,2,1024]{2,1,0:T(2,128)S(1)}) custom-call(s32[4]{0:T(128)S(1)} %compare_select_fusion.8.start_ref, s32[4]{0:T(128)S(1)} %get-tuple-element.178.kind_ref, bf16[1024,1536]{1,0:T(8,128)(2,1)S(1)} %add_convert_fusion.query_ref.key_ref.value_ref, ...), custom_call_target="tpu_custom_call" | custom-call | tf_op jit(solution)/shard_map/pallas_call | solution.py:245
  376.9 7.2 all-to-all-start.1
  396.5 7.5 multiply_convert_fusion.2
  438.1 9.5 multiply_convert_fusion.1
  492.5 25.4 %shard_map.171 = (bf16[1024,1536]{1,0:T(8,128)(2,1)S(1)}, f32[4,2,128]{2,1,0:T(2,128)S(1)}) custom-call(s32[4]{0:T(128)S(1)} %compare_select_fusion.8.start_ref, s32[4]{0:T(128)S(1)} %get-tuple-element.178.kind_ref, bf16[1024,1536]{1,0:T(8,128)(2,1)} %copy-done.1, bf16[1024,1536]{1,0:T(8,128)(2,1)} %copy-done.1, bf16[1024,1536]{1,0:T(8,128)(2,1)} %copy-done.1, ...), custom_call_target="tpu_custom_call" | custom-call | tf_op jit(solution)/shard_map/pallas_call | solution.py:270
  519.6 8.1 collective-permute-done.53
  560.1 9.5 multiply_convert_fusion
  635.5 9.5 collective-permute-start.59
  654.7 25.5 %shard_map.172 = (bf16[1024,1536]{1,0:T(8,128)(2,1)S(1)}, f32[4,2,128]{2,1,0:T(2,128)S(1)}) custom-call(s32[4]{0:T(128)S(1)} %compare_select_fusion.8.start_ref, s32[4]{0:T(128)S(1)} %get-tuple-element.178.kind_ref, bf16[1024,1536]{1,0:T(8,128)(2,1)} %copy-done, bf16[1024,1536]{1,0:T(8,128)(2,1)} %copy-done, bf16[1024,1536]{1,0:T(8,128)(2,1)} %copy-done, ...), custom_call_target="tpu_custom_call" | custom-call | tf_op jit(solution)/shard_map/pallas_call | solution.py:270
  715.0 9.6 %all-to-all-done.4 = bf16[4,512,1024]{2,1,0:T(8,128)(2,1)} async-done(((bf16[4,512,1024]{2,1,0:T(8,128)(2,1)}), bf16[4,512,1024]{2,1,0:T(8,128)(2,1)}, u32[]{:S(2)}, u32[]{:S(2)}) %all-to-all-start.4) | async-done | bytes 4194336 | tf_op jit(solution)/shard_map/all_to_all | solution.py:484
  724.7 17.6 %collective-permute-done.64 = bf16[4,512,512]{2,1,0:T(8,128)(2,1)} collective-permute-done((bf16[4,512,512]{2,1,0:T(8,128)(2,1)}, bf16[4,512,512]{2,1,0:T(8,128)(2,1)}, u32[]{:S(2)}, u32[]{:S(2)}) %collective-permute-start.64) | collective-permute-done | bytes 2097184 | tf_op jit(solution)/shard_map/ppermute | solution.py:27
  784.4 10.9 %collective-permute-done.70 = bf16[512,512]{1,0:T(8,128)(2,1)S(1)} collective-permute-done((bf16[512,512]{1,0:T(8,128)(2,1)S(1)}, bf16[512,512]{1,0:T(8,128)(2,1)S(1)}, u32[]{:S(2)}, u32[]{:S(2)}) %collective-permute-start.70) | collective-permute-done | bytes 524320 | tf_op jit(solution)/shard_map/ppermute | solution.py:27
  795.4 40.3 %collective-permute-done.69 = bf16[512,512]{1,0:T(8,128)(2,1)S(1)} collective-permute-done((bf16[512,512]{1,0:T(8,128)(2,1)S(1)}, bf16[512,512]{1,0:T(8,128)(2,1)S(1)}, u32[]{:S(2)}, u32[]{:S(2)}) %collective-permute-start.69) | collective-permute-done | bytes 524320 | tf_op jit(solution)/shard_map/ppermute | solution.py:27
  866.1 41.8 %collective-permute-done.83 = bf16[512,512]{1,0:T(8,128)(2,1)S(1)} collective-permute-done((bf16[512,512]{1,0:T(8,128)(2,1)S(1)}, bf16[512,512]{1,0:T(8,128)(2,1)S(1)}, u32[]{:S(2)}, u32[]{:S(2)}) %collective-permute-start.83) | collective-permute-done | bytes 524320 | tf_op jit(solution)/shard_map/ppermute | solution.py:27
  928.2 21.4 %collective-permute-done.79 = bf16[512,512]{1,0:T(8,128)(2,1)} collective-permute-done((bf16[512,512]{1,0:T(8,128)(2,1)}, bf16[512,512]{1,0:T(8,128)(2,1)}, u32[]{:S(2)}, u32[]{:S(2)}) %collective-permute-start.79) | collective-permute-done | bytes 524320 | tf_op jit(solution)/shard_map/ppermute | solution.py:27
  (687 shorter events, 600.6 us)
Async XLA Ops:
  67.5 53.5 %collective-permute-start.20 = (bf16[4,528,512]{2,1,0:T(8,128)(2,1)S(1)}, bf16[4,528,512]{2,1,0:T(8,128)(2,1)}, u32[]{:S(2)}, u32[]{:S(2)}) collective-permute-start(bf16[4,528,512]{2,1,0:T(8,128)(2,1)S(1)} %bitcast_dynamic-update-slice_fusion.4), channel_id=1, source_target_pairs={{0,8},{1,9},{2,10},{3,11},{4,12},{5,13},{6,14},{7,15},{8,0},{9,1},... | collective-permute-start | bytes 6488072 | tf_op jit(solution)/shard_map/ppermute | solution.py:27
  68.7 53.0 %collective-permute-start.19 = (bf16[4,528,512]{2,1,0:T(8,128)(2,1)S(1)}, bf16[4,528,512]{2,1,0:T(8,128)(2,1)}, u32[]{:S(2)}, u32[]{:S(2)}) collective-permute-start(bf16[4,528,512]{2,1,0:T(8,128)(2,1)S(1)} %bitcast_dynamic-update-slice_fusion.4), channel_id=1, source_target_pairs={{0,16},{1,17},{2,18},{3,19},{4,20},{5,21},{6,22},{7,23},{8,24},{9,... | collective-permute-start | bytes 6488072 | tf_op jit(solution)/shard_map/ppermute | solution.py:27
  172.6 61.7 %collective-permute-start.34 = (bf16[4,512,512]{2,1,0:T(8,128)(2,1)}, bf16[4,512,512]{2,1,0:T(8,128)(2,1)}, u32[]{:S(2)}, u32[]{:S(2)}) collective-permute-start(bf16[4,512,512]{2,1,0:T(8,128)(2,1)} %bitcast_dynamic-update-slice_fusion.7), channel_id=1, source_target_pairs={{0,8},{1,9},{2,10},{3,11},{4,12},{5,13},{6,14},{7,15},{8,0},{9,1},... | collective-permute-start | bytes 6291464 | tf_op jit(solution)/shard_map/ppermute | solution.py:27
  173.1 61.2 %collective-permute-start.33 = (bf16[4,512,512]{2,1,0:T(8,128)(2,1)}, bf16[4,512,512]{2,1,0:T(8,128)(2,1)}, u32[]{:S(2)}, u32[]{:S(2)}) collective-permute-start(bf16[4,512,512]{2,1,0:T(8,128)(2,1)} %bitcast_dynamic-update-slice_fusion.7), channel_id=1, source_target_pairs={{0,16},{1,17},{2,18},{3,19},{4,20},{5,21},{6,22},{7,23},{8,24},{9,... | collective-permute-start | bytes 6291464 | tf_op jit(solution)/shard_map/ppermute | solution.py:27
  463.5 64.2 %all-to-all-start.2 = ((bf16[4,256,1024]{2,1,0:T(8,128)(2,1)}), bf16[4,256,1024]{2,1,0:T(8,128)(2,1)}, u32[]{:S(2)}, u32[]{:S(2)}) async-start(bf16[4,256,1024]{2,1,0:T(8,128)(2,1)} %bitcast.78), calls=%async_computation.2 | async-start | bytes 4194304 | tf_op jit(solution)/shard_map/all_to_all | solution.py:393
  480.6 138.6 %collective-permute-start.58 = (bf16[4,512,512]{2,1,0:T(8,128)(2,1)}, bf16[4,512,512]{2,1,0:T(8,128)(2,1)}, u32[]{:S(2)}, u32[]{:S(2)}) collective-permute-start(bf16[4,512,512]{2,1,0:T(8,128)(2,1)} %bitcast.81), channel_id=1, source_target_pairs={{0,8},{1,9},{2,10},{3,11},{4,12},{5,13},{6,14},{7,15},{8,0},{9,1},... | collective-permute-start | bytes 6291464 | tf_op jit(solution)/shard_map/ppermute | solution.py:27
  539.5 79.7 %collective-permute-start.56 = (bf16[4,512,512]{2,1,0:T(8,128)(2,1)}, bf16[4,512,512]{2,1,0:T(8,128)(2,1)}, u32[]{:S(2)}, u32[]{:S(2)}) collective-permute-start(bf16[4,512,512]{2,1,0:T(8,128)(2,1)} %fusion.27), channel_id=1, source_target_pairs={{0,16},{1,17},{2,18},{3,19},{4,20},{5,21},{6,22},{7,23},{8,24},{9,... | collective-permute-start | bytes 6291464 | tf_op jit(solution)/shard_map/ppermute | solution.py:27
  544.8 62.3 %collective-permute-start.57 = (bf16[4,256,1024]{2,1,0:T(8,128)(2,1)}, bf16[4,256,1024]{2,1,0:T(8,128)(2,1)}, u32[]{:S(2)}, u32[]{:S(2)}) collective-permute-start(bf16[4,256,1024]{2,1,0:T(8,128)(2,1)} %all-to-all-done.2), channel_id=1, source_target_pairs={{4,16},{5,17},{6,18},{7,19},{12,24},{13,25},{14,26},{15,27},{16,4}... | collective-permute-start | bytes 6291464 | tf_op jit(solution)/shard_map/ppermute | solution.py:27
  599.0 82.1 %collective-permute-start.60 = (bf16[4,512,512]{2,1,0:T(8,128)(2,1)}, bf16[4,512,512]{2,1,0:T(8,128)(2,1)}, u32[]{:S(2)}, u32[]{:S(2)}) collective-permute-start(bf16[4,512,512]{2,1,0:T(8,128)(2,1)} %bitcast.395), channel_id=1, source_target_pairs={{0,8},{1,9},{2,10},{3,11},{4,12},{5,13},{6,14},{7,15},{8,0},{9,1},... | collective-permute-start | bytes 6291464 | tf_op jit(solution)/shard_map/ppermute | solution.py:27
  607.1 108.0 %collective-permute-start.63 = (bf16[4,512,512]{2,1,0:T(8,128)(2,1)}, bf16[4,512,512]{2,1,0:T(8,128)(2,1)}, u32[]{:S(2)}, u32[]{:S(2)}) collective-permute-start(bf16[4,512,512]{2,1,0:T(8,128)(2,1)} %bitcast.89), channel_id=1, source_target_pairs={{0,8},{1,9},{2,10},{3,11},{4,12},{5,13},{6,14},{7,15},{8,0},{9,1},... | collective-permute-start | bytes 6291464 | tf_op jit(solution)/shard_map/ppermute | solution.py:27
  626.3 98.4 %all-to-all-start.4 = ((bf16[4,512,1024]{2,1,0:T(8,128)(2,1)}), bf16[4,512,1024]{2,1,0:T(8,128)(2,1)}, u32[]{:S(2)}, u32[]{:S(2)}) async-start(bf16[4,512,1024]{2,1,0:T(8,128)(2,1)} %pad_maximum_fusion.4), calls=%async_computation.4 | async-start | bytes 8388608 | tf_op jit(solution)/shard_map/all_to_all | solution.py:484
  635.5 50.3 %collective-permute-start.59 = (bf16[4,512,512]{2,1,0:T(8,128)(2,1)}, bf16[4,512,512]{2,1,0:T(8,128)(2,1)}, u32[]{:S(2)}, u32[]{:S(2)}) collective-permute-start(bf16[4,512,512]{2,1,0:T(8,128)(2,1)} %fusion.25), channel_id=1, source_target_pairs={{0,16},{1,17},{2,18},{3,19},{4,20},{5,21},{6,22},{7,23},{8,24},{9,... | collective-permute-start | bytes 6291464 | tf_op jit(solution)/shard_map/ppermute | solution.py:27
  701.5 63.4 %collective-permute-start.66 = (f32[2,12,1024]{2,1,0:T(8,128)}, f32[2,12,1024]{2,1,0:T(8,128)S(1)}, u32[]{:S(2)}, u32[]{:S(2)}) collective-permute-start(f32[2,12,1024]{2,1,0:T(8,128)} %pad_maximum_fusion.15), channel_id=1, source_target_pairs={{0,4},{1,5},{2,6},{3,7},{4,0},{5,1},{6,2},{7,3},{8,12},{9,13},{10,... | collective-permute-start | bytes 294920 | tf_op jit(solution)/shard_map/ppermute | solution.py:27
  709.8 68.3 %collective-permute-start.74 = (bf16[4,128,1024]{2,1,0:T(8,128)(2,1)S(1)}, bf16[4,128,1024]{2,1,0:T(8,128)(2,1)}, u32[]{:S(2)}, u32[]{:S(2)}) collective-permute-start(bf16[4,128,1024]{2,1,0:T(8,128)(2,1)S(1)} %copy-done.61), channel_id=1, source_target_pairs={{4,16},{5,17},{6,18},{7,19},{12,24},{13,25},{14,26},{15,27}} | collective-permute-start | bytes 3145736 | tf_op jit(solution)/shard_map/ppermute | solution.py:27
  753.3 83.2 %collective-permute-start.65 = (bf16[4,512,512]{2,1,0:T(8,128)(2,1)}, bf16[4,512,512]{2,1,0:T(8,128)(2,1)}, u32[]{:S(2)}, u32[]{:S(2)}) collective-permute-start(bf16[4,512,512]{2,1,0:T(8,128)(2,1)} %fusion.26), channel_id=1, source_target_pairs={{16,0},{17,1},{18,2},{19,3},{20,4},{21,5},{22,6},{23,7},{24,8},{25... | collective-permute-start | bytes 6291464 | tf_op jit(solution)/shard_map/ppermute | solution.py:27
  760.1 76.4 %all-to-all-start.5 = ((bf16[4,128,1024]{2,1,0:T(8,128)(2,1)}), bf16[4,128,1024]{2,1,0:T(8,128)(2,1)}, u32[]{:S(2)}, u32[]{:S(2)}) async-start(bf16[4,128,1024]{2,1,0:T(8,128)(2,1)} %slice_select_fusion), calls=%async_computation.5 | async-start | bytes 2097152 | tf_op jit(solution)/shard_map/all_to_all | solution.py:404
  778.0 57.6 %collective-permute-start.69 = (bf16[512,512]{1,0:T(8,128)(2,1)S(1)}, bf16[512,512]{1,0:T(8,128)(2,1)S(1)}, u32[]{:S(2)}, u32[]{:S(2)}) collective-permute-start(bf16[512,512]{1,0:T(8,128)(2,1)S(1)} %get-tuple-element.198), channel_id=1, source_target_pairs={{0,2},{1,3},{2,0},{3,1},{4,6},{5,7},{6,4},{7,5},{8,10},{9,11},{10,... | collective-permute-start | bytes 1572872 | tf_op jit(solution)/shard_map/ppermute | solution.py:27
  778.1 58.4 %collective-permute-start.68 = (bf16[512,512]{1,0:T(8,128)(2,1)S(1)}, bf16[512,512]{1,0:T(8,128)(2,1)}, u32[]{:S(2)}, u32[]{:S(2)}) collective-permute-start(bf16[512,512]{1,0:T(8,128)(2,1)S(1)} %get-tuple-element.199), channel_id=1, source_target_pairs={{0,1},{1,2},{2,3},{3,0},{4,5},{5,6},{6,7},{7,4},{8,9},{9,10},{10,1... | collective-permute-start | bytes 1572872 | tf_op jit(solution)/shard_map/ppermute | solution.py:27
  781.8 70.5 %collective-permute-start.75 = (bf16[4,512,512]{2,1,0:T(8,128)(2,1)S(1)}, bf16[4,512,512]{2,1,0:T(8,128)(2,1)}, u32[]{:S(2)}, u32[]{:S(2)}) collective-permute-start(bf16[4,512,512]{2,1,0:T(8,128)(2,1)S(1)} %add_convert_fusion.5), channel_id=1, source_target_pairs={{16,0},{17,1},{18,2},{19,3},{20,4},{21,5},{22,6},{23,7},{24,8},{25... | collective-permute-start | bytes 6291464 | tf_op jit(solution)/shard_map/ppermute | solution.py:27
  844.4 107.5 %collective-permute-start.71 = (bf16[4,128,1024]{2,1,0:T(8,128)(2,1)}, bf16[4,128,1024]{2,1,0:T(8,128)(2,1)}, u32[]{:S(2)}, u32[]{:S(2)}) collective-permute-start(bf16[4,128,1024]{2,1,0:T(8,128)(2,1)} %all-to-all-done.5), channel_id=1, source_target_pairs={{16,4},{17,5},{18,6},{19,7},{24,12},{25,13},{26,14},{27,15}} | collective-permute-start | bytes 3145736 | tf_op jit(solution)/shard_map/ppermute | solution.py:27
  852.3 55.6 %collective-permute-start.83 = (bf16[512,512]{1,0:T(8,128)(2,1)S(1)}, bf16[512,512]{1,0:T(8,128)(2,1)S(1)}, u32[]{:S(2)}, u32[]{:S(2)}) collective-permute-start(bf16[512,512]{1,0:T(8,128)(2,1)S(1)} %get-tuple-element.192), channel_id=1, source_target_pairs={{0,2},{1,3},{2,0},{3,1},{4,6},{5,7},{6,4},{7,5},{8,10},{9,11},{10,... | collective-permute-start | bytes 1572872 | tf_op jit(solution)/shard_map/ppermute | solution.py:27
  852.3 55.6 %collective-permute-start.82 = (bf16[512,512]{1,0:T(8,128)(2,1)S(1)}, bf16[512,512]{1,0:T(8,128)(2,1)S(1)}, u32[]{:S(2)}, u32[]{:S(2)}) collective-permute-start(bf16[512,512]{1,0:T(8,128)(2,1)S(1)} %get-tuple-element.193), channel_id=1, source_target_pairs={{0,1},{1,2},{2,3},{3,0},{4,5},{5,6},{6,7},{7,4},{8,9},{9,10},{10,1... | collective-permute-start | bytes 1572872 | tf_op jit(solution)/shard_map/ppermute | solution.py:27
  856.2 51.9 %collective-permute-start.87 = (f32[12,1024]{1,0:T(8,128)S(1)}, f32[12,1024]{1,0:T(8,128)S(1)}, u32[]{:S(2)}, u32[]{:S(2)}) collective-permute-start(f32[12,1024]{1,0:T(8,128)S(1)} %bitcast_add_fusion), channel_id=1, source_target_pairs={{0,8},{1,9},{2,10},{3,11},{4,12},{5,13},{6,14},{7,15},{8,0},{9,1},... | collective-permute-start | bytes 147464 | tf_op jit(solution)/shard_map/ppermute | solution.py:27
  866.1 58.6 %collective-permute-start.78 = (bf16[512,512]{1,0:T(8,128)(2,1)S(1)}, bf16[512,512]{1,0:T(8,128)(2,1)S(1)}, u32[]{:S(2)}, u32[]{:S(2)}) collective-permute-start(bf16[512,512]{1,0:T(8,128)(2,1)S(1)} %get-tuple-element.194), channel_id=1, source_target_pairs={{0,1},{1,2},{2,3},{3,0},{4,5},{5,6},{6,7},{7,4},{8,9},{9,10},{10,1... | collective-permute-start | bytes 1572872 | tf_op jit(solution)/shard_map/ppermute | solution.py:27
  (195 other events, 3109.3 us)
